TPU v7x, 256 devices: a whole 4x4x8 slice. The times are simulated.
256 devices in a mesh: lat: 64 (over y, x, z_lo), rad: 4 (over z_hi, core).
Axes of the slice: x: 4, y: 4, z: 8 (z_hi: 2, z_lo: 4; z = z_hi * 4 + z_lo), core: 2. Of those that a mesh axis runs over, the one named last changes fastest.
Arguments:
- source: float32 [16, 1024, 1024], P('rad', 'lat'), may hold values from -8 to 8
- kappa: float32 [16, 1024, 1024], P('rad', 'lat'), may hold values from 0.02 to 0.5
- forward: float32 [16, 1024, 1024], P('rad', 'lat'), may hold values from -8 to 8
- viscosity: float32 [16, 1024, 1024], P('rad', 'lat'), may hold values from 0.1 to 10
Outputs:
- adjoint: float32 [16, 1024, 1024], P('rad', 'lat')
- gradient: float32 [16, 1024, 1024], P('rad', 'lat')
All inputs are finite; a program needn't handle non-finite values.
Results may differ from a plain program's by a relative error of at most 0.00002.
Values sent between devices are 32-bit elements; how exact they have to be, the bound alone decides.
No kernel may reach another device: no remote copies, remote signals or barrier semaphores. Data moves between devices by JAX's collectives and lax.ppermute only.
A program may use at most 128 MiB of HBM per device.

v0:
```python
import jax
import jax.numpy as jnp
from jax import lax
from jax.experimental import pallas as pl
from jax.experimental.pallas import tpu as pltpu
from jax.sharding import PartitionSpec as P

S_F = 8
S_C = 8
FINE = (1.5, 12.5)
COARSE = (0.05, 3.5)

LAYERS = 4
ROWS = 16
NR = 16
HALO = 8
MAIN = 256
WIDE = 384
PACKED = 640
EDGE = 32
VMEM = pltpu.CompilerParams(vmem_limit_bytes=40 * 1024 * 1024)
F32 = jnp.float32


def lanes(shape):
    return lax.broadcasted_iota(jnp.int32, shape, len(shape) - 1)


def coefficients(low, high, sweeps):
    theta = (high + low) / 2.0
    delta = (high - low) / 2.0
    sigma = theta / delta
    rho = 1.0 / sigma
    pairs = []
    for _ in range(sweeps):
        rho_new = 1.0 / (2.0 * sigma - rho)
        pairs.append((rho_new * rho, 2.0 * rho_new / delta))
        rho = rho_new
    return 1.0 / theta, pairs


def pack_windows(ids, source, kappa, *outs):
    lane = lanes((LAYERS, ROWS, 128))
    right = lane < EDGE
    left = lane >= 128 - EDGE
    for m, out in enumerate(outs):
        base = ids[m] * MAIN
        main = pl.ds(pl.multiple_of(base, 128), MAIN)
        after = pl.ds(pl.multiple_of(lax.rem(base + MAIN, 1024), 128), 128)
        before = pl.ds(pl.multiple_of(lax.rem(base + 1024 - 128, 1024), 128), 128)
        out[:, :, 0:MAIN] = source[:, :, main]
        out[:, :, MAIN : 2 * MAIN] = kappa[:, :, main]
        edge_s = jnp.where(right, source[:, :, after], source[:, :, before])
        edge_k = jnp.where(right, kappa[:, :, after], kappa[:, :, before])
        edge_k = pltpu.roll(edge_k, 64, 2)
        out[:, :, 2 * MAIN :] = jnp.where(right | left, edge_s, edge_k)


def pack_rows(ids, p0, p1, p2, p3, up, down):
    for m, piece in enumerate((p0, p1, p2, p3)):
        at = pl.ds((ids[4] ^ m) * LAYERS, LAYERS)
        up[at] = piece[:, HALO:, :]
        down[at] = piece[:, :HALO, :]


def spread(packed, rhs, diag):
    lane = lanes(packed.shape[:-1] + (128,))
    keep = (lane < EDGE) | (lane >= 128 - EDGE)
    edge = packed[..., 2 * MAIN :]
    rhs_edge = jnp.where(keep, edge, 0.0)
    diag_edge = jnp.where(keep, pltpu.roll(edge, 64, edge.ndim - 1), 0.0)
    rhs[..., :MAIN] = packed[..., :MAIN]
    rhs[..., MAIN:] = rhs_edge
    diag[..., :MAIN] = packed[..., MAIN : 2 * MAIN] + 6.0
    diag[..., MAIN:] = diag_edge + 6.0


def lateral(v, step_x, step_y):
    rows, width = v.shape
    return (
        pltpu.roll(v, step_x, 0)
        + pltpu.roll(v, rows - step_x, 0)
        + pltpu.roll(v, step_y, 1)
        + pltpu.roll(v, width - step_y, 1)
    )


def fine_kernel(ids, p0, p1, p2, p3, lo, hi, smooth, packed, rhs, diag, xa, xb, step):
    me = ids[4]
    for m, piece in enumerate((p0, p1, p2, p3)):
        base = (me ^ m) * LAYERS

        def fill(j, _, piece=piece, base=base):
            own = pl.ds(HALO, ROWS)
            spread(piece[j], rhs.at[base + j, own], diag.at[base + j, own])
            return 0

        lax.fori_loop(0, LAYERS, fill, 0)

    first, pairs = coefficients(*FINE, S_F)
    zero = jnp.zeros((2 * ROWS, WIDE), F32)
    xa[0] = zero
    xb[0] = zero
    xa[NR + 1] = zero
    xb[NR + 1] = zero

    def begin(r, _):
        spread(lo[r], rhs.at[r, pl.ds(0, HALO)], diag.at[r, pl.ds(0, HALO)])
        top = pl.ds(HALO + ROWS, HALO)
        spread(hi[r], rhs.at[r, top], diag.at[r, top])
        d = rhs[r] * first
        step[r] = d
        xa[r + 1] = d
        return 0

    lax.fori_loop(0, NR, begin, 0)

    old, new = xa, xb
    for damp, gain in pairs[: S_F - 1]:

        def sweep(r, _, old=old, new=new, damp=damp, gain=gain):
            v = old[r + 1]
            near = old[r] + old[r + 2] + lateral(v, 1, 1)
            resid = rhs[r] - diag[r] * v + near
            d = damp * step[r] + gain * resid
            step[r] = d
            new[r + 1] = v + d
            return 0

        lax.fori_loop(0, NR, sweep, 0)
        old, new = new, old

    even_row = lax.rem(lax.broadcasted_iota(jnp.int32, (ROWS, WIDE), 0), 2) == 0
    even_lane = lax.rem(lanes((HALO, WIDE)), 2) == 0
    pick_r = lax.broadcasted_iota(jnp.int32, (HALO, ROWS), 0)
    pick_c = lax.broadcasted_iota(jnp.int32, (HALO, ROWS), 1)
    pick = jnp.where(lax.shift_right_logical(pick_c, 1) == pick_r, 0.125, 0.0).astype(F32)

    def block_mean(v):
        s = jnp.dot(pick, v, precision=lax.Precision.HIGHEST, preferred_element_type=F32)
        return s + jnp.where(even_lane, pltpu.roll(s, WIDE - 1, 1), pltpu.roll(s, 1, 1))

    def residual(q, _):
        total = None
        diags = None
        for j in range(2):
            r = 2 * q + j
            v = old[r + 1]
            near = old[r] + old[r + 2] + lateral(v, 1, 1)
            resid = (rhs[r] - diag[r] * v + near)[HALO : HALO + ROWS]
            total = resid if total is None else total + resid
            k = diag[r, HALO : HALO + ROWS] - 6.0
            diags = k if diags is None else diags + k
            smooth[r] = v[HALO:, :MAIN]
        packed[q] = jnp.where(even_lane, block_mean(total), block_mean(diags))
        return 0

    lax.fori_loop(0, NR // 2, residual, 0)


def coarse_kernel(ids, lo, own, hi, smooth, o0, o1, o2, o3, rhs, diag, xa, xb, step, adj):
    first, pairs = coefficients(*COARSE, S_C)
    half = NR // 2
    rows = 3 * HALO
    zero = jnp.zeros((rows, WIDE), F32)
    xa[0] = zero
    xb[0] = zero
    xa[half + 1] = zero
    xb[half + 1] = zero
    even = lax.rem(lanes((HALO, WIDE)), 2) == 0

    def begin(q, _):
        for part, src in enumerate((lo, own, hi)):
            v = src[q]
            at = pl.ds(part * HALO, HALO)
            rhs[q, at] = jnp.where(even, v, pltpu.roll(v, 1, 1))
            diag[q, at] = jnp.where(even, pltpu.roll(v, WIDE - 1, 1), v) + 1.5
        d = rhs[q] * first
        step[q] = d
        xa[q + 1] = d
        return 0

    lax.fori_loop(0, half, begin, 0)
    old, new = xa, xb
    for damp, gain in pairs[: S_C - 1]:

        def sweep(q, _, old=old, new=new, damp=damp, gain=gain):
            v = old[q + 1]
            near = old[q] + old[q + 2] + lateral(v, 1, 2)
            resid = rhs[q] - diag[q] * v + 0.25 * near
            d = damp * step[q] + gain * resid
            step[q] = d
            new[q + 1] = v + d
            return 0

        lax.fori_loop(0, half, sweep, 0)
        old, new = new, old

    copy_r = lax.broadcasted_iota(jnp.int32, (rows, 2 * HALO), 0)
    copy_c = lax.broadcasted_iota(jnp.int32, (rows, 2 * HALO), 1)
    copy = jnp.where(lax.shift_right_logical(copy_r, 1) == copy_c, 1.0, 0.0).astype(F32)

    def refine(q, _):
        c = jnp.dot(copy, old[q + 1, HALO:, :MAIN], precision=lax.Precision.HIGHEST, preferred_element_type=F32)
        for j in range(2):
            adj[2 * q + j] = smooth[2 * q + j] + c
        return 0

    lax.fori_loop(0, half, refine, 0)
    adj[NR] = jnp.zeros((rows, MAIN), F32)
    for m, out in enumerate((o0, o1, o2, o3)):
        base = (ids[4] ^ m) * LAYERS
        for j in range(LAYERS + 1):
            out[2 * j] = adj[base + j, 0:8]
            out[2 * j + 1] = adj[base + j, 8:16]
        for j in range(LAYERS):
            out[2 * LAYERS + 2, pl.ds(j, 1)] = adj[base + j, 16:17]
        out[2 * LAYERS + 2, pl.ds(LAYERS, 4)] = jnp.zeros((4, MAIN), F32)


def gradient_kernel(ids, p0, p1, p2, p3, forward, forward_x, forward_r, viscosity, adjoint, gradient, above, beyond):
    for m, piece in enumerate((p0, p1, p2, p3)):
        at = pl.ds(pl.multiple_of(ids[m] * MAIN, 128), MAIN)
        for j in range(LAYERS):
            adjoint[j, 0:8, at] = piece[2 * j]
            adjoint[j, 8:16, at] = piece[2 * j + 1]
        above[0:8, at] = piece[2 * LAYERS]
        above[8:16, at] = piece[2 * LAYERS + 1]
        beyond[:, at] = piece[2 * LAYERS + 2]
    last = lax.broadcasted_iota(jnp.int32, (ROWS, 1024), 0) == ROWS - 1
    for j in range(LAYERS):
        a = adjoint[j]
        f = forward[j]
        a_r = (adjoint[j + 1] if j + 1 < LAYERS else above[...]) - a
        f_r = (forward[j + 1] if j + 1 < LAYERS else forward_r[0]) - f
        a_x = jnp.where(last, beyond[pl.ds(j, 1)], pltpu.roll(a, ROWS - 1, 0)) - a
        f_x = jnp.where(last, forward_x[j], pltpu.roll(f, ROWS - 1, 0)) - f
        a_y = pltpu.roll(a, 1023, 1) - a
        f_y = pltpu.roll(f, 1023, 1) - f
        gradient[j] = viscosity[j] * (f_r * a_r + f_x * a_x + f_y * a_y)


def struct(*shape):
    return jax.ShapeDtypeStruct(shape, F32)


def call(kernel, outs, scratch, ids, *args):
    whole = pl.BlockSpec(memory_space=pltpu.VMEM)
    return pl.pallas_call(
        kernel,
        out_shape=outs,
        in_specs=[pl.BlockSpec(memory_space=pltpu.SMEM)] + [whole] * len(args),
        out_specs=[whole] * len(outs),
        scratch_shapes=[pltpu.VMEM(s, F32) for s in scratch],
        compiler_params=VMEM,
    )(ids, *args)


def body(source, kappa, forward, viscosity):
    lat_n = lax.axis_size("lat")
    rad_n = lax.axis_size("rad")
    lat = lax.axis_index("lat")
    rad = lax.axis_index("rad")

    def flip(i):
        return ((i // 4) % 2) * 2

    turn = flip(lat)
    ids = jnp.stack([rad ^ turn, rad ^ 1 ^ turn, rad ^ 2 ^ turn, rad ^ 3 ^ turn, rad]).astype(jnp.int32)

    def trade(pieces):
        out = [pieces[0]]
        for m in range(1, rad_n):
            out.append(lax.ppermute(pieces[m], "rad", [(k, k ^ m) for k in range(rad_n)]))
        return out

    def beside(v, way):
        pairs = []
        for i in range(lat_n):
            to = (i + way) % lat_n
            for k in range(rad_n):
                pairs.append((i * rad_n + k, to * rad_n + (k ^ flip(i) ^ flip(to))))
        return lax.ppermute(v, ("lat", "rad"), pairs)

    pieces = call(pack_windows, [struct(LAYERS, ROWS, PACKED)] * 4, [], ids, source, kappa)
    pieces = trade(pieces)
    up, down = call(pack_rows, [struct(NR, HALO, PACKED)] * 2, [], ids, *pieces)
    lo = beside(up, 1)
    hi = beside(down, -1)
    deep = (NR, 2 * ROWS, WIDE)
    padded = (NR + 2, 2 * ROWS, WIDE)
    smooth, packed = call(
        fine_kernel,
        [struct(NR, 3 * HALO, MAIN), struct(NR // 2, HALO, WIDE)],
        [deep, deep, padded, padded, deep],
        ids,
        *pieces,
        lo,
        hi,
    )
    below = beside(packed, 1)
    over = beside(packed, -1)
    deep = (NR // 2, 3 * HALO, WIDE)
    padded = (NR // 2 + 2, 3 * HALO, WIDE)
    backs = call(
        coarse_kernel,
        [struct(2 * LAYERS + 3, 8, MAIN)] * 4,
        [deep, deep, padded, padded, deep, (NR + 1, 3 * HALO, MAIN)],
        ids,
        below,
        packed,
        over,
        smooth,
    )
    backs = trade(backs)
    forward_x = lax.ppermute(forward[:, :1], "lat", [((i + 1) % lat_n, i) for i in range(lat_n)])
    forward_r = lax.ppermute(forward[:1], "rad", [(k + 1, k) for k in range(rad_n - 1)])
    adjoint, gradient = call(
        gradient_kernel,
        [struct(LAYERS, ROWS, 1024)] * 2,
        [(ROWS, 1024), (8, 1024)],
        ids,
        *backs,
        forward,
        forward_x,
        forward_r,
        viscosity,
    )
    return adjoint, gradient


def solution(mesh):
    placed = P("rad", "lat", None)
    return jax.shard_map(
        body,
        mesh=mesh,
        in_specs=(placed,) * 4,
        out_specs=(placed,) * 2,
        check_vma=False,
    )
```

profile of v0, /device:TPU:1, one launch (start us, length us, event | category | flops | bytes accessed | tf_op | source)
XLA Modules:
  0.0 95.2 jit_solution(380006244539296350)
XLA Ops:
  0.7 0.1 stack.23.ids
  0.7 0.0 copy-start.2
  0.8 0.9 copy-done.2
  1.7 0.0 copy-start.3
  1.7 0.9 copy-done.3
  2.7 0.7 shard_map.59
  3.3 3.3 %collective-permute-start = (f32[4,16,640]{2,1,0:T(8,128)S(1)}, f32[4,16,640]{2,1,0:T(8,128)S(1)}, u32[]{:S(2)}, u32[]{:S(2)}) collective-permute-start(f32[4,16,640]{2,1,0:T(8,128)S(1)} %get-tuple-element.15), channel_id=1, source_target_pairs={{0,1},{1,0},{2,3},{3,2},{4,5},{5,4},{6,7},{7,6},{8,9},{9,8},{10,11... | collective-permute-start | bytes 491528 | tf_op jit(solution)/shard_map/ppermute | solution.py:274
  6.7 5.2 %collective-permute-start.1 = (f32[4,16,640]{2,1,0:T(8,128)S(1)}, f32[4,16,640]{2,1,0:T(8,128)S(1)}, u32[]{:S(2)}, u32[]{:S(2)}) collective-permute-start(f32[4,16,640]{2,1,0:T(8,128)S(1)} %get-tuple-element.16), channel_id=1, source_target_pairs={{0,2},{1,3},{2,0},{3,1},{4,6},{5,7},{6,4},{7,5},{8,10},{9,11},{10,... | collective-permute-start | bytes 491528 | tf_op jit(solution)/shard_map/ppermute | solution.py:274
  11.9 0.4 collective-permute-start.2
  12.3 0.0 collective-permute-done.p1
  12.3 4.0 %collective-permute-done.1.p2 = f32[4,16,640]{2,1,0:T(8,128)S(1)} collective-permute-done((f32[4,16,640]{2,1,0:T(8,128)S(1)}, f32[4,16,640]{2,1,0:T(8,128)S(1)}, u32[]{:S(2)}, u32[]{:S(2)}) %collective-permute-start.1) | collective-permute-done | bytes 163872 | tf_op jit(solution)/shard_map/ppermute | solution.py:274
  16.3 7.7 %collective-permute-done.2.p3 = f32[4,16,640]{2,1,0:T(8,128)S(1)} collective-permute-done((f32[4,16,640]{2,1,0:T(8,128)S(1)}, f32[4,16,640]{2,1,0:T(8,128)S(1)}, u32[]{:S(2)}, u32[]{:S(2)}) %collective-permute-start.2) | collective-permute-done | bytes 163872 | tf_op jit(solution)/shard_map/ppermute | solution.py:274
  24.0 0.6 shard_map.60
  24.6 3.7 %collective-permute-start.3 = (f32[16,8,640]{2,1,0:T(8,128)S(1)}, f32[16,8,640]{2,1,0:T(8,128)S(1)}, u32[]{:S(2)}, u32[]{:S(2)}) collective-permute-start(f32[16,8,640]{2,1,0:T(8,128)S(1)} %get-tuple-element.18), channel_id=1, source_target_pairs={{0,4},{1,5},{2,6},{3,7},{4,8},{5,9},{6,10},{7,11},{8,12},{9,13},{1... | collective-permute-start | bytes 983048 | tf_op jit(solution)/shard_map/ppermute | solution.py:283
  28.3 6.2 %collective-permute-start.4 = (f32[16,8,640]{2,1,0:T(8,128)S(1)}, f32[16,8,640]{2,1,0:T(8,128)S(1)}, u32[]{:S(2)}, u32[]{:S(2)}) collective-permute-start(f32[16,8,640]{2,1,0:T(8,128)S(1)} %get-tuple-element.19), channel_id=1, source_target_pairs={{0,254},{1,255},{2,252},{3,253},{4,0},{5,1},{6,2},{7,3},{8,4},{9,5... | collective-permute-start | bytes 983048 | tf_op jit(solution)/shard_map/ppermute | solution.py:283
  34.6 7.6 %collective-permute-done.3.lo = f32[16,8,640]{2,1,0:T(8,128)S(1)} collective-permute-done((f32[16,8,640]{2,1,0:T(8,128)S(1)}, f32[16,8,640]{2,1,0:T(8,128)S(1)}, u32[]{:S(2)}, u32[]{:S(2)}) %collective-permute-start.3) | collective-permute-done | bytes 327712 | tf_op jit(solution)/shard_map/ppermute | solution.py:283
  42.2 0.0 collective-permute-done.4.hi
  42.2 17.0 %shard_map.61 = (f32[16,24,256]{2,1,0:T(8,128)S(1)}, f32[8,8,384]{2,1,0:T(8,128)S(1)}) custom-call(s32[5]{0:T(128)S(1)} %stack.23.ids, f32[4,16,640]{2,1,0:T(8,128)S(1)} %get-tuple-element.14.p0, f32[4,16,640]{2,1,0:T(8,128)S(1)} %collective-permute-done.p1, f32[4,16,640]{2,1,0:T(8,128)S(1)} %collective-permute-done.1.p2, ...), custom_call_target="tpu_custom_call" | custom-call | tf_op jit(solution)/shard_map/pallas_call | solution.py:249
  59.2 0.1 collective-permute-start.5
  59.3 6.9 %collective-permute-start.6 = (f32[8,8,384]{2,1,0:T(8,128)S(1)}, f32[8,8,384]{2,1,0:T(8,128)S(1)}, u32[]{:S(2)}, u32[]{:S(2)}) collective-permute-start(f32[8,8,384]{2,1,0:T(8,128)S(1)} %get-tuple-element.20.own), channel_id=1, source_target_pairs={{0,254},{1,255},{2,252},{3,253},{4,0},{5,1},{6,2},{7,3},{8,4},{9,5... | collective-permute-start | bytes 294920 | tf_op jit(solution)/shard_map/ppermute | solution.py:283
  66.2 2.0 %collective-permute-done.5.lo = f32[8,8,384]{2,1,0:T(8,128)S(1)} collective-permute-done((f32[8,8,384]{2,1,0:T(8,128)S(1)}, f32[8,8,384]{2,1,0:T(8,128)S(1)}, u32[]{:S(2)}, u32[]{:S(2)}) %collective-permute-start.5) | collective-permute-done | bytes 98336 | tf_op jit(solution)/shard_map/ppermute | solution.py:283
  68.2 0.0 collective-permute-done.6.hi
  68.2 0.0 copy-start
  68.2 0.0 copy-start.1
  68.2 8.0 %shard_map.62 = (f32[11,8,256]{2,1,0:T(8,128)S(1)}, f32[11,8,256]{2,1,0:T(8,128)S(1)}, f32[11,8,256]{2,1,0:T(8,128)S(1)}, f32[11,8,256]{2,1,0:T(8,128)S(1)}) custom-call(s32[5]{0:T(128)S(1)} %stack.23.ids, f32[8,8,384]{2,1,0:T(8,128)S(1)} %collective-permute-done.5.lo, f32[8,8,384]{2,1,0:T(8,128)S(1)} %get-tuple-element.20.own, ...), custom_call_target="tpu_custom_call" | custom-call | tf_op jit(solution)/shard_map/pallas_call | solution.py:249
  76.2 2.2 %collective-permute-start.7 = (f32[11,8,256]{2,1,0:T(8,128)S(1)}, f32[11,8,256]{2,1,0:T(8,128)S(1)}, u32[]{:S(2)}, u32[]{:S(2)}) collective-permute-start(f32[11,8,256]{2,1,0:T(8,128)S(1)} %get-tuple-element.23), channel_id=1, source_target_pairs={{0,1},{1,0},{2,3},{3,2},{4,5},{5,4},{6,7},{7,6},{8,9},{9,8},{10,11... | collective-permute-start | bytes 270344 | tf_op jit(solution)/shard_map/ppermute | solution.py:274
  78.4 1.3 %collective-permute-start.8 = (f32[11,8,256]{2,1,0:T(8,128)S(1)}, f32[11,8,256]{2,1,0:T(8,128)S(1)}, u32[]{:S(2)}, u32[]{:S(2)}) collective-permute-start(f32[11,8,256]{2,1,0:T(8,128)S(1)} %get-tuple-element.24), channel_id=1, source_target_pairs={{0,2},{1,3},{2,0},{3,1},{4,6},{5,7},{6,4},{7,5},{8,10},{9,11},{10,... | collective-permute-start | bytes 270344 | tf_op jit(solution)/shard_map/ppermute | solution.py:274
  79.7 4.3 %collective-permute-start.9 = (f32[11,8,256]{2,1,0:T(8,128)S(1)}, f32[11,8,256]{2,1,0:T(8,128)S(1)}, u32[]{:S(2)}, u32[]{:S(2)}) collective-permute-start(f32[11,8,256]{2,1,0:T(8,128)S(1)} %get-tuple-element.25), channel_id=1, source_target_pairs={{0,3},{1,2},{2,1},{3,0},{4,7},{5,6},{6,5},{7,4},{8,11},{9,10},{10,... | collective-permute-start | bytes 270344 | tf_op jit(solution)/shard_map/ppermute | solution.py:274
  84.1 0.0 copy-done
  84.1 2.1 %collective-permute-start.11 = (f32[1,16,1024]{2,1,0:T(8,128)S(1)}, f32[1,16,1024]{2,1,0:T(8,128)S(1)}, u32[]{:S(2)}, u32[]{:S(2)}) collective-permute-start(f32[1,16,1024]{2,1,0:T(8,128)S(1)} %slice.7), channel_id=1, source_target_pairs={{1,0},{2,1},{3,2},{5,4},{6,5},{7,6},{9,8},{10,9},{11,10},{13,12},{... | collective-permute-start | bytes 196616 | tf_op jit(solution)/shard_map/ppermute | solution.py:317
  86.2 5.9 %collective-permute-start.10 = (f32[4,1,1024]{2,1,0:T(1,128)S(1)}, f32[4,1,1024]{2,1,0:T(1,128)S(1)}, u32[]{:S(2)}, u32[]{:S(2)}) collective-permute-start(f32[4,1,1024]{2,1,0:T(1,128)S(1)} %slice.6), channel_id=1, source_target_pairs={{4,0},{8,4},{12,8},{16,12},{20,16},{24,20},{28,24},{32,28},{36,32}... | collective-permute-start | bytes 49160 | tf_op jit(solution)/shard_map/ppermute | solution.py:316
  92.1 0.9 collective-permute-done.10.forward_x
  93.0 0.6 collective-permute-done.11.forward_r
  93.6 0.0 collective-permute-done.7.p1
  93.6 0.0 collective-permute-done.8.p2
  93.6 0.0 collective-permute-done.9.p3
  93.6 0.0 copy-done.1
  93.6 1.6 %shard_map.63 = (f32[4,16,1024]{2,1,0:T(8,128)}, f32[4,16,1024]{2,1,0:T(8,128)}) custom-call(s32[5]{0:T(128)S(1)} %stack.23.ids, f32[11,8,256]{2,1,0:T(8,128)S(1)} %get-tuple-element.22.p0, f32[11,8,256]{2,1,0:T(8,128)S(1)} %collective-permute-done.7.p1, f32[11,8,256]{2,1,0:T(8,128)S(1)} %collective-permute-done.8.p2, ...), custom_call_target="tpu_custom_call" | custom-call | tf_op jit(solution)/shard_map/pallas_call | solution.py:249
  (2 shorter events, 0.0 us)
Async XLA Ops:
  0.7 1.0 copy-start.2
  1.7 0.9 copy-start.3
  3.3 9.0 %collective-permute-start = (f32[4,16,640]{2,1,0:T(8,128)S(1)}, f32[4,16,640]{2,1,0:T(8,128)S(1)}, u32[]{:S(2)}, u32[]{:S(2)}) collective-permute-start(f32[4,16,640]{2,1,0:T(8,128)S(1)} %get-tuple-element.15), channel_id=1, source_target_pairs={{0,1},{1,0},{2,3},{3,2},{4,5},{5,4},{6,7},{7,6},{8,9},{9,8},{10,11... | collective-permute-start | bytes 491528 | tf_op jit(solution)/shard_map/ppermute | solution.py:274
  6.7 9.7 %collective-permute-start.1 = (f32[4,16,640]{2,1,0:T(8,128)S(1)}, f32[4,16,640]{2,1,0:T(8,128)S(1)}, u32[]{:S(2)}, u32[]{:S(2)}) collective-permute-start(f32[4,16,640]{2,1,0:T(8,128)S(1)} %get-tuple-element.16), channel_id=1, source_target_pairs={{0,2},{1,3},{2,0},{3,1},{4,6},{5,7},{6,4},{7,5},{8,10},{9,11},{10,... | collective-permute-start | bytes 491528 | tf_op jit(solution)/shard_map/ppermute | solution.py:274
  11.9 12.2 %collective-permute-start.2 = (f32[4,16,640]{2,1,0:T(8,128)S(1)}, f32[4,16,640]{2,1,0:T(8,128)S(1)}, u32[]{:S(2)}, u32[]{:S(2)}) collective-permute-start(f32[4,16,640]{2,1,0:T(8,128)S(1)} %get-tuple-element.17), channel_id=1, source_target_pairs={{0,3},{1,2},{2,1},{3,0},{4,7},{5,6},{6,5},{7,4},{8,11},{9,10},{10,... | collective-permute-start | bytes 491528 | tf_op jit(solution)/shard_map/ppermute | solution.py:274
  24.6 17.5 %collective-permute-start.3 = (f32[16,8,640]{2,1,0:T(8,128)S(1)}, f32[16,8,640]{2,1,0:T(8,128)S(1)}, u32[]{:S(2)}, u32[]{:S(2)}) collective-permute-start(f32[16,8,640]{2,1,0:T(8,128)S(1)} %get-tuple-element.18), channel_id=1, source_target_pairs={{0,4},{1,5},{2,6},{3,7},{4,8},{5,9},{6,10},{7,11},{8,12},{9,13},{1... | collective-permute-start | bytes 983048 | tf_op jit(solution)/shard_map/ppermute | solution.py:283
  28.3 13.8 %collective-permute-start.4 = (f32[16,8,640]{2,1,0:T(8,128)S(1)}, f32[16,8,640]{2,1,0:T(8,128)S(1)}, u32[]{:S(2)}, u32[]{:S(2)}) collective-permute-start(f32[16,8,640]{2,1,0:T(8,128)S(1)} %get-tuple-element.19), channel_id=1, source_target_pairs={{0,254},{1,255},{2,252},{3,253},{4,0},{5,1},{6,2},{7,3},{8,4},{9,5... | collective-permute-start | bytes 983048 | tf_op jit(solution)/shard_map/ppermute | solution.py:283
  59.2 9.0 %collective-permute-start.5 = (f32[8,8,384]{2,1,0:T(8,128)S(1)}, f32[8,8,384]{2,1,0:T(8,128)S(1)}, u32[]{:S(2)}, u32[]{:S(2)}) collective-permute-start(f32[8,8,384]{2,1,0:T(8,128)S(1)} %get-tuple-element.20.own), channel_id=1, source_target_pairs={{0,4},{1,5},{2,6},{3,7},{4,8},{5,9},{6,10},{7,11},{8,12},{9,13},{1... | collective-permute-start | bytes 294920 | tf_op jit(solution)/shard_map/ppermute | solution.py:283
  59.3 8.9 %collective-permute-start.6 = (f32[8,8,384]{2,1,0:T(8,128)S(1)}, f32[8,8,384]{2,1,0:T(8,128)S(1)}, u32[]{:S(2)}, u32[]{:S(2)}) collective-permute-start(f32[8,8,384]{2,1,0:T(8,128)S(1)} %get-tuple-element.20.own), channel_id=1, source_target_pairs={{0,254},{1,255},{2,252},{3,253},{4,0},{5,1},{6,2},{7,3},{8,4},{9,5... | collective-permute-start | bytes 294920 | tf_op jit(solution)/shard_map/ppermute | solution.py:283
  68.2 15.9 %copy-start = (f32[4,16,1024]{2,1,0:T(8,128)S(1)}, f32[4,16,1024]{2,1,0:T(8,128)}, u32[]{:S(2)}) copy-start(f32[4,16,1024]{2,1,0:T(8,128)} %forward.1) | copy-start | bytes 786436
  68.2 25.4 %copy-start.1 = (f32[4,16,1024]{2,1,0:T(8,128)S(1)}, f32[4,16,1024]{2,1,0:T(8,128)}, u32[]{:S(2)}) copy-start(f32[4,16,1024]{2,1,0:T(8,128)} %viscosity.1) | copy-start | bytes 786436
  76.2 17.4 %collective-permute-start.7 = (f32[11,8,256]{2,1,0:T(8,128)S(1)}, f32[11,8,256]{2,1,0:T(8,128)S(1)}, u32[]{:S(2)}, u32[]{:S(2)}) collective-permute-start(f32[11,8,256]{2,1,0:T(8,128)S(1)} %get-tuple-element.23), channel_id=1, source_target_pairs={{0,1},{1,0},{2,3},{3,2},{4,5},{5,4},{6,7},{7,6},{8,9},{9,8},{10,11... | collective-permute-start | bytes 270344 | tf_op jit(solution)/shard_map/ppermute | solution.py:274
  78.4 15.1 %collective-permute-start.8 = (f32[11,8,256]{2,1,0:T(8,128)S(1)}, f32[11,8,256]{2,1,0:T(8,128)S(1)}, u32[]{:S(2)}, u32[]{:S(2)}) collective-permute-start(f32[11,8,256]{2,1,0:T(8,128)S(1)} %get-tuple-element.24), channel_id=1, source_target_pairs={{0,2},{1,3},{2,0},{3,1},{4,6},{5,7},{6,4},{7,5},{8,10},{9,11},{10,... | collective-permute-start | bytes 270344 | tf_op jit(solution)/shard_map/ppermute | solution.py:274
  79.7 13.9 %collective-permute-start.9 = (f32[11,8,256]{2,1,0:T(8,128)S(1)}, f32[11,8,256]{2,1,0:T(8,128)S(1)}, u32[]{:S(2)}, u32[]{:S(2)}) collective-permute-start(f32[11,8,256]{2,1,0:T(8,128)S(1)} %get-tuple-element.25), channel_id=1, source_target_pairs={{0,3},{1,2},{2,1},{3,0},{4,7},{5,6},{6,5},{7,4},{8,11},{9,10},{10,... | collective-permute-start | bytes 270344 | tf_op jit(solution)/shard_map/ppermute | solution.py:274
  84.1 9.5 %collective-permute-start.11 = (f32[1,16,1024]{2,1,0:T(8,128)S(1)}, f32[1,16,1024]{2,1,0:T(8,128)S(1)}, u32[]{:S(2)}, u32[]{:S(2)}) collective-permute-start(f32[1,16,1024]{2,1,0:T(8,128)S(1)} %slice.7), channel_id=1, source_target_pairs={{1,0},{2,1},{3,2},{5,4},{6,5},{7,6},{9,8},{10,9},{11,10},{13,12},{... | collective-permute-start | bytes 196616 | tf_op jit(solution)/shard_map/ppermute | solution.py:317
  86.2 6.8 %collective-permute-start.10 = (f32[4,1,1024]{2,1,0:T(1,128)S(1)}, f32[4,1,1024]{2,1,0:T(1,128)S(1)}, u32[]{:S(2)}, u32[]{:S(2)}) collective-permute-start(f32[4,1,1024]{2,1,0:T(1,128)S(1)} %slice.6), channel_id=1, source_target_pairs={{4,0},{8,4},{12,8},{16,12},{20,16},{24,20},{28,24},{32,28},{36,32}... | collective-permute-start | bytes 49160 | tf_op jit(solution)/shard_map/ppermute | solution.py:316
where the time goes:
time: 95.3 us; the launch traced here: 95.2 us
  starting transfers between devices  41.7 us (44%)
  Pallas kernels  27.9 us (29%)
  waiting for transfers between devices  22.8 us (24%)
  local copies, waits for them, and re-layouts  2.01 us (2%)
    pallas_call x5, Pallas kernels, call(): pl.pallas_call(kernel, out_shape=outs, in_specs=[pl.BlockSpec(memory_spac...  27.9 us
    ppermute x4, starting transfers between devices, beside(): return lax.ppermute(v, ('lat', 'rad'), pairs)  16.9 us
    ppermute x6, starting transfers between devices, trade(): lax.ppermute(pieces[m], 'rad', [(k, k ^ m) for k in range(rad_n)])  16.8 us
    ppermute x6, waiting for transfers between devices, trade(): lax.ppermute(pieces[m], 'rad', [(k, k ^ m) for k in range(rad_n)])  11.7 us
    ppermute x4, waiting for transfers between devices, beside(): return lax.ppermute(v, ('lat', 'rad'), pairs)  9.6 us
    ppermute x1, starting transfers between devices, body(): lax.ppermute(forward[:, :1], 'lat', [((i + 1) % lat_n, i) for i in range(...  5.93 us
    ppermute x1, starting transfers between devices, body(): lax.ppermute(forward[:1], 'rad', [(k + 1, k) for k in range(rad_n - 1)])  2.06 us
    unnamed x8, local copies, waits for them, and re-layouts  1.91 us
  transfers between devices with their start and end apart: 12, of which 6 were waited for; matrix products, arithmetic and copies ran while one was open for 0% of the time, Pallas kernels for 0%

commit v1 on v0

--- a/solution.py
+++ b/solution.py
@@ -39,7 +39,15 @@
     return 1.0 / theta, pairs
 
 
-def pack_windows(ids, source, kappa, *outs):
+def pack_windows(ids, source_hbm, kappa_hbm, *refs):
+    outs, (source, kappa, done) = refs[:4], refs[4:]
+    loads = []
+    for f, (src, dst) in enumerate(((source_hbm, source), (kappa_hbm, kappa))):
+        for j in range(LAYERS):
+            loads.append(pltpu.make_async_copy(src.at[j], dst.at[j], done.at[f, j]))
+            loads[-1].start()
+    for load in loads:
+        load.wait()
     lane = lanes((LAYERS, ROWS, 128))
     right = lane < EDGE
     left = lane >= 128 - EDGE
@@ -95,7 +103,7 @@
             spread(piece[j], rhs.at[base + j, own], diag.at[base + j, own])
             return 0
 
-        lax.fori_loop(0, LAYERS, fill, 0)
+        lax.fori_loop(0, LAYERS, fill, 0, unroll=True)
 
     first, pairs = coefficients(*FINE, S_F)
     zero = jnp.zeros((2 * ROWS, WIDE), F32)
@@ -113,7 +121,7 @@
         xa[r + 1] = d
         return 0
 
-    lax.fori_loop(0, NR, begin, 0)
+    lax.fori_loop(0, NR, begin, 0, unroll=True)
 
     old, new = xa, xb
     for damp, gain in pairs[: S_F - 1]:
@@ -127,7 +135,7 @@
             new[r + 1] = v + d
             return 0
 
-        lax.fori_loop(0, NR, sweep, 0)
+        lax.fori_loop(0, NR, sweep, 0, unroll=True)
         old, new = new, old
 
     even_row = lax.rem(lax.broadcasted_iota(jnp.int32, (ROWS, WIDE), 0), 2) == 0
@@ -155,7 +163,7 @@
         packed[q] = jnp.where(even_lane, block_mean(total), block_mean(diags))
         return 0
 
-    lax.fori_loop(0, NR // 2, residual, 0)
+    lax.fori_loop(0, NR // 2, residual, 0, unroll=True)
 
 
 def coarse_kernel(ids, lo, own, hi, smooth, o0, o1, o2, o3, rhs, diag, xa, xb, step, adj):
@@ -180,7 +188,7 @@
         xa[q + 1] = d
         return 0
 
-    lax.fori_loop(0, half, begin, 0)
+    lax.fori_loop(0, half, begin, 0, unroll=True)
     old, new = xa, xb
     for damp, gain in pairs[: S_C - 1]:
 
@@ -193,7 +201,7 @@
             new[q + 1] = v + d
             return 0
 
-        lax.fori_loop(0, half, sweep, 0)
+        lax.fori_loop(0, half, sweep, 0, unroll=True)
         old, new = new, old
 
     copy_r = lax.broadcasted_iota(jnp.int32, (rows, 2 * HALO), 0)
@@ -206,7 +214,7 @@
             adj[2 * q + j] = smooth[2 * q + j] + c
         return 0
 
-    lax.fori_loop(0, half, refine, 0)
+    lax.fori_loop(0, half, refine, 0, unroll=True)
     adj[NR] = jnp.zeros((rows, MAIN), F32)
     for m, out in enumerate((o0, o1, o2, o3)):
         base = (ids[4] ^ m) * LAYERS
@@ -282,8 +290,20 @@
                 pairs.append((i * rad_n + k, to * rad_n + (k ^ flip(i) ^ flip(to))))
         return lax.ppermute(v, ("lat", "rad"), pairs)
 
-    pieces = call(pack_windows, [struct(LAYERS, ROWS, PACKED)] * 4, [], ids, source, kappa)
+    slab = pltpu.VMEM((LAYERS, ROWS, 1024), F32)
+    pieces = pl.pallas_call(
+        pack_windows,
+        out_shape=[struct(LAYERS, ROWS, PACKED)] * 4,
+        in_specs=[pl.BlockSpec(memory_space=pltpu.SMEM)] + [pl.BlockSpec(memory_space=pltpu.HBM)] * 2,
+        out_specs=[pl.BlockSpec(memory_space=pltpu.VMEM)] * 4,
+        scratch_shapes=[slab, slab, pltpu.SemaphoreType.DMA((2, LAYERS))],
+        compiler_params=VMEM,
+    )(ids, source, kappa)
     pieces = trade(pieces)
+    near, ahead = lax.optimization_barrier((pieces[1], forward))
+    forward_x = lax.ppermute(ahead[:, :1], "lat", [((i + 1) % lat_n, i) for i in range(lat_n)])
+    forward_r = lax.ppermute(ahead[:1], "rad", [(k + 1, k) for k in range(rad_n - 1)])
+    forward_x, forward_r, *pieces = lax.optimization_barrier((forward_x, forward_r, pieces[0], near, *pieces[2:]))
     up, down = call(pack_rows, [struct(NR, HALO, PACKED)] * 2, [], ids, *pieces)
     lo = beside(up, 1)
     hi = beside(down, -1)
@@ -313,8 +333,6 @@
         smooth,
     )
     backs = trade(backs)
-    forward_x = lax.ppermute(forward[:, :1], "lat", [((i + 1) % lat_n, i) for i in range(lat_n)])
-    forward_r = lax.ppermute(forward[:1], "rad", [(k + 1, k) for k in range(rad_n - 1)])
     adjoint, gradient = call(
         gradient_kernel,
         [struct(LAYERS, ROWS, 1024)] * 2,

time: 95.3 us -> 83 us (0.87)
  Pallas kernels: 27.9 us -> 10.8 us
  waiting for transfers between devices: 22.8 us -> 25.8 us
  starting transfers between devices: 41.7 us -> 43.5 us
    pallas_call x5 -> x4, Pallas kernels: 27.9 us -> 9.39 us  [call(): pl.pallas_call(kernel, out_shape=outs, in_specs=[pl.BlockSpec(memory_spac...]
    ppermute x4, waiting for transfers between devices: 9.6 us -> 15.5 us  [beside(): return lax.ppermute(v, ('lat', 'rad'), pairs)]
    ppermute x6, waiting for transfers between devices: 11.7 us -> 6.87 us  [trade(): lax.ppermute(pieces[m], 'rad', [(k, k ^ m) for k in range(rad_n)])]
    ppermute x6, starting transfers between devices: 16.8 us -> 20.4 us  [trade(): lax.ppermute(pieces[m], 'rad', [(k, k ^ m) for k in range(rad_n)])]
    ppermute x4, starting transfers between devices: 16.9 us -> 13.7 us  [beside(): return lax.ppermute(v, ('lat', 'rad'), pairs)]
    ppermute x2, waiting for transfers between devices: 1.48 us -> 3.43 us  [the longest x1 3.43 us: body(): lax.ppermute(ahead[:, :1], 'lat', [((i + 1) % lat_n, i) for i in range(la...]
    pallas_call x0 -> x1, Pallas kernels: none -> 1.45 us  [body(): pl.pallas_call(pack_windows, out_shape=[struct(LAYERS, ROWS, PACKED)] * 4...]
    ppermute x2, starting transfers between devices: 7.99 us -> 9.39 us  [the longest x1 7.33 us: body(): lax.ppermute(ahead[:, :1], 'lat', [((i + 1) % lat_n, i) for i in range(la...]
  transfers between devices with their start and end apart: 12 -> 12, of which waited for: 6 -> 7; matrix products, arithmetic and copies ran while one was open for 0% -> 0% of each run, Pallas kernels for 0% -> 0%
where the time goes in v1:
time: 83 us; the launch traced here: 82.8 us
  starting transfers between devices  43.5 us (52%)
  waiting for transfers between devices  25.8 us (31%)
  Pallas kernels  10.8 us (13%)
  local copies, waits for them, and re-layouts  2.01 us (2%)
    ppermute x6, starting transfers between devices, trade(): lax.ppermute(pieces[m], 'rad', [(k, k ^ m) for k in range(rad_n)])  20.4 us
    ppermute x4, waiting for transfers between devices, beside(): return lax.ppermute(v, ('lat', 'rad'), pairs)  15.5 us
    ppermute x4, starting transfers between devices, beside(): return lax.ppermute(v, ('lat', 'rad'), pairs)  13.7 us
    pallas_call x4, Pallas kernels, call(): pl.pallas_call(kernel, out_shape=outs, in_specs=[pl.BlockSpec(memory_spac...  9.39 us
    ppermute x1, starting transfers between devices, body(): lax.ppermute(ahead[:, :1], 'lat', [((i + 1) % lat_n, i) for i in range(la...  7.33 us
    ppermute x6, waiting for transfers between devices, trade(): lax.ppermute(pieces[m], 'rad', [(k, k ^ m) for k in range(rad_n)])  6.87 us
    ppermute x1, waiting for transfers between devices, body(): lax.ppermute(ahead[:, :1], 'lat', [((i + 1) % lat_n, i) for i in range(la...  3.43 us
    ppermute x1, starting transfers between devices, body(): lax.ppermute(ahead[:1], 'rad', [(k + 1, k) for k in range(rad_n - 1)])  2.06 us
  transfers between devices with their start and end apart: 12, of which 7 were waited for; matrix products, arithmetic and copies ran while one was open for 0% of the time, Pallas kernels for 0%

profile of v1, /device:TPU:1, one launch (start us, length us, event | category | flops | bytes accessed | tf_op | source)
XLA Modules:
  0.0 82.8 jit_solution(12936813969188429666)
XLA Ops:
  0.7 0.1 stack.23.ids
  0.7 0.0 copy-start.2
  0.8 0.9 %copy-done.2 = f32[4,16,1024]{2,1,0:T(8,128)S(1)} copy-done((f32[4,16,1024]{2,1,0:T(8,128)S(1)}, f32[4,16,1024]{2,1,0:T(8,128)}, u32[]{:S(2)}) %copy-start.2) | copy-done | bytes 262168
  1.7 0.0 copy-start.3
  1.7 0.9 %copy-done.3 = f32[4,16,1024]{2,1,0:T(8,128)S(1)} copy-done((f32[4,16,1024]{2,1,0:T(8,128)S(1)}, f32[4,16,1024]{2,1,0:T(8,128)}, u32[]{:S(2)}) %copy-start.3) | copy-done | bytes 262168
  2.7 0.0 copy-start
  2.7 1.4 %shard_map.59 = (f32[4,16,640]{2,1,0:T(8,128)S(1)}, f32[4,16,640]{2,1,0:T(8,128)S(1)}, f32[4,16,640]{2,1,0:T(8,128)S(1)}, f32[4,16,640]{2,1,0:T(8,128)S(1)}) custom-call(s32[5]{0:T(128)S(1)} %stack.23.ids, f32[4,16,1024]{2,1,0:T(8,128)S(1)} %copy-done.2, f32[4,16,1024]{2,1,0:T(8,128)S(1)} %copy-done.3), custom_call_target="tpu_custom_call" | custom-call | tf_op jit(solution)/shard_map/pallas_call | solution.py:294
  4.1 3.3 %collective-permute-start = (f32[4,16,640]{2,1,0:T(8,128)S(1)}, f32[4,16,640]{2,1,0:T(8,128)S(1)}, u32[]{:S(2)}, u32[]{:S(2)}) collective-permute-start(f32[4,16,640]{2,1,0:T(8,128)S(1)} %get-tuple-element.22), channel_id=1, source_target_pairs={{0,1},{1,0},{2,3},{3,2},{4,5},{5,4},{6,7},{7,6},{8,9},{9,8},{10,11... | collective-permute-start | bytes 491528 | tf_op jit(solution)/shard_map/ppermute | solution.py:282
  7.4 5.2 %collective-permute-start.3 = (f32[4,16,640]{2,1,0:T(8,128)S(1)}, f32[4,16,640]{2,1,0:T(8,128)S(1)}, u32[]{:S(2)}, u32[]{:S(2)}) collective-permute-start(f32[4,16,640]{2,1,0:T(8,128)S(1)} %get-tuple-element.26), channel_id=1, source_target_pairs={{0,2},{1,3},{2,0},{3,1},{4,6},{5,7},{6,4},{7,5},{8,10},{9,11},{10,... | collective-permute-start | bytes 491528 | tf_op jit(solution)/shard_map/ppermute | solution.py:282
  12.6 0.4 collective-permute-start.4
  13.1 0.0 collective-permute-done.p1
  13.1 0.0 copy-done
  13.1 2.1 %collective-permute-start.2 = (f32[1,16,1024]{2,1,0:T(8,128)S(1)}, f32[1,16,1024]{2,1,0:T(8,128)S(1)}, u32[]{:S(2)}, u32[]{:S(2)}) collective-permute-start(f32[1,16,1024]{2,1,0:T(8,128)S(1)} %slice.7), channel_id=1, source_target_pairs={{1,0},{2,1},{3,2},{5,4},{6,5},{7,6},{9,8},{10,9},{11,10},{13,12},{... | collective-permute-start | bytes 196616 | tf_op jit(solution)/shard_map/ppermute | solution.py:305
  15.2 7.3 %collective-permute-start.1 = (f32[4,1,1024]{2,1,0:T(1,128)S(1)}, f32[4,1,1024]{2,1,0:T(1,128)S(1)}, u32[]{:S(2)}, u32[]{:S(2)}) collective-permute-start(f32[4,1,1024]{2,1,0:T(1,128)S(1)} %slice.6), channel_id=1, source_target_pairs={{4,0},{8,4},{12,8},{16,12},{20,16},{24,20},{28,24},{32,28},{36,32}... | collective-permute-start | bytes 49160 | tf_op jit(solution)/shard_map/ppermute | solution.py:304
  22.5 0.0 collective-permute-done.3.p2
  22.5 2.3 %collective-permute-done.4.p3 = f32[4,16,640]{2,1,0:T(8,128)S(1)} collective-permute-done((f32[4,16,640]{2,1,0:T(8,128)S(1)}, f32[4,16,640]{2,1,0:T(8,128)S(1)}, u32[]{:S(2)}, u32[]{:S(2)}) %collective-permute-start.4) | collective-permute-done | bytes 163872 | tf_op jit(solution)/shard_map/ppermute | solution.py:282
  24.8 3.4 %collective-permute-done.1.forward_x = f32[4,1,1024]{2,1,0:T(1,128)S(1)} collective-permute-done((f32[4,1,1024]{2,1,0:T(1,128)S(1)}, f32[4,1,1024]{2,1,0:T(1,128)S(1)}, u32[]{:S(2)}, u32[]{:S(2)}) %collective-permute-start.1) | collective-permute-done | bytes 16416 | tf_op jit(solution)/shard_map/ppermute | solution.py:304
  28.2 0.0 collective-permute-done.2.forward_r
  28.2 0.6 shard_map.60
  28.8 1.8 %collective-permute-start.5 = (f32[16,8,640]{2,1,0:T(8,128)S(1)}, f32[16,8,640]{2,1,0:T(8,128)S(1)}, u32[]{:S(2)}, u32[]{:S(2)}) collective-permute-start(f32[16,8,640]{2,1,0:T(8,128)S(1)} %get-tuple-element.32), channel_id=1, source_target_pairs={{0,4},{1,5},{2,6},{3,7},{4,8},{5,9},{6,10},{7,11},{8,12},{9,13},{1... | collective-permute-start | bytes 983048 | tf_op jit(solution)/shard_map/ppermute | solution.py:291
  30.6 5.2 %collective-permute-start.6 = (f32[16,8,640]{2,1,0:T(8,128)S(1)}, f32[16,8,640]{2,1,0:T(8,128)S(1)}, u32[]{:S(2)}, u32[]{:S(2)}) collective-permute-start(f32[16,8,640]{2,1,0:T(8,128)S(1)} %get-tuple-element.33), channel_id=1, source_target_pairs={{0,254},{1,255},{2,252},{3,253},{4,0},{5,1},{6,2},{7,3},{8,4},{9,5... | collective-permute-start | bytes 983048 | tf_op jit(solution)/shard_map/ppermute | solution.py:291
  35.8 6.6 %collective-permute-done.5.lo = f32[16,8,640]{2,1,0:T(8,128)S(1)} collective-permute-done((f32[16,8,640]{2,1,0:T(8,128)S(1)}, f32[16,8,640]{2,1,0:T(8,128)S(1)}, u32[]{:S(2)}, u32[]{:S(2)}) %collective-permute-start.5) | collective-permute-done | bytes 327712 | tf_op jit(solution)/shard_map/ppermute | solution.py:291
  42.4 0.0 collective-permute-done.6.hi
  42.4 4.9 %shard_map.61 = (f32[16,24,256]{2,1,0:T(8,128)S(1)}, f32[8,8,384]{2,1,0:T(8,128)S(1)}) custom-call(s32[5]{0:T(128)S(1)} %stack.23.ids, f32[4,16,640]{2,1,0:T(8,128)S(1)} %get-tuple-element.28.p0, f32[4,16,640]{2,1,0:T(8,128)S(1)} %collective-permute-done.p1, f32[4,16,640]{2,1,0:T(8,128)S(1)} %collective-permute-done.3.p2, ...), custom_call_target="tpu_custom_call" | custom-call | tf_op jit(solution)/shard_map/pallas_call | solution.py:257
  47.3 6.7 %collective-permute-start.8 = (f32[8,8,384]{2,1,0:T(8,128)S(1)}, f32[8,8,384]{2,1,0:T(8,128)S(1)}, u32[]{:S(2)}, u32[]{:S(2)}) collective-permute-start(f32[8,8,384]{2,1,0:T(8,128)S(1)} %get-tuple-element.34.own), channel_id=1, source_target_pairs={{0,254},{1,255},{2,252},{3,253},{4,0},{5,1},{6,2},{7,3},{8,4},{9,5... | collective-permute-start | bytes 294920 | tf_op jit(solution)/shard_map/ppermute | solution.py:291
  54.0 0.0 collective-permute-start.7
  54.0 1.6 %collective-permute-done.8.hi = f32[8,8,384]{2,1,0:T(8,128)S(1)} collective-permute-done((f32[8,8,384]{2,1,0:T(8,128)S(1)}, f32[8,8,384]{2,1,0:T(8,128)S(1)}, u32[]{:S(2)}, u32[]{:S(2)}) %collective-permute-start.8) | collective-permute-done | bytes 98336 | tf_op jit(solution)/shard_map/ppermute | solution.py:291
  55.6 7.3 %collective-permute-done.7.lo = f32[8,8,384]{2,1,0:T(8,128)S(1)} collective-permute-done((f32[8,8,384]{2,1,0:T(8,128)S(1)}, f32[8,8,384]{2,1,0:T(8,128)S(1)}, u32[]{:S(2)}, u32[]{:S(2)}) %collective-permute-start.7) | collective-permute-done | bytes 98336 | tf_op jit(solution)/shard_map/ppermute | solution.py:291
  62.9 0.0 copy-start.1
  62.9 2.3 %shard_map.62 = (f32[11,8,256]{2,1,0:T(8,128)S(1)}, f32[11,8,256]{2,1,0:T(8,128)S(1)}, f32[11,8,256]{2,1,0:T(8,128)S(1)}, f32[11,8,256]{2,1,0:T(8,128)S(1)}) custom-call(s32[5]{0:T(128)S(1)} %stack.23.ids, f32[8,8,384]{2,1,0:T(8,128)S(1)} %collective-permute-done.7.lo, f32[8,8,384]{2,1,0:T(8,128)S(1)} %get-tuple-element.34.own, ...), custom_call_target="tpu_custom_call" | custom-call | tf_op jit(solution)/shard_map/pallas_call | solution.py:257
  65.2 5.8 %collective-permute-start.9 = (f32[11,8,256]{2,1,0:T(8,128)S(1)}, f32[11,8,256]{2,1,0:T(8,128)S(1)}, u32[]{:S(2)}, u32[]{:S(2)}) collective-permute-start(f32[11,8,256]{2,1,0:T(8,128)S(1)} %get-tuple-element.37), channel_id=1, source_target_pairs={{0,1},{1,0},{2,3},{3,2},{4,5},{5,4},{6,7},{7,6},{8,9},{9,8},{10,11... | collective-permute-start | bytes 270344 | tf_op jit(solution)/shard_map/ppermute | solution.py:282
  71.0 0.0 collective-permute-start.10
  71.1 5.6 %collective-permute-start.11 = (f32[11,8,256]{2,1,0:T(8,128)S(1)}, f32[11,8,256]{2,1,0:T(8,128)S(1)}, u32[]{:S(2)}, u32[]{:S(2)}) collective-permute-start(f32[11,8,256]{2,1,0:T(8,128)S(1)} %get-tuple-element.39), channel_id=1, source_target_pairs={{0,3},{1,2},{2,1},{3,0},{4,7},{5,6},{6,5},{7,4},{8,11},{9,10},{10,... | collective-permute-start | bytes 270344 | tf_op jit(solution)/shard_map/ppermute | solution.py:282
  76.7 0.0 collective-permute-done.9.p1
  76.7 2.4 %collective-permute-done.10.p2 = f32[11,8,256]{2,1,0:T(8,128)S(1)} collective-permute-done((f32[11,8,256]{2,1,0:T(8,128)S(1)}, f32[11,8,256]{2,1,0:T(8,128)S(1)}, u32[]{:S(2)}, u32[]{:S(2)}) %collective-permute-start.10) | collective-permute-done | bytes 90144 | tf_op jit(solution)/shard_map/ppermute | solution.py:282
  79.1 2.1 %collective-permute-done.11.p3 = f32[11,8,256]{2,1,0:T(8,128)S(1)} collective-permute-done((f32[11,8,256]{2,1,0:T(8,128)S(1)}, f32[11,8,256]{2,1,0:T(8,128)S(1)}, u32[]{:S(2)}, u32[]{:S(2)}) %collective-permute-start.11) | collective-permute-done | bytes 90144 | tf_op jit(solution)/shard_map/ppermute | solution.py:282
  81.2 0.0 copy-done.1
  81.2 1.6 %shard_map.63 = (f32[4,16,1024]{2,1,0:T(8,128)}, f32[4,16,1024]{2,1,0:T(8,128)}) custom-call(s32[5]{0:T(128)S(1)} %stack.23.ids, f32[11,8,256]{2,1,0:T(8,128)S(1)} %get-tuple-element.36.p0, f32[11,8,256]{2,1,0:T(8,128)S(1)} %collective-permute-done.9.p1, f32[11,8,256]{2,1,0:T(8,128)S(1)} %collective-permute-done.10.p2, ...), custom_call_target="tpu_custom_call" | custom-call | tf_op jit(solution)/shard_map/pallas_call | solution.py:257
  (2 shorter events, 0.0 us)
Async XLA Ops:
  0.7 1.0 %copy-start.2 = (f32[4,16,1024]{2,1,0:T(8,128)S(1)}, f32[4,16,1024]{2,1,0:T(8,128)}, u32[]{:S(2)}) copy-start(f32[4,16,1024]{2,1,0:T(8,128)} %source_hbm.1) | copy-start | bytes 786436
  1.7 0.9 %copy-start.3 = (f32[4,16,1024]{2,1,0:T(8,128)S(1)}, f32[4,16,1024]{2,1,0:T(8,128)}, u32[]{:S(2)}) copy-start(f32[4,16,1024]{2,1,0:T(8,128)} %kappa_hbm.1) | copy-start | bytes 786436
  2.7 10.4 %copy-start = (f32[4,16,1024]{2,1,0:T(8,128)S(1)}, f32[4,16,1024]{2,1,0:T(8,128)}, u32[]{:S(2)}) copy-start(f32[4,16,1024]{2,1,0:T(8,128)} %forward.1) | copy-start | bytes 786436
  4.1 9.0 %collective-permute-start = (f32[4,16,640]{2,1,0:T(8,128)S(1)}, f32[4,16,640]{2,1,0:T(8,128)S(1)}, u32[]{:S(2)}, u32[]{:S(2)}) collective-permute-start(f32[4,16,640]{2,1,0:T(8,128)S(1)} %get-tuple-element.22), channel_id=1, source_target_pairs={{0,1},{1,0},{2,3},{3,2},{4,5},{5,4},{6,7},{7,6},{8,9},{9,8},{10,11... | collective-permute-start | bytes 491528 | tf_op jit(solution)/shard_map/ppermute | solution.py:282
  7.4 15.1 %collective-permute-start.3 = (f32[4,16,640]{2,1,0:T(8,128)S(1)}, f32[4,16,640]{2,1,0:T(8,128)S(1)}, u32[]{:S(2)}, u32[]{:S(2)}) collective-permute-start(f32[4,16,640]{2,1,0:T(8,128)S(1)} %get-tuple-element.26), channel_id=1, source_target_pairs={{0,2},{1,3},{2,0},{3,1},{4,6},{5,7},{6,4},{7,5},{8,10},{9,11},{10,... | collective-permute-start | bytes 491528 | tf_op jit(solution)/shard_map/ppermute | solution.py:282
  12.6 12.2 %collective-permute-start.4 = (f32[4,16,640]{2,1,0:T(8,128)S(1)}, f32[4,16,640]{2,1,0:T(8,128)S(1)}, u32[]{:S(2)}, u32[]{:S(2)}) collective-permute-start(f32[4,16,640]{2,1,0:T(8,128)S(1)} %get-tuple-element.27), channel_id=1, source_target_pairs={{0,3},{1,2},{2,1},{3,0},{4,7},{5,6},{6,5},{7,4},{8,11},{9,10},{10,... | collective-permute-start | bytes 491528 | tf_op jit(solution)/shard_map/ppermute | solution.py:282
  13.1 15.1 %collective-permute-start.2 = (f32[1,16,1024]{2,1,0:T(8,128)S(1)}, f32[1,16,1024]{2,1,0:T(8,128)S(1)}, u32[]{:S(2)}, u32[]{:S(2)}) collective-permute-start(f32[1,16,1024]{2,1,0:T(8,128)S(1)} %slice.7), channel_id=1, source_target_pairs={{1,0},{2,1},{3,2},{5,4},{6,5},{7,6},{9,8},{10,9},{11,10},{13,12},{... | collective-permute-start | bytes 196616 | tf_op jit(solution)/shard_map/ppermute | solution.py:305
  15.2 13.1 %collective-permute-start.1 = (f32[4,1,1024]{2,1,0:T(1,128)S(1)}, f32[4,1,1024]{2,1,0:T(1,128)S(1)}, u32[]{:S(2)}, u32[]{:S(2)}) collective-permute-start(f32[4,1,1024]{2,1,0:T(1,128)S(1)} %slice.6), channel_id=1, source_target_pairs={{4,0},{8,4},{12,8},{16,12},{20,16},{24,20},{28,24},{32,28},{36,32}... | collective-permute-start | bytes 49160 | tf_op jit(solution)/shard_map/ppermute | solution.py:304
  28.8 13.5 %collective-permute-start.5 = (f32[16,8,640]{2,1,0:T(8,128)S(1)}, f32[16,8,640]{2,1,0:T(8,128)S(1)}, u32[]{:S(2)}, u32[]{:S(2)}) collective-permute-start(f32[16,8,640]{2,1,0:T(8,128)S(1)} %get-tuple-element.32), channel_id=1, source_target_pairs={{0,4},{1,5},{2,6},{3,7},{4,8},{5,9},{6,10},{7,11},{8,12},{9,13},{1... | collective-permute-start | bytes 983048 | tf_op jit(solution)/shard_map/ppermute | solution.py:291
  30.6 11.8 %collective-permute-start.6 = (f32[16,8,640]{2,1,0:T(8,128)S(1)}, f32[16,8,640]{2,1,0:T(8,128)S(1)}, u32[]{:S(2)}, u32[]{:S(2)}) collective-permute-start(f32[16,8,640]{2,1,0:T(8,128)S(1)} %get-tuple-element.33), channel_id=1, source_target_pairs={{0,254},{1,255},{2,252},{3,253},{4,0},{5,1},{6,2},{7,3},{8,4},{9,5... | collective-permute-start | bytes 983048 | tf_op jit(solution)/shard_map/ppermute | solution.py:291
  47.3 8.3 %collective-permute-start.8 = (f32[8,8,384]{2,1,0:T(8,128)S(1)}, f32[8,8,384]{2,1,0:T(8,128)S(1)}, u32[]{:S(2)}, u32[]{:S(2)}) collective-permute-start(f32[8,8,384]{2,1,0:T(8,128)S(1)} %get-tuple-element.34.own), channel_id=1, source_target_pairs={{0,254},{1,255},{2,252},{3,253},{4,0},{5,1},{6,2},{7,3},{8,4},{9,5... | collective-permute-start | bytes 294920 | tf_op jit(solution)/shard_map/ppermute | solution.py:291
  54.0 8.9 %collective-permute-start.7 = (f32[8,8,384]{2,1,0:T(8,128)S(1)}, f32[8,8,384]{2,1,0:T(8,128)S(1)}, u32[]{:S(2)}, u32[]{:S(2)}) collective-permute-start(f32[8,8,384]{2,1,0:T(8,128)S(1)} %get-tuple-element.34.own), channel_id=1, source_target_pairs={{0,4},{1,5},{2,6},{3,7},{4,8},{5,9},{6,10},{7,11},{8,12},{9,13},{1... | collective-permute-start | bytes 294920 | tf_op jit(solution)/shard_map/ppermute | solution.py:291
  62.9 18.4 %copy-start.1 = (f32[4,16,1024]{2,1,0:T(8,128)S(1)}, f32[4,16,1024]{2,1,0:T(8,128)}, u32[]{:S(2)}) copy-start(f32[4,16,1024]{2,1,0:T(8,128)} %viscosity.1) | copy-start | bytes 786436
  65.2 11.5 %collective-permute-start.9 = (f32[11,8,256]{2,1,0:T(8,128)S(1)}, f32[11,8,256]{2,1,0:T(8,128)S(1)}, u32[]{:S(2)}, u32[]{:S(2)}) collective-permute-start(f32[11,8,256]{2,1,0:T(8,128)S(1)} %get-tuple-element.37), channel_id=1, source_target_pairs={{0,1},{1,0},{2,3},{3,2},{4,5},{5,4},{6,7},{7,6},{8,9},{9,8},{10,11... | collective-permute-start | bytes 270344 | tf_op jit(solution)/shard_map/ppermute | solution.py:282
  71.0 8.1 %collective-permute-start.10 = (f32[11,8,256]{2,1,0:T(8,128)S(1)}, f32[11,8,256]{2,1,0:T(8,128)S(1)}, u32[]{:S(2)}, u32[]{:S(2)}) collective-permute-start(f32[11,8,256]{2,1,0:T(8,128)S(1)} %get-tuple-element.38), channel_id=1, source_target_pairs={{0,2},{1,3},{2,0},{3,1},{4,6},{5,7},{6,4},{7,5},{8,10},{9,11},{10,... | collective-permute-start | bytes 270344 | tf_op jit(solution)/shard_map/ppermute | solution.py:282
  71.1 10.2 %collective-permute-start.11 = (f32[11,8,256]{2,1,0:T(8,128)S(1)}, f32[11,8,256]{2,1,0:T(8,128)S(1)}, u32[]{:S(2)}, u32[]{:S(2)}) collective-permute-start(f32[11,8,256]{2,1,0:T(8,128)S(1)} %get-tuple-element.39), channel_id=1, source_target_pairs={{0,3},{1,2},{2,1},{3,0},{4,7},{5,6},{6,5},{7,4},{8,11},{9,10},{10,... | collective-permute-start | bytes 270344 | tf_op jit(solution)/shard_map/ppermute | solution.py:282

commit v2 on v1

--- a/solution.py
+++ b/solution.py
@@ -64,11 +64,13 @@
         out[:, :, 2 * MAIN :] = jnp.where(right | left, edge_s, edge_k)
 
 
-def pack_rows(ids, p0, p1, p2, p3, up, down):
+def pack_rows(ids, p0, p1, p2, p3, near, far):
+    near_rows = pl.ds(pl.multiple_of((1 - ids[5]) * HALO, HALO), HALO)
+    far_rows = pl.ds(pl.multiple_of(ids[5] * HALO, HALO), HALO)
     for m, piece in enumerate((p0, p1, p2, p3)):
         at = pl.ds((ids[4] ^ m) * LAYERS, LAYERS)
-        up[at] = piece[:, HALO:, :]
-        down[at] = piece[:, :HALO, :]
+        near[at] = piece[:, near_rows, :]
+        far[at] = piece[:, far_rows, :]
 
 
 def spread(packed, rhs, diag):
@@ -93,7 +95,7 @@
     )
 
 
-def fine_kernel(ids, p0, p1, p2, p3, lo, hi, smooth, packed, rhs, diag, xa, xb, step):
+def fine_kernel(ids, p0, p1, p2, p3, near, far, packed, o0, o1, o2, o3, rhs, diag, xa, xb, step):
     me = ids[4]
     for m, piece in enumerate((p0, p1, p2, p3)):
         base = (me ^ m) * LAYERS
@@ -105,6 +107,8 @@
 
         lax.fori_loop(0, LAYERS, fill, 0, unroll=True)
 
+    near_at = pl.ds(pl.multiple_of((1 - ids[5]) * (HALO + ROWS), HALO), HALO)
+    far_at = pl.ds(pl.multiple_of(ids[5] * (HALO + ROWS), HALO), HALO)
     first, pairs = coefficients(*FINE, S_F)
     zero = jnp.zeros((2 * ROWS, WIDE), F32)
     xa[0] = zero
@@ -113,9 +117,8 @@
     xb[NR + 1] = zero
 
     def begin(r, _):
-        spread(lo[r], rhs.at[r, pl.ds(0, HALO)], diag.at[r, pl.ds(0, HALO)])
-        top = pl.ds(HALO + ROWS, HALO)
-        spread(hi[r], rhs.at[r, top], diag.at[r, top])
+        spread(near[r], rhs.at[r, near_at], diag.at[r, near_at])
+        spread(far[r], rhs.at[r, far_at], diag.at[r, far_at])
         d = rhs[r] * first
         step[r] = d
         xa[r + 1] = d
@@ -128,8 +131,8 @@
 
         def sweep(r, _, old=old, new=new, damp=damp, gain=gain):
             v = old[r + 1]
-            near = old[r] + old[r + 2] + lateral(v, 1, 1)
-            resid = rhs[r] - diag[r] * v + near
+            around = old[r] + old[r + 2] + lateral(v, 1, 1)
+            resid = rhs[r] - diag[r] * v + around
             d = damp * step[r] + gain * resid
             step[r] = d
             new[r + 1] = v + d
@@ -154,19 +157,26 @@
         for j in range(2):
             r = 2 * q + j
             v = old[r + 1]
-            near = old[r] + old[r + 2] + lateral(v, 1, 1)
-            resid = (rhs[r] - diag[r] * v + near)[HALO : HALO + ROWS]
+            around = old[r] + old[r + 2] + lateral(v, 1, 1)
+            resid = (rhs[r] - diag[r] * v + around)[HALO : HALO + ROWS]
             total = resid if total is None else total + resid
             k = diag[r, HALO : HALO + ROWS] - 6.0
             diags = k if diags is None else diags + k
-            smooth[r] = v[HALO:, :MAIN]
         packed[q] = jnp.where(even_lane, block_mean(total), block_mean(diags))
         return 0
 
     lax.fori_loop(0, NR // 2, residual, 0, unroll=True)
-
-
-def coarse_kernel(ids, lo, own, hi, smooth, o0, o1, o2, o3, rhs, diag, xa, xb, step, adj):
+    for m, out in enumerate((o0, o1, o2, o3)):
+        base = (me ^ m) * LAYERS + 1
+        for j in range(LAYERS + 1):
+            for h in range(2):
+                out[2 * j + h] = old[base + j, (1 + h) * HALO : (2 + h) * HALO, :MAIN]
+        for j in range(LAYERS):
+            out[2 * LAYERS + 2, pl.ds(j, 1)] = old[base + j, 3 * HALO : 3 * HALO + 1, :MAIN]
+        out[2 * LAYERS + 2, pl.ds(LAYERS, 4)] = jnp.zeros((4, MAIN), F32)
+
+
+def coarse_kernel(ids, near, own, far, o0, o1, o2, o3, rhs, diag, xa, xb, step):
     first, pairs = coefficients(*COARSE, S_C)
     half = NR // 2
     rows = 3 * HALO
@@ -178,9 +188,9 @@
     even = lax.rem(lanes((HALO, WIDE)), 2) == 0
 
     def begin(q, _):
-        for part, src in enumerate((lo, own, hi)):
+        for part, src in (((1 - ids[5]) * 2, near), (1, own), (ids[5] * 2, far)):
             v = src[q]
-            at = pl.ds(part * HALO, HALO)
+            at = pl.ds(pl.multiple_of(part * HALO, HALO), HALO)
             rhs[q, at] = jnp.where(even, v, pltpu.roll(v, 1, 1))
             diag[q, at] = jnp.where(even, pltpu.roll(v, WIDE - 1, 1), v) + 1.5
         d = rhs[q] * first
@@ -194,8 +204,8 @@
 
         def sweep(q, _, old=old, new=new, damp=damp, gain=gain):
             v = old[q + 1]
-            near = old[q] + old[q + 2] + lateral(v, 1, 2)
-            resid = rhs[q] - diag[q] * v + 0.25 * near
+            around = old[q] + old[q + 2] + lateral(v, 1, 2)
+            resid = rhs[q] - diag[q] * v + 0.25 * around
             d = damp * step[q] + gain * resid
             step[q] = d
             new[q + 1] = v + d
@@ -204,37 +214,52 @@
         lax.fori_loop(0, half, sweep, 0, unroll=True)
         old, new = new, old
 
-    copy_r = lax.broadcasted_iota(jnp.int32, (rows, 2 * HALO), 0)
-    copy_c = lax.broadcasted_iota(jnp.int32, (rows, 2 * HALO), 1)
+    even = even[:, :MAIN]
+    top = lax.broadcasted_iota(jnp.int32, (HALO, MAIN), 0) == 0
+    own_rows = slice(HALO, 2 * HALO)
+    after = slice(2 * HALO, 2 * HALO + 1)
+    for m, out in enumerate((o0, o1, o2, o3)):
+        base = (ids[4] ^ m) * (LAYERS // 2) + 1
+        a, b, c = (old[base + j, own_rows, :MAIN] for j in range(3))
+        out[0] = jnp.where(even, a, b)
+        out[1] = jnp.where(even, c, jnp.where(top, old[base, after, :MAIN], old[base + 1, after, :MAIN]))
+
+
+def gradient_kernel(ids, *refs):
+    smooths, fixes = refs[:4], refs[4:8]
+    forward, forward_x, forward_r, viscosity, adjoint, gradient, above, beyond, fix = refs[8:]
+    for m in range(4):
+        at = pl.ds(pl.multiple_of(ids[m] * MAIN, 128), MAIN)
+        fix[:, :, at] = fixes[m][...]
+    even = lax.rem(lanes((HALO, 1024)), 2) == 0
+    low, high = fix[0], fix[1]
+    coarse = (
+        jnp.where(even, low, pltpu.roll(low, 1, 1)),
+        jnp.where(even, pltpu.roll(low, 1023, 1), low),
+        jnp.where(even, high, pltpu.roll(high, 1, 1)),
+    )
+    rest = jnp.where(even, pltpu.roll(high, 1023, 1), high)
+    copy_r = lax.broadcasted_iota(jnp.int32, (ROWS, HALO), 0)
+    copy_c = lax.broadcasted_iota(jnp.int32, (ROWS, HALO), 1)
     copy = jnp.where(lax.shift_right_logical(copy_r, 1) == copy_c, 1.0, 0.0).astype(F32)
-
-    def refine(q, _):
-        c = jnp.dot(copy, old[q + 1, HALO:, :MAIN], precision=lax.Precision.HIGHEST, preferred_element_type=F32)
-        for j in range(2):
-            adj[2 * q + j] = smooth[2 * q + j] + c
-        return 0
-
-    lax.fori_loop(0, half, refine, 0, unroll=True)
-    adj[NR] = jnp.zeros((rows, MAIN), F32)
-    for m, out in enumerate((o0, o1, o2, o3)):
-        base = (ids[4] ^ m) * LAYERS
-        for j in range(LAYERS + 1):
-            out[2 * j] = adj[base + j, 0:8]
-            out[2 * j + 1] = adj[base + j, 8:16]
-        for j in range(LAYERS):
-            out[2 * LAYERS + 2, pl.ds(j, 1)] = adj[base + j, 16:17]
-        out[2 * LAYERS + 2, pl.ds(LAYERS, 4)] = jnp.zeros((4, MAIN), F32)
-
-
-def gradient_kernel(ids, p0, p1, p2, p3, forward, forward_x, forward_r, viscosity, adjoint, gradient, above, beyond):
-    for m, piece in enumerate((p0, p1, p2, p3)):
+    for l, c in enumerate(coarse):
+        c = jnp.dot(copy, c, precision=lax.Precision.HIGHEST, preferred_element_type=F32)
+        for j in (2 * l, 2 * l + 1):
+            if j < LAYERS:
+                adjoint[j] = c
+            elif j == LAYERS:
+                above[...] = c
+    for j in range(LAYERS):
+        beyond[pl.ds(j, 1)] = rest[j // 2 : j // 2 + 1]
+    for m in range(4):
         at = pl.ds(pl.multiple_of(ids[m] * MAIN, 128), MAIN)
-        for j in range(LAYERS):
-            adjoint[j, 0:8, at] = piece[2 * j]
-            adjoint[j, 8:16, at] = piece[2 * j + 1]
-        above[0:8, at] = piece[2 * LAYERS]
-        above[8:16, at] = piece[2 * LAYERS + 1]
-        beyond[:, at] = piece[2 * LAYERS + 2]
+        piece = smooths[m]
+        for h in range(2):
+            rows = slice(h * HALO, (h + 1) * HALO)
+            for j in range(LAYERS):
+                adjoint[j, rows, at] += piece[2 * j + h]
+            above[rows, at] += piece[2 * LAYERS + h]
+        beyond[0:LAYERS, at] += piece[2 * LAYERS + 2, 0:LAYERS]
     last = lax.broadcasted_iota(jnp.int32, (ROWS, 1024), 0) == ROWS - 1
     for j in range(LAYERS):
         a = adjoint[j]
@@ -274,7 +299,8 @@
         return ((i // 4) % 2) * 2
 
     turn = flip(lat)
-    ids = jnp.stack([rad ^ turn, rad ^ 1 ^ turn, rad ^ 2 ^ turn, rad ^ 3 ^ turn, rad]).astype(jnp.int32)
+    ids = [rad ^ turn, rad ^ 1 ^ turn, rad ^ 2 ^ turn, rad ^ 3 ^ turn, rad, lat % 2]
+    ids = jnp.stack(ids).astype(jnp.int32)
 
     def trade(pieces):
         out = [pieces[0]]
@@ -282,13 +308,16 @@
             out.append(lax.ppermute(pieces[m], "rad", [(k, k ^ m) for k in range(rad_n)]))
         return out
 
-    def beside(v, way):
-        pairs = []
-        for i in range(lat_n):
-            to = (i + way) % lat_n
-            for k in range(rad_n):
-                pairs.append((i * rad_n + k, to * rad_n + (k ^ flip(i) ^ flip(to))))
-        return lax.ppermute(v, ("lat", "rad"), pairs)
+    def beside(near, far):
+        out = []
+        for shift, v in ((1, far), (0, near)):
+            pairs = []
+            for i in range(lat_n):
+                to = (((i + shift) ^ 1) - shift) % lat_n
+                for k in range(rad_n):
+                    pairs.append((i * rad_n + k, to * rad_n + (k ^ flip(i) ^ flip(to))))
+            out.append(lax.ppermute(v, ("lat", "rad"), pairs))
+        return out[1], out[0]
 
     slab = pltpu.VMEM((LAYERS, ROWS, 1024), F32)
     pieces = pl.pallas_call(
@@ -297,48 +326,49 @@
         in_specs=[pl.BlockSpec(memory_space=pltpu.SMEM)] + [pl.BlockSpec(memory_space=pltpu.HBM)] * 2,
         out_specs=[pl.BlockSpec(memory_space=pltpu.VMEM)] * 4,
         scratch_shapes=[slab, slab, pltpu.SemaphoreType.DMA((2, LAYERS))],
-        compiler_params=VMEM,
+        compiler_params=pltpu.CompilerParams(vmem_limit_bytes=56 * 1024 * 1024),
     )(ids, source, kappa)
     pieces = trade(pieces)
-    near, ahead = lax.optimization_barrier((pieces[1], forward))
+    first, ahead = lax.optimization_barrier((pieces[1], forward))
     forward_x = lax.ppermute(ahead[:, :1], "lat", [((i + 1) % lat_n, i) for i in range(lat_n)])
     forward_r = lax.ppermute(ahead[:1], "rad", [(k + 1, k) for k in range(rad_n - 1)])
-    forward_x, forward_r, *pieces = lax.optimization_barrier((forward_x, forward_r, pieces[0], near, *pieces[2:]))
-    up, down = call(pack_rows, [struct(NR, HALO, PACKED)] * 2, [], ids, *pieces)
-    lo = beside(up, 1)
-    hi = beside(down, -1)
+    forward_x, forward_r, *pieces = lax.optimization_barrier((forward_x, forward_r, pieces[0], first, *pieces[2:]))
+    near, far = call(pack_rows, [struct(NR, HALO, PACKED)] * 2, [], ids, *pieces)
+    near, far = beside(near, far)
     deep = (NR, 2 * ROWS, WIDE)
     padded = (NR + 2, 2 * ROWS, WIDE)
-    smooth, packed = call(
+    packed, *smooths = call(
         fine_kernel,
-        [struct(NR, 3 * HALO, MAIN), struct(NR // 2, HALO, WIDE)],
+        [struct(NR // 2, HALO, WIDE)] + [struct(2 * LAYERS + 3, HALO, MAIN)] * 4,
         [deep, deep, padded, padded, deep],
         ids,
         *pieces,
-        lo,
-        hi,
-    )
-    below = beside(packed, 1)
-    over = beside(packed, -1)
+        near,
+        far,
+    )
+    near, far = beside(packed, packed)
+    near, *smooths = lax.optimization_barrier((near, *smooths))
+    smooths = trade(smooths)
     deep = (NR // 2, 3 * HALO, WIDE)
     padded = (NR // 2 + 2, 3 * HALO, WIDE)
-    backs = call(
+    fixes = call(
         coarse_kernel,
-        [struct(2 * LAYERS + 3, 8, MAIN)] * 4,
-        [deep, deep, padded, padded, deep, (NR + 1, 3 * HALO, MAIN)],
+        [struct(2, HALO, MAIN)] * 4,
+        [deep, deep, padded, padded, deep],
         ids,
-        below,
+        near,
         packed,
-        over,
-        smooth,
-    )
-    backs = trade(backs)
+        far,
+    )
+    joined = lax.optimization_barrier((*smooths, *fixes))
+    smooths, fixes = joined[:4], trade(joined[4:])
     adjoint, gradient = call(
         gradient_kernel,
         [struct(LAYERS, ROWS, 1024)] * 2,
-        [(ROWS, 1024), (8, 1024)],
+        [(ROWS, 1024), (HALO, 1024), (2, HALO, 1024)],
         ids,
-        *backs,
+        *smooths,
+        *fixes,
         forward,
         forward_x,
         forward_r,

time: 83 us -> 82.9 us (level)
  waiting for transfers between devices: 25.8 us -> 21.1 us
  starting transfers between devices: 43.5 us -> 47.6 us
  Pallas kernels: 10.8 us -> 12.6 us
  local copies, waits for them, and re-layouts: 2.01 us -> 0.64 us
    ppermute x4, waiting for transfers between devices: 15.5 us -> 9.92 us  [beside(): out.append(lax.ppermute(v, ('lat', 'rad'), pairs))]
    ppermute x4, starting transfers between devices: 13.7 us -> 16 us  [beside(): out.append(lax.ppermute(v, ('lat', 'rad'), pairs))]
    unnamed x8, local copies, waits for them, and re-layouts: 1.91 us -> 0.02 us
    ppermute x6 -> x9, starting transfers between devices: 20.4 us -> 22.2 us  [trade(): lax.ppermute(pieces[m], 'rad', [(k, k ^ m) for k in range(rad_n)])]
    pallas_call x1, Pallas kernels: 1.45 us -> 2.86 us  [body(): pl.pallas_call(pack_windows, out_shape=[struct(LAYERS, ROWS, PACKED)] * 4...]
    ppermute x6 -> x9, waiting for transfers between devices: 6.87 us -> 7.74 us  [trade(): lax.ppermute(pieces[m], 'rad', [(k, k ^ m) for k in range(rad_n)])]
  transfers between devices with their start and end apart: 12 -> 15, of which waited for: 7 -> 7; matrix products, arithmetic and copies ran while one was open for 0% -> 0% of each run, Pallas kernels for 0% -> 3%
where the time goes in v2:
time: 82.9 us; the launch traced here: 82.7 us
  starting transfers between devices  47.6 us (57%)
  waiting for transfers between devices  21.1 us (25%)
  Pallas kernels  12.6 us (15%)
    ppermute x9, starting transfers between devices, trade(): lax.ppermute(pieces[m], 'rad', [(k, k ^ m) for k in range(rad_n)])  22.2 us
    ppermute x4, starting transfers between devices, beside(): out.append(lax.ppermute(v, ('lat', 'rad'), pairs))  16 us
    ppermute x4, waiting for transfers between devices, beside(): out.append(lax.ppermute(v, ('lat', 'rad'), pairs))  9.92 us
    pallas_call x4, Pallas kernels, call(): pl.pallas_call(kernel, out_shape=outs, in_specs=[pl.BlockSpec(memory_spac...  9.78 us
    ppermute x9, waiting for transfers between devices, trade(): lax.ppermute(pieces[m], 'rad', [(k, k ^ m) for k in range(rad_n)])  7.74 us
    ppermute x1, starting transfers between devices, body(): lax.ppermute(ahead[:, :1], 'lat', [((i + 1) % lat_n, i) for i in range(la...  7.33 us
    ppermute x1, waiting for transfers between devices, body(): lax.ppermute(ahead[:, :1], 'lat', [((i + 1) % lat_n, i) for i in range(la...  3.43 us
    pallas_call x1, Pallas kernels, body(): pl.pallas_call(pack_windows, out_shape=[struct(LAYERS, ROWS, PACKED)] * 4...  2.86 us
  transfers between devices with their start and end apart: 15, of which 7 were waited for; matrix products, arithmetic and copies ran while one was open for 0% of the time, Pallas kernels for 3%

profile of v2, /device:TPU:1, one launch (start us, length us, event | category | flops | bytes accessed | tf_op | source)
XLA Modules:
  0.0 82.7 jit_solution(11553058945830716041)
XLA Ops:
  0.7 0.6 stack.27.ids
  1.3 0.0 copy-start.1
  1.3 2.9 %shard_map.59 = (f32[4,16,640]{2,1,0:T(8,128)}, f32[4,16,640]{2,1,0:T(8,128)}, f32[4,16,640]{2,1,0:T(8,128)}, f32[4,16,640]{2,1,0:T(8,128)}) custom-call(s32[6]{0:T(128)} %stack.27.ids, f32[4,16,1024]{2,1,0:T(8,128)} %source_hbm.1, f32[4,16,1024]{2,1,0:T(8,128)} %kappa_hbm.1), custom_call_target="tpu_custom_call" | custom-call | tf_op jit(solution)/shard_map/pallas_call | solution.py:323
  4.1 0.0 copy-start
  4.2 3.3 %collective-permute-start = (f32[4,16,640]{2,1,0:T(8,128)}, f32[4,16,640]{2,1,0:T(8,128)S(1)}, u32[]{:S(2)}, u32[]{:S(2)}) collective-permute-start(f32[4,16,640]{2,1,0:T(8,128)} %get-tuple-element.38), channel_id=1, source_target_pairs={{0,1},{1,0},{2,3},{3,2},{4,5},{5,4},{6,7},{7,6},{8,9},{9,8},{10,11... | collective-permute-start | bytes 491528 | tf_op jit(solution)/shard_map/ppermute | solution.py:308
  7.5 5.2 %collective-permute-start.3 = (f32[4,16,640]{2,1,0:T(8,128)}, f32[4,16,640]{2,1,0:T(8,128)S(1)}, u32[]{:S(2)}, u32[]{:S(2)}) collective-permute-start(f32[4,16,640]{2,1,0:T(8,128)} %get-tuple-element.42), channel_id=1, source_target_pairs={{0,2},{1,3},{2,0},{3,1},{4,6},{5,7},{6,4},{7,5},{8,10},{9,11},{10,... | collective-permute-start | bytes 491528 | tf_op jit(solution)/shard_map/ppermute | solution.py:308
  12.7 0.4 collective-permute-start.4
  13.1 0.0 collective-permute-done.p1
  13.1 0.0 copy-done.1
  13.1 2.1 %collective-permute-start.2 = (f32[1,16,1024]{2,1,0:T(8,128)S(1)}, f32[1,16,1024]{2,1,0:T(8,128)S(1)}, u32[]{:S(2)}, u32[]{:S(2)}) collective-permute-start(f32[1,16,1024]{2,1,0:T(8,128)S(1)} %slice.7), channel_id=1, source_target_pairs={{1,0},{2,1},{3,2},{5,4},{6,5},{7,6},{9,8},{10,9},{11,10},{13,12},{... | collective-permute-start | bytes 196616 | tf_op jit(solution)/shard_map/ppermute | solution.py:334
  15.2 0.0 copy-start.3
  15.2 7.3 %collective-permute-start.1 = (f32[4,1,1024]{2,1,0:T(1,128)S(1)}, f32[4,1,1024]{2,1,0:T(1,128)S(1)}, u32[]{:S(2)}, u32[]{:S(2)}) collective-permute-start(f32[4,1,1024]{2,1,0:T(1,128)S(1)} %slice.6), channel_id=1, source_target_pairs={{4,0},{8,4},{12,8},{16,12},{20,16},{24,20},{28,24},{32,28},{36,32}... | collective-permute-start | bytes 49160 | tf_op jit(solution)/shard_map/ppermute | solution.py:333
  22.6 0.0 collective-permute-done.3.p2
  22.6 2.5 %collective-permute-done.4.p3 = f32[4,16,640]{2,1,0:T(8,128)S(1)} collective-permute-done((f32[4,16,640]{2,1,0:T(8,128)}, f32[4,16,640]{2,1,0:T(8,128)S(1)}, u32[]{:S(2)}, u32[]{:S(2)}) %collective-permute-start.4) | collective-permute-done | bytes 163872 | tf_op jit(solution)/shard_map/ppermute | solution.py:308
  25.1 3.4 %collective-permute-done.1.refs_9_ = f32[4,1,1024]{2,1,0:T(1,128)S(1)} collective-permute-done((f32[4,1,1024]{2,1,0:T(1,128)S(1)}, f32[4,1,1024]{2,1,0:T(1,128)S(1)}, u32[]{:S(2)}, u32[]{:S(2)}) %collective-permute-start.1) | collective-permute-done | bytes 16416 | tf_op jit(solution)/shard_map/ppermute | solution.py:333
  28.5 0.0 collective-permute-done.2.refs_10_
  28.5 0.0 copy-done
  28.5 0.0 copy-done.3
  28.5 0.6 shard_map.60
  29.1 1.8 %collective-permute-start.5 = (f32[16,8,640]{2,1,0:T(8,128)S(1)}, f32[16,8,640]{2,1,0:T(8,128)S(1)}, u32[]{:S(2)}, u32[]{:S(2)}) collective-permute-start(f32[16,8,640]{2,1,0:T(8,128)S(1)} %get-tuple-element.48), channel_id=1, source_target_pairs={{0,4},{1,5},{2,6},{3,7},{4,0},{5,1},{6,2},{7,3},{8,12},{9,13},{10,... | collective-permute-start | bytes 983048 | tf_op jit(solution)/shard_map/ppermute | solution.py:319
  30.9 7.5 %collective-permute-start.6 = (f32[16,8,640]{2,1,0:T(8,128)S(1)}, f32[16,8,640]{2,1,0:T(8,128)S(1)}, u32[]{:S(2)}, u32[]{:S(2)}) collective-permute-start(f32[16,8,640]{2,1,0:T(8,128)S(1)} %get-tuple-element.49), channel_id=1, source_target_pairs={{0,254},{1,255},{2,252},{3,253},{4,8},{5,9},{6,10},{7,11},{8,4},{9... | collective-permute-start | bytes 983048 | tf_op jit(solution)/shard_map/ppermute | solution.py:319
  38.4 0.0 collective-permute-done.5.near
  38.4 7.6 %collective-permute-done.6.far = f32[16,8,640]{2,1,0:T(8,128)S(1)} collective-permute-done((f32[16,8,640]{2,1,0:T(8,128)S(1)}, f32[16,8,640]{2,1,0:T(8,128)S(1)}, u32[]{:S(2)}, u32[]{:S(2)}) %collective-permute-start.6) | collective-permute-done | bytes 327712 | tf_op jit(solution)/shard_map/ppermute | solution.py:319
  46.0 5.1 %shard_map.61 = (f32[8,8,384]{2,1,0:T(8,128)S(1)}, f32[11,8,256]{2,1,0:T(8,128)S(1)}, f32[11,8,256]{2,1,0:T(8,128)S(1)}, f32[11,8,256]{2,1,0:T(8,128)S(1)}, f32[11,8,256]{2,1,0:T(8,128)S(1)}) custom-call(s32[6]{0:T(128)S(1)} %copy-done.3, f32[4,16,640]{2,1,0:T(8,128)S(1)} %copy-done, f32[4,16,640]{2,1,0:T(8,128)S(1)} %collective-permute-done.p1, ...), custom_call_target="tpu_custom_call" | custom-call | tf_op jit(solution)/shard_map/pallas_call | solution.py:282
  51.2 0.0 copy-start.2
  51.2 0.1 collective-permute-start.7
  51.3 6.7 %collective-permute-start.11 = (f32[8,8,384]{2,1,0:T(8,128)S(1)}, f32[8,8,384]{2,1,0:T(8,128)S(1)}, u32[]{:S(2)}, u32[]{:S(2)}) collective-permute-start(f32[8,8,384]{2,1,0:T(8,128)S(1)} %get-tuple-element.50.own), channel_id=1, source_target_pairs={{0,254},{1,255},{2,252},{3,253},{4,8},{5,9},{6,10},{7,11},{8,4},{9... | collective-permute-start | bytes 294920 | tf_op jit(solution)/shard_map/ppermute | solution.py:319
  57.9 0.0 collective-permute-done.7.near
  57.9 1.6 %collective-permute-start.8 = (f32[11,8,256]{2,1,0:T(8,128)S(1)}, f32[11,8,256]{2,1,0:T(8,128)S(1)}, u32[]{:S(2)}, u32[]{:S(2)}) collective-permute-start(f32[11,8,256]{2,1,0:T(8,128)S(1)} %get-tuple-element.56), channel_id=1, source_target_pairs={{0,1},{1,0},{2,3},{3,2},{4,5},{5,4},{6,7},{7,6},{8,9},{9,8},{10,11... | collective-permute-start | bytes 270344 | tf_op jit(solution)/shard_map/ppermute | solution.py:308
  59.5 1.6 %collective-permute-start.9 = (f32[11,8,256]{2,1,0:T(8,128)S(1)}, f32[11,8,256]{2,1,0:T(8,128)S(1)}, u32[]{:S(2)}, u32[]{:S(2)}) collective-permute-start(f32[11,8,256]{2,1,0:T(8,128)S(1)} %get-tuple-element.57), channel_id=1, source_target_pairs={{0,2},{1,3},{2,0},{3,1},{4,6},{5,7},{6,4},{7,5},{8,10},{9,11},{10,... | collective-permute-start | bytes 270344 | tf_op jit(solution)/shard_map/ppermute | solution.py:308
  61.2 3.9 %collective-permute-start.10 = (f32[11,8,256]{2,1,0:T(8,128)S(1)}, f32[11,8,256]{2,1,0:T(8,128)S(1)}, u32[]{:S(2)}, u32[]{:S(2)}) collective-permute-start(f32[11,8,256]{2,1,0:T(8,128)S(1)} %get-tuple-element.58), channel_id=1, source_target_pairs={{0,3},{1,2},{2,1},{3,0},{4,7},{5,6},{6,5},{7,4},{8,11},{9,10},{10,... | collective-permute-start | bytes 270344 | tf_op jit(solution)/shard_map/ppermute | solution.py:308
  65.1 2.3 %collective-permute-done.11.far = f32[8,8,384]{2,1,0:T(8,128)S(1)} collective-permute-done((f32[8,8,384]{2,1,0:T(8,128)S(1)}, f32[8,8,384]{2,1,0:T(8,128)S(1)}, u32[]{:S(2)}, u32[]{:S(2)}) %collective-permute-start.11) | collective-permute-done | bytes 98336 | tf_op jit(solution)/shard_map/ppermute | solution.py:319
  67.4 2.1 %shard_map.62 = (f32[2,8,256]{2,1,0:T(8,128)S(1)}, f32[2,8,256]{2,1,0:T(8,128)S(1)}, f32[2,8,256]{2,1,0:T(8,128)S(1)}, f32[2,8,256]{2,1,0:T(8,128)S(1)}) custom-call(s32[6]{0:T(128)S(1)} %copy-done.3, f32[8,8,384]{2,1,0:T(8,128)S(1)} %collective-permute-done.7.near, f32[8,8,384]{2,1,0:T(8,128)S(1)} %get-tuple-element.50.own, ...), custom_call_target="tpu_custom_call" | custom-call | tf_op jit(solution)/shard_map/pallas_call | solution.py:282
  69.5 0.0 collective-permute-done.8.refs_1_
  69.5 0.0 collective-permute-done.9.refs_2_
  69.5 1.5 %collective-permute-done.10.refs_3_ = f32[11,8,256]{2,1,0:T(8,128)S(1)} collective-permute-done((f32[11,8,256]{2,1,0:T(8,128)S(1)}, f32[11,8,256]{2,1,0:T(8,128)S(1)}, u32[]{:S(2)}, u32[]{:S(2)}) %collective-permute-start.10) | collective-permute-done | bytes 90144 | tf_op jit(solution)/shard_map/ppermute | solution.py:308
  71.0 0.4 collective-permute-start.12
  71.4 2.3 %collective-permute-start.13 = (f32[2,8,256]{2,1,0:T(8,128)S(1)}, f32[2,8,256]{2,1,0:T(8,128)S(1)}, u32[]{:S(2)}, u32[]{:S(2)}) collective-permute-start(f32[2,8,256]{2,1,0:T(8,128)S(1)} %get-tuple-element.70), channel_id=1, source_target_pairs={{0,2},{1,3},{2,0},{3,1},{4,6},{5,7},{6,4},{7,5},{8,10},{9,11},{10,... | collective-permute-start | bytes 49160 | tf_op jit(solution)/shard_map/ppermute | solution.py:308
  73.7 3.4 %collective-permute-start.14 = (f32[2,8,256]{2,1,0:T(8,128)S(1)}, f32[2,8,256]{2,1,0:T(8,128)S(1)}, u32[]{:S(2)}, u32[]{:S(2)}) collective-permute-start(f32[2,8,256]{2,1,0:T(8,128)S(1)} %get-tuple-element.71), channel_id=1, source_target_pairs={{0,3},{1,2},{2,1},{3,0},{4,7},{5,6},{6,5},{7,4},{8,11},{9,10},{10,... | collective-permute-start | bytes 49160 | tf_op jit(solution)/shard_map/ppermute | solution.py:308
  77.1 0.0 collective-permute-done.12.refs_5_
  77.1 0.9 %collective-permute-done.13.refs_6_ = f32[2,8,256]{2,1,0:T(8,128)S(1)} collective-permute-done((f32[2,8,256]{2,1,0:T(8,128)S(1)}, f32[2,8,256]{2,1,0:T(8,128)S(1)}, u32[]{:S(2)}, u32[]{:S(2)}) %collective-permute-start.13) | collective-permute-done | bytes 16416 | tf_op jit(solution)/shard_map/ppermute | solution.py:308
  78.0 2.8 %collective-permute-done.14.refs_7_ = f32[2,8,256]{2,1,0:T(8,128)S(1)} collective-permute-done((f32[2,8,256]{2,1,0:T(8,128)S(1)}, f32[2,8,256]{2,1,0:T(8,128)S(1)}, u32[]{:S(2)}, u32[]{:S(2)}) %collective-permute-start.14) | collective-permute-done | bytes 16416 | tf_op jit(solution)/shard_map/ppermute | solution.py:308
  80.8 0.0 copy-done.2
  80.8 1.9 %shard_map.63 = (f32[4,16,1024]{2,1,0:T(8,128)}, f32[4,16,1024]{2,1,0:T(8,128)}) custom-call(s32[6]{0:T(128)S(1)} %copy-done.3, f32[11,8,256]{2,1,0:T(8,128)S(1)} %get-tuple-element.64.refs_0_, f32[11,8,256]{2,1,0:T(8,128)S(1)} %collective-permute-done.8.refs_1_, f32[11,8,256]{2,1,0:T(8,128)S(1)} %collective-permute-done.9.refs_2_, ...), custom_call_target="tpu_custom_call" | custom-call | tf_op jit(solution)/shard_map/pallas_call | solution.py:282
  (2 shorter events, 0.0 us)
Async XLA Ops:
  1.3 11.9 %copy-start.1 = (f32[4,16,1024]{2,1,0:T(8,128)S(1)}, f32[4,16,1024]{2,1,0:T(8,128)}, u32[]{:S(2)}) copy-start(f32[4,16,1024]{2,1,0:T(8,128)} %refs_8_.1) | copy-start | bytes 786436
  4.1 24.4 %copy-start = (f32[4,16,640]{2,1,0:T(8,128)S(1)}, f32[4,16,640]{2,1,0:T(8,128)}, u32[]{:S(2)}) copy-start(f32[4,16,640]{2,1,0:T(8,128)} %get-tuple-element.44.p0) | copy-start | bytes 491524
  4.2 9.0 %collective-permute-start = (f32[4,16,640]{2,1,0:T(8,128)}, f32[4,16,640]{2,1,0:T(8,128)S(1)}, u32[]{:S(2)}, u32[]{:S(2)}) collective-permute-start(f32[4,16,640]{2,1,0:T(8,128)} %get-tuple-element.38), channel_id=1, source_target_pairs={{0,1},{1,0},{2,3},{3,2},{4,5},{5,4},{6,7},{7,6},{8,9},{9,8},{10,11... | collective-permute-start | bytes 491528 | tf_op jit(solution)/shard_map/ppermute | solution.py:308
  7.5 15.1 %collective-permute-start.3 = (f32[4,16,640]{2,1,0:T(8,128)}, f32[4,16,640]{2,1,0:T(8,128)S(1)}, u32[]{:S(2)}, u32[]{:S(2)}) collective-permute-start(f32[4,16,640]{2,1,0:T(8,128)} %get-tuple-element.42), channel_id=1, source_target_pairs={{0,2},{1,3},{2,0},{3,1},{4,6},{5,7},{6,4},{7,5},{8,10},{9,11},{10,... | collective-permute-start | bytes 491528 | tf_op jit(solution)/shard_map/ppermute | solution.py:308
  12.7 12.4 %collective-permute-start.4 = (f32[4,16,640]{2,1,0:T(8,128)}, f32[4,16,640]{2,1,0:T(8,128)S(1)}, u32[]{:S(2)}, u32[]{:S(2)}) collective-permute-start(f32[4,16,640]{2,1,0:T(8,128)} %get-tuple-element.43), channel_id=1, source_target_pairs={{0,3},{1,2},{2,1},{3,0},{4,7},{5,6},{6,5},{7,4},{8,11},{9,10},{10,... | collective-permute-start | bytes 491528 | tf_op jit(solution)/shard_map/ppermute | solution.py:308
  13.1 15.4 %collective-permute-start.2 = (f32[1,16,1024]{2,1,0:T(8,128)S(1)}, f32[1,16,1024]{2,1,0:T(8,128)S(1)}, u32[]{:S(2)}, u32[]{:S(2)}) collective-permute-start(f32[1,16,1024]{2,1,0:T(8,128)S(1)} %slice.7), channel_id=1, source_target_pairs={{1,0},{2,1},{3,2},{5,4},{6,5},{7,6},{9,8},{10,9},{11,10},{13,12},{... | collective-permute-start | bytes 196616 | tf_op jit(solution)/shard_map/ppermute | solution.py:334
  15.2 13.3 %copy-start.3 = (s32[6]{0:T(128)S(1)}, s32[6]{0:T(128)}, u32[]{:S(2)}) copy-start(s32[6]{0:T(128)} %stack.27.ids) | copy-start | bytes 76
  15.2 13.3 %collective-permute-start.1 = (f32[4,1,1024]{2,1,0:T(1,128)S(1)}, f32[4,1,1024]{2,1,0:T(1,128)S(1)}, u32[]{:S(2)}, u32[]{:S(2)}) collective-permute-start(f32[4,1,1024]{2,1,0:T(1,128)S(1)} %slice.6), channel_id=1, source_target_pairs={{4,0},{8,4},{12,8},{16,12},{20,16},{24,20},{28,24},{32,28},{36,32}... | collective-permute-start | bytes 49160 | tf_op jit(solution)/shard_map/ppermute | solution.py:333
  29.1 9.3 %collective-permute-start.5 = (f32[16,8,640]{2,1,0:T(8,128)S(1)}, f32[16,8,640]{2,1,0:T(8,128)S(1)}, u32[]{:S(2)}, u32[]{:S(2)}) collective-permute-start(f32[16,8,640]{2,1,0:T(8,128)S(1)} %get-tuple-element.48), channel_id=1, source_target_pairs={{0,4},{1,5},{2,6},{3,7},{4,0},{5,1},{6,2},{7,3},{8,12},{9,13},{10,... | collective-permute-start | bytes 983048 | tf_op jit(solution)/shard_map/ppermute | solution.py:319
  30.9 15.1 %collective-permute-start.6 = (f32[16,8,640]{2,1,0:T(8,128)S(1)}, f32[16,8,640]{2,1,0:T(8,128)S(1)}, u32[]{:S(2)}, u32[]{:S(2)}) collective-permute-start(f32[16,8,640]{2,1,0:T(8,128)S(1)} %get-tuple-element.49), channel_id=1, source_target_pairs={{0,254},{1,255},{2,252},{3,253},{4,8},{5,9},{6,10},{7,11},{8,4},{9... | collective-permute-start | bytes 983048 | tf_op jit(solution)/shard_map/ppermute | solution.py:319
  51.2 29.7 %copy-start.2 = (f32[4,16,1024]{2,1,0:T(8,128)S(1)}, f32[4,16,1024]{2,1,0:T(8,128)}, u32[]{:S(2)}) copy-start(f32[4,16,1024]{2,1,0:T(8,128)} %refs_11_.1) | copy-start | bytes 786436
  51.2 6.8 %collective-permute-start.7 = (f32[8,8,384]{2,1,0:T(8,128)S(1)}, f32[8,8,384]{2,1,0:T(8,128)S(1)}, u32[]{:S(2)}, u32[]{:S(2)}) collective-permute-start(f32[8,8,384]{2,1,0:T(8,128)S(1)} %get-tuple-element.50.own), channel_id=1, source_target_pairs={{0,4},{1,5},{2,6},{3,7},{4,0},{5,1},{6,2},{7,3},{8,12},{9,13},{10,... | collective-permute-start | bytes 294920 | tf_op jit(solution)/shard_map/ppermute | solution.py:319
  51.3 16.1 %collective-permute-start.11 = (f32[8,8,384]{2,1,0:T(8,128)S(1)}, f32[8,8,384]{2,1,0:T(8,128)S(1)}, u32[]{:S(2)}, u32[]{:S(2)}) collective-permute-start(f32[8,8,384]{2,1,0:T(8,128)S(1)} %get-tuple-element.50.own), channel_id=1, source_target_pairs={{0,254},{1,255},{2,252},{3,253},{4,8},{5,9},{6,10},{7,11},{8,4},{9... | collective-permute-start | bytes 294920 | tf_op jit(solution)/shard_map/ppermute | solution.py:319
  57.9 11.6 %collective-permute-start.8 = (f32[11,8,256]{2,1,0:T(8,128)S(1)}, f32[11,8,256]{2,1,0:T(8,128)S(1)}, u32[]{:S(2)}, u32[]{:S(2)}) collective-permute-start(f32[11,8,256]{2,1,0:T(8,128)S(1)} %get-tuple-element.56), channel_id=1, source_target_pairs={{0,1},{1,0},{2,3},{3,2},{4,5},{5,4},{6,7},{7,6},{8,9},{9,8},{10,11... | collective-permute-start | bytes 270344 | tf_op jit(solution)/shard_map/ppermute | solution.py:308
  59.5 10.0 %collective-permute-start.9 = (f32[11,8,256]{2,1,0:T(8,128)S(1)}, f32[11,8,256]{2,1,0:T(8,128)S(1)}, u32[]{:S(2)}, u32[]{:S(2)}) collective-permute-start(f32[11,8,256]{2,1,0:T(8,128)S(1)} %get-tuple-element.57), channel_id=1, source_target_pairs={{0,2},{1,3},{2,0},{3,1},{4,6},{5,7},{6,4},{7,5},{8,10},{9,11},{10,... | collective-permute-start | bytes 270344 | tf_op jit(solution)/shard_map/ppermute | solution.py:308
  61.2 9.8 %collective-permute-start.10 = (f32[11,8,256]{2,1,0:T(8,128)S(1)}, f32[11,8,256]{2,1,0:T(8,128)S(1)}, u32[]{:S(2)}, u32[]{:S(2)}) collective-permute-start(f32[11,8,256]{2,1,0:T(8,128)S(1)} %get-tuple-element.58), channel_id=1, source_target_pairs={{0,3},{1,2},{2,1},{3,0},{4,7},{5,6},{6,5},{7,4},{8,11},{9,10},{10,... | collective-permute-start | bytes 270344 | tf_op jit(solution)/shard_map/ppermute | solution.py:308
  71.0 6.1 %collective-permute-start.12 = (f32[2,8,256]{2,1,0:T(8,128)S(1)}, f32[2,8,256]{2,1,0:T(8,128)S(1)}, u32[]{:S(2)}, u32[]{:S(2)}) collective-permute-start(f32[2,8,256]{2,1,0:T(8,128)S(1)} %get-tuple-element.69), channel_id=1, source_target_pairs={{0,1},{1,0},{2,3},{3,2},{4,5},{5,4},{6,7},{7,6},{8,9},{9,8},{10,11... | collective-permute-start | bytes 49160 | tf_op jit(solution)/shard_map/ppermute | solution.py:308
  71.4 6.6 %collective-permute-start.13 = (f32[2,8,256]{2,1,0:T(8,128)S(1)}, f32[2,8,256]{2,1,0:T(8,128)S(1)}, u32[]{:S(2)}, u32[]{:S(2)}) collective-permute-start(f32[2,8,256]{2,1,0:T(8,128)S(1)} %get-tuple-element.70), channel_id=1, source_target_pairs={{0,2},{1,3},{2,0},{3,1},{4,6},{5,7},{6,4},{7,5},{8,10},{9,11},{10,... | collective-permute-start | bytes 49160 | tf_op jit(solution)/shard_map/ppermute | solution.py:308
  73.7 7.1 %collective-permute-start.14 = (f32[2,8,256]{2,1,0:T(8,128)S(1)}, f32[2,8,256]{2,1,0:T(8,128)S(1)}, u32[]{:S(2)}, u32[]{:S(2)}) collective-permute-start(f32[2,8,256]{2,1,0:T(8,128)S(1)} %get-tuple-element.71), channel_id=1, source_target_pairs={{0,3},{1,2},{2,1},{3,0},{4,7},{5,6},{6,5},{7,4},{8,11},{9,10},{10,... | collective-permute-start | bytes 49160 | tf_op jit(solution)/shard_map/ppermute | solution.py:308

commit v3 on v1

--- a/solution.py
+++ b/solution.py
@@ -166,7 +166,7 @@
     lax.fori_loop(0, NR // 2, residual, 0, unroll=True)
 
 
-def coarse_kernel(ids, lo, own, hi, smooth, o0, o1, o2, o3, rhs, diag, xa, xb, step, adj):
+def coarse_kernel(ids, near, own, far, smooth, o0, o1, o2, o3, rhs, diag, xa, xb, step, adj):
     first, pairs = coefficients(*COARSE, S_C)
     half = NR // 2
     rows = 3 * HALO
@@ -178,9 +178,9 @@
     even = lax.rem(lanes((HALO, WIDE)), 2) == 0
 
     def begin(q, _):
-        for part, src in enumerate((lo, own, hi)):
+        for part, src in (((1 - ids[5]) * 2, near), (1, own), (ids[5] * 2, far)):
             v = src[q]
-            at = pl.ds(part * HALO, HALO)
+            at = pl.ds(pl.multiple_of(part * HALO, HALO), HALO)
             rhs[q, at] = jnp.where(even, v, pltpu.roll(v, 1, 1))
             diag[q, at] = jnp.where(even, pltpu.roll(v, WIDE - 1, 1), v) + 1.5
         d = rhs[q] * first
@@ -194,8 +194,8 @@
 
         def sweep(q, _, old=old, new=new, damp=damp, gain=gain):
             v = old[q + 1]
-            near = old[q] + old[q + 2] + lateral(v, 1, 2)
-            resid = rhs[q] - diag[q] * v + 0.25 * near
+            around = old[q] + old[q + 2] + lateral(v, 1, 2)
+            resid = rhs[q] - diag[q] * v + 0.25 * around
             d = damp * step[q] + gain * resid
             step[q] = d
             new[q + 1] = v + d
@@ -274,7 +274,8 @@
         return ((i // 4) % 2) * 2
 
     turn = flip(lat)
-    ids = jnp.stack([rad ^ turn, rad ^ 1 ^ turn, rad ^ 2 ^ turn, rad ^ 3 ^ turn, rad]).astype(jnp.int32)
+    ids = [rad ^ turn, rad ^ 1 ^ turn, rad ^ 2 ^ turn, rad ^ 3 ^ turn, rad, lat % 2]
+    ids = jnp.stack(ids).astype(jnp.int32)
 
     def trade(pieces):
         out = [pieces[0]]
@@ -289,6 +290,17 @@
             for k in range(rad_n):
                 pairs.append((i * rad_n + k, to * rad_n + (k ^ flip(i) ^ flip(to))))
         return lax.ppermute(v, ("lat", "rad"), pairs)
+
+    def swaps(near, far):
+        out = []
+        for shift, v in ((1, far), (0, near)):
+            pairs = []
+            for i in range(lat_n):
+                to = (((i + shift) ^ 1) - shift) % lat_n
+                for k in range(rad_n):
+                    pairs.append((i * rad_n + k, to * rad_n + (k ^ flip(i) ^ flip(to))))
+            out.append(lax.ppermute(v, ("lat", "rad"), pairs))
+        return out[1], out[0]
 
     slab = pltpu.VMEM((LAYERS, ROWS, 1024), F32)
     pieces = pl.pallas_call(
@@ -318,8 +330,7 @@
         lo,
         hi,
     )
-    below = beside(packed, 1)
-    over = beside(packed, -1)
+    near, far = swaps(packed, packed)
     deep = (NR // 2, 3 * HALO, WIDE)
     padded = (NR // 2 + 2, 3 * HALO, WIDE)
     backs = call(
@@ -327,9 +338,9 @@
         [struct(2 * LAYERS + 3, 8, MAIN)] * 4,
         [deep, deep, padded, padded, deep, (NR + 1, 3 * HALO, MAIN)],
         ids,
-        below,
+        near,
         packed,
-        over,
+        far,
         smooth,
     )
     backs = trade(backs)

time: 83 us -> 75.9 us (0.914)
  waiting for transfers between devices: 25.8 us -> 20.9 us
  starting transfers between devices: 43.5 us -> 41.2 us
    ppermute x4 -> x2, waiting for transfers between devices: 15.5 us -> 6.57 us  [beside(): return lax.ppermute(v, ('lat', 'rad'), pairs)]
    ppermute x0 -> x2, starting transfers between devices: none -> 6.69 us  [swaps(): out.append(lax.ppermute(v, ('lat', 'rad'), pairs))]
    ppermute x4 -> x2, starting transfers between devices: 13.7 us -> 6.97 us  [beside(): return lax.ppermute(v, ('lat', 'rad'), pairs)]
    ppermute x0 -> x2, waiting for transfers between devices: none -> 3.76 us  [swaps(): out.append(lax.ppermute(v, ('lat', 'rad'), pairs))]
    ppermute x6, starting transfers between devices: 20.4 us -> 18.2 us  [trade(): lax.ppermute(pieces[m], 'rad', [(k, k ^ m) for k in range(rad_n)])]
where the time goes in v3:
time: 75.9 us; the launch traced here: 75.7 us
  starting transfers between devices  41.2 us (54%)
  waiting for transfers between devices  20.9 us (28%)
  Pallas kernels  10.8 us (14%)
  local copies, waits for them, and re-layouts  2.01 us (3%)
    ppermute x6, starting transfers between devices, trade(): lax.ppermute(pieces[m], 'rad', [(k, k ^ m) for k in range(rad_n)])  18.2 us
    pallas_call x4, Pallas kernels, call(): pl.pallas_call(kernel, out_shape=outs, in_specs=[pl.BlockSpec(memory_spac...  9.35 us
    ppermute x1, starting transfers between devices, body(): lax.ppermute(ahead[:, :1], 'lat', [((i + 1) % lat_n, i) for i in range(la...  7.33 us
    ppermute x6, waiting for transfers between devices, trade(): lax.ppermute(pieces[m], 'rad', [(k, k ^ m) for k in range(rad_n)])  7.14 us
    ppermute x2, starting transfers between devices, beside(): return lax.ppermute(v, ('lat', 'rad'), pairs)  6.97 us
    ppermute x2, starting transfers between devices, swaps(): out.append(lax.ppermute(v, ('lat', 'rad'), pairs))  6.69 us
    ppermute x2, waiting for transfers between devices, beside(): return lax.ppermute(v, ('lat', 'rad'), pairs)  6.57 us
    ppermute x2, waiting for transfers between devices, swaps(): out.append(lax.ppermute(v, ('lat', 'rad'), pairs))  3.76 us
  transfers between devices with their start and end apart: 12, of which 7 were waited for; matrix products, arithmetic and copies ran while one was open for 0% of the time, Pallas kernels for 0%

profile of v3, /device:TPU:1, one launch (start us, length us, event | category | flops | bytes accessed | tf_op | source)
XLA Modules:
  0.0 75.7 jit_solution(5542481890538699920)
XLA Ops:
  0.7 0.1 stack.27.ids
  0.8 0.0 copy-start.2
  0.8 1.0 %copy-done.2 = f32[4,16,1024]{2,1,0:T(8,128)S(1)} copy-done((f32[4,16,1024]{2,1,0:T(8,128)S(1)}, f32[4,16,1024]{2,1,0:T(8,128)}, u32[]{:S(2)}) %copy-start.2) | copy-done | bytes 262168
  1.7 0.0 copy-start.3
  1.7 0.9 %copy-done.3 = f32[4,16,1024]{2,1,0:T(8,128)S(1)} copy-done((f32[4,16,1024]{2,1,0:T(8,128)S(1)}, f32[4,16,1024]{2,1,0:T(8,128)}, u32[]{:S(2)}) %copy-start.3) | copy-done | bytes 262168
  2.7 0.0 copy-start
  2.7 1.4 %shard_map.59 = (f32[4,16,640]{2,1,0:T(8,128)S(1)}, f32[4,16,640]{2,1,0:T(8,128)S(1)}, f32[4,16,640]{2,1,0:T(8,128)S(1)}, f32[4,16,640]{2,1,0:T(8,128)S(1)}) custom-call(s32[6]{0:T(128)S(1)} %stack.27.ids, f32[4,16,1024]{2,1,0:T(8,128)S(1)} %copy-done.2, f32[4,16,1024]{2,1,0:T(8,128)S(1)} %copy-done.3), custom_call_target="tpu_custom_call" | custom-call | tf_op jit(solution)/shard_map/pallas_call | solution.py:306
  4.1 3.3 %collective-permute-start = (f32[4,16,640]{2,1,0:T(8,128)S(1)}, f32[4,16,640]{2,1,0:T(8,128)S(1)}, u32[]{:S(2)}, u32[]{:S(2)}) collective-permute-start(f32[4,16,640]{2,1,0:T(8,128)S(1)} %get-tuple-element.22), channel_id=1, source_target_pairs={{0,1},{1,0},{2,3},{3,2},{4,5},{5,4},{6,7},{7,6},{8,9},{9,8},{10,11... | collective-permute-start | bytes 491528 | tf_op jit(solution)/shard_map/ppermute | solution.py:283
  7.4 5.2 %collective-permute-start.3 = (f32[4,16,640]{2,1,0:T(8,128)S(1)}, f32[4,16,640]{2,1,0:T(8,128)S(1)}, u32[]{:S(2)}, u32[]{:S(2)}) collective-permute-start(f32[4,16,640]{2,1,0:T(8,128)S(1)} %get-tuple-element.26), channel_id=1, source_target_pairs={{0,2},{1,3},{2,0},{3,1},{4,6},{5,7},{6,4},{7,5},{8,10},{9,11},{10,... | collective-permute-start | bytes 491528 | tf_op jit(solution)/shard_map/ppermute | solution.py:283
  12.6 0.4 collective-permute-start.4
  13.1 0.0 collective-permute-done.p1
  13.1 0.0 copy-done
  13.1 2.1 %collective-permute-start.2 = (f32[1,16,1024]{2,1,0:T(8,128)S(1)}, f32[1,16,1024]{2,1,0:T(8,128)S(1)}, u32[]{:S(2)}, u32[]{:S(2)}) collective-permute-start(f32[1,16,1024]{2,1,0:T(8,128)S(1)} %slice.7), channel_id=1, source_target_pairs={{1,0},{2,1},{3,2},{5,4},{6,5},{7,6},{9,8},{10,9},{11,10},{13,12},{... | collective-permute-start | bytes 196616 | tf_op jit(solution)/shard_map/ppermute | solution.py:317
  15.2 7.3 %collective-permute-start.1 = (f32[4,1,1024]{2,1,0:T(1,128)S(1)}, f32[4,1,1024]{2,1,0:T(1,128)S(1)}, u32[]{:S(2)}, u32[]{:S(2)}) collective-permute-start(f32[4,1,1024]{2,1,0:T(1,128)S(1)} %slice.6), channel_id=1, source_target_pairs={{4,0},{8,4},{12,8},{16,12},{20,16},{24,20},{28,24},{32,28},{36,32}... | collective-permute-start | bytes 49160 | tf_op jit(solution)/shard_map/ppermute | solution.py:316
  22.5 0.0 collective-permute-done.3.p2
  22.5 2.3 %collective-permute-done.4.p3 = f32[4,16,640]{2,1,0:T(8,128)S(1)} collective-permute-done((f32[4,16,640]{2,1,0:T(8,128)S(1)}, f32[4,16,640]{2,1,0:T(8,128)S(1)}, u32[]{:S(2)}, u32[]{:S(2)}) %collective-permute-start.4) | collective-permute-done | bytes 163872 | tf_op jit(solution)/shard_map/ppermute | solution.py:283
  24.8 3.4 %collective-permute-done.1.forward_x = f32[4,1,1024]{2,1,0:T(1,128)S(1)} collective-permute-done((f32[4,1,1024]{2,1,0:T(1,128)S(1)}, f32[4,1,1024]{2,1,0:T(1,128)S(1)}, u32[]{:S(2)}, u32[]{:S(2)}) %collective-permute-start.1) | collective-permute-done | bytes 16416 | tf_op jit(solution)/shard_map/ppermute | solution.py:316
  28.2 0.0 collective-permute-done.2.forward_r
  28.2 0.6 shard_map.60
  28.8 1.8 %collective-permute-start.5 = (f32[16,8,640]{2,1,0:T(8,128)S(1)}, f32[16,8,640]{2,1,0:T(8,128)S(1)}, u32[]{:S(2)}, u32[]{:S(2)}) collective-permute-start(f32[16,8,640]{2,1,0:T(8,128)S(1)} %get-tuple-element.32), channel_id=1, source_target_pairs={{0,4},{1,5},{2,6},{3,7},{4,8},{5,9},{6,10},{7,11},{8,12},{9,13},{1... | collective-permute-start | bytes 983048 | tf_op jit(solution)/shard_map/ppermute | solution.py:292
  30.6 5.2 %collective-permute-start.6 = (f32[16,8,640]{2,1,0:T(8,128)S(1)}, f32[16,8,640]{2,1,0:T(8,128)S(1)}, u32[]{:S(2)}, u32[]{:S(2)}) collective-permute-start(f32[16,8,640]{2,1,0:T(8,128)S(1)} %get-tuple-element.33), channel_id=1, source_target_pairs={{0,254},{1,255},{2,252},{3,253},{4,0},{5,1},{6,2},{7,3},{8,4},{9,5... | collective-permute-start | bytes 983048 | tf_op jit(solution)/shard_map/ppermute | solution.py:292
  35.8 6.6 %collective-permute-done.5.lo = f32[16,8,640]{2,1,0:T(8,128)S(1)} collective-permute-done((f32[16,8,640]{2,1,0:T(8,128)S(1)}, f32[16,8,640]{2,1,0:T(8,128)S(1)}, u32[]{:S(2)}, u32[]{:S(2)}) %collective-permute-start.5) | collective-permute-done | bytes 327712 | tf_op jit(solution)/shard_map/ppermute | solution.py:292
  42.4 0.0 collective-permute-done.6.hi
  42.4 4.9 %shard_map.61 = (f32[16,24,256]{2,1,0:T(8,128)S(1)}, f32[8,8,384]{2,1,0:T(8,128)S(1)}) custom-call(s32[6]{0:T(128)S(1)} %stack.27.ids, f32[4,16,640]{2,1,0:T(8,128)S(1)} %get-tuple-element.28.p0, f32[4,16,640]{2,1,0:T(8,128)S(1)} %collective-permute-done.p1, f32[4,16,640]{2,1,0:T(8,128)S(1)} %collective-permute-done.3.p2, ...), custom_call_target="tpu_custom_call" | custom-call | tf_op jit(solution)/shard_map/pallas_call | solution.py:257
  47.3 6.7 %collective-permute-start.8 = (f32[8,8,384]{2,1,0:T(8,128)S(1)}, f32[8,8,384]{2,1,0:T(8,128)S(1)}, u32[]{:S(2)}, u32[]{:S(2)}) collective-permute-start(f32[8,8,384]{2,1,0:T(8,128)S(1)} %get-tuple-element.34.own), channel_id=1, source_target_pairs={{0,254},{1,255},{2,252},{3,253},{4,8},{5,9},{6,10},{7,11},{8,4},{9... | collective-permute-start | bytes 294920 | tf_op jit(solution)/shard_map/ppermute | solution.py:302
  54.0 0.0 collective-permute-start.7
  54.0 2.3 %collective-permute-done.8.far = f32[8,8,384]{2,1,0:T(8,128)S(1)} collective-permute-done((f32[8,8,384]{2,1,0:T(8,128)S(1)}, f32[8,8,384]{2,1,0:T(8,128)S(1)}, u32[]{:S(2)}, u32[]{:S(2)}) %collective-permute-start.8) | collective-permute-done | bytes 98336 | tf_op jit(solution)/shard_map/ppermute | solution.py:302
  56.3 1.5 %collective-permute-done.7.near = f32[8,8,384]{2,1,0:T(8,128)S(1)} collective-permute-done((f32[8,8,384]{2,1,0:T(8,128)S(1)}, f32[8,8,384]{2,1,0:T(8,128)S(1)}, u32[]{:S(2)}, u32[]{:S(2)}) %collective-permute-start.7) | collective-permute-done | bytes 98336 | tf_op jit(solution)/shard_map/ppermute | solution.py:302
  57.7 0.0 copy-start.1
  57.7 2.3 %shard_map.62 = (f32[11,8,256]{2,1,0:T(8,128)S(1)}, f32[11,8,256]{2,1,0:T(8,128)S(1)}, f32[11,8,256]{2,1,0:T(8,128)S(1)}, f32[11,8,256]{2,1,0:T(8,128)S(1)}) custom-call(s32[6]{0:T(128)S(1)} %stack.27.ids, f32[8,8,384]{2,1,0:T(8,128)S(1)} %collective-permute-done.7.near, f32[8,8,384]{2,1,0:T(8,128)S(1)} %get-tuple-element.34.own, ...), custom_call_target="tpu_custom_call" | custom-call | tf_op jit(solution)/shard_map/pallas_call | solution.py:257
  60.1 3.6 %collective-permute-start.9 = (f32[11,8,256]{2,1,0:T(8,128)S(1)}, f32[11,8,256]{2,1,0:T(8,128)S(1)}, u32[]{:S(2)}, u32[]{:S(2)}) collective-permute-start(f32[11,8,256]{2,1,0:T(8,128)S(1)} %get-tuple-element.37), channel_id=1, source_target_pairs={{0,1},{1,0},{2,3},{3,2},{4,5},{5,4},{6,7},{7,6},{8,9},{9,8},{10,11... | collective-permute-start | bytes 270344 | tf_op jit(solution)/shard_map/ppermute | solution.py:283
  63.6 2.0 %collective-permute-start.10 = (f32[11,8,256]{2,1,0:T(8,128)S(1)}, f32[11,8,256]{2,1,0:T(8,128)S(1)}, u32[]{:S(2)}, u32[]{:S(2)}) collective-permute-start(f32[11,8,256]{2,1,0:T(8,128)S(1)} %get-tuple-element.38), channel_id=1, source_target_pairs={{0,2},{1,3},{2,0},{3,1},{4,6},{5,7},{6,4},{7,5},{8,10},{9,11},{10,... | collective-permute-start | bytes 270344 | tf_op jit(solution)/shard_map/ppermute | solution.py:283
  65.6 3.7 %collective-permute-start.11 = (f32[11,8,256]{2,1,0:T(8,128)S(1)}, f32[11,8,256]{2,1,0:T(8,128)S(1)}, u32[]{:S(2)}, u32[]{:S(2)}) collective-permute-start(f32[11,8,256]{2,1,0:T(8,128)S(1)} %get-tuple-element.39), channel_id=1, source_target_pairs={{0,3},{1,2},{2,1},{3,0},{4,7},{5,6},{6,5},{7,4},{8,11},{9,10},{10,... | collective-permute-start | bytes 270344 | tf_op jit(solution)/shard_map/ppermute | solution.py:283
  69.3 0.0 collective-permute-done.9.p1
  69.3 2.4 %collective-permute-done.10.p2 = f32[11,8,256]{2,1,0:T(8,128)S(1)} collective-permute-done((f32[11,8,256]{2,1,0:T(8,128)S(1)}, f32[11,8,256]{2,1,0:T(8,128)S(1)}, u32[]{:S(2)}, u32[]{:S(2)}) %collective-permute-start.10) | collective-permute-done | bytes 90144 | tf_op jit(solution)/shard_map/ppermute | solution.py:283
  71.7 2.4 %collective-permute-done.11.p3 = f32[11,8,256]{2,1,0:T(8,128)S(1)} collective-permute-done((f32[11,8,256]{2,1,0:T(8,128)S(1)}, f32[11,8,256]{2,1,0:T(8,128)S(1)}, u32[]{:S(2)}, u32[]{:S(2)}) %collective-permute-start.11) | collective-permute-done | bytes 90144 | tf_op jit(solution)/shard_map/ppermute | solution.py:283
  74.1 0.0 copy-done.1
  74.1 1.6 %shard_map.63 = (f32[4,16,1024]{2,1,0:T(8,128)}, f32[4,16,1024]{2,1,0:T(8,128)}) custom-call(s32[6]{0:T(128)S(1)} %stack.27.ids, f32[11,8,256]{2,1,0:T(8,128)S(1)} %get-tuple-element.36.p0, f32[11,8,256]{2,1,0:T(8,128)S(1)} %collective-permute-done.9.p1, f32[11,8,256]{2,1,0:T(8,128)S(1)} %collective-permute-done.10.p2, ...), custom_call_target="tpu_custom_call" | custom-call | tf_op jit(solution)/shard_map/pallas_call | solution.py:257
  (2 shorter events, 0.0 us)
Async XLA Ops:
  0.8 1.0 %copy-start.2 = (f32[4,16,1024]{2,1,0:T(8,128)S(1)}, f32[4,16,1024]{2,1,0:T(8,128)}, u32[]{:S(2)}) copy-start(f32[4,16,1024]{2,1,0:T(8,128)} %source_hbm.1) | copy-start | bytes 786436
  1.7 0.9 %copy-start.3 = (f32[4,16,1024]{2,1,0:T(8,128)S(1)}, f32[4,16,1024]{2,1,0:T(8,128)}, u32[]{:S(2)}) copy-start(f32[4,16,1024]{2,1,0:T(8,128)} %kappa_hbm.1) | copy-start | bytes 786436
  2.7 10.4 %copy-start = (f32[4,16,1024]{2,1,0:T(8,128)S(1)}, f32[4,16,1024]{2,1,0:T(8,128)}, u32[]{:S(2)}) copy-start(f32[4,16,1024]{2,1,0:T(8,128)} %forward.1) | copy-start | bytes 786436
  4.1 9.0 %collective-permute-start = (f32[4,16,640]{2,1,0:T(8,128)S(1)}, f32[4,16,640]{2,1,0:T(8,128)S(1)}, u32[]{:S(2)}, u32[]{:S(2)}) collective-permute-start(f32[4,16,640]{2,1,0:T(8,128)S(1)} %get-tuple-element.22), channel_id=1, source_target_pairs={{0,1},{1,0},{2,3},{3,2},{4,5},{5,4},{6,7},{7,6},{8,9},{9,8},{10,11... | collective-permute-start | bytes 491528 | tf_op jit(solution)/shard_map/ppermute | solution.py:283
  7.4 15.1 %collective-permute-start.3 = (f32[4,16,640]{2,1,0:T(8,128)S(1)}, f32[4,16,640]{2,1,0:T(8,128)S(1)}, u32[]{:S(2)}, u32[]{:S(2)}) collective-permute-start(f32[4,16,640]{2,1,0:T(8,128)S(1)} %get-tuple-element.26), channel_id=1, source_target_pairs={{0,2},{1,3},{2,0},{3,1},{4,6},{5,7},{6,4},{7,5},{8,10},{9,11},{10,... | collective-permute-start | bytes 491528 | tf_op jit(solution)/shard_map/ppermute | solution.py:283
  12.6 12.2 %collective-permute-start.4 = (f32[4,16,640]{2,1,0:T(8,128)S(1)}, f32[4,16,640]{2,1,0:T(8,128)S(1)}, u32[]{:S(2)}, u32[]{:S(2)}) collective-permute-start(f32[4,16,640]{2,1,0:T(8,128)S(1)} %get-tuple-element.27), channel_id=1, source_target_pairs={{0,3},{1,2},{2,1},{3,0},{4,7},{5,6},{6,5},{7,4},{8,11},{9,10},{10,... | collective-permute-start | bytes 491528 | tf_op jit(solution)/shard_map/ppermute | solution.py:283
  13.1 15.1 %collective-permute-start.2 = (f32[1,16,1024]{2,1,0:T(8,128)S(1)}, f32[1,16,1024]{2,1,0:T(8,128)S(1)}, u32[]{:S(2)}, u32[]{:S(2)}) collective-permute-start(f32[1,16,1024]{2,1,0:T(8,128)S(1)} %slice.7), channel_id=1, source_target_pairs={{1,0},{2,1},{3,2},{5,4},{6,5},{7,6},{9,8},{10,9},{11,10},{13,12},{... | collective-permute-start | bytes 196616 | tf_op jit(solution)/shard_map/ppermute | solution.py:317
  15.2 13.1 %collective-permute-start.1 = (f32[4,1,1024]{2,1,0:T(1,128)S(1)}, f32[4,1,1024]{2,1,0:T(1,128)S(1)}, u32[]{:S(2)}, u32[]{:S(2)}) collective-permute-start(f32[4,1,1024]{2,1,0:T(1,128)S(1)} %slice.6), channel_id=1, source_target_pairs={{4,0},{8,4},{12,8},{16,12},{20,16},{24,20},{28,24},{32,28},{36,32}... | collective-permute-start | bytes 49160 | tf_op jit(solution)/shard_map/ppermute | solution.py:316
  28.8 13.5 %collective-permute-start.5 = (f32[16,8,640]{2,1,0:T(8,128)S(1)}, f32[16,8,640]{2,1,0:T(8,128)S(1)}, u32[]{:S(2)}, u32[]{:S(2)}) collective-permute-start(f32[16,8,640]{2,1,0:T(8,128)S(1)} %get-tuple-element.32), channel_id=1, source_target_pairs={{0,4},{1,5},{2,6},{3,7},{4,8},{5,9},{6,10},{7,11},{8,12},{9,13},{1... | collective-permute-start | bytes 983048 | tf_op jit(solution)/shard_map/ppermute | solution.py:292
  30.6 11.8 %collective-permute-start.6 = (f32[16,8,640]{2,1,0:T(8,128)S(1)}, f32[16,8,640]{2,1,0:T(8,128)S(1)}, u32[]{:S(2)}, u32[]{:S(2)}) collective-permute-start(f32[16,8,640]{2,1,0:T(8,128)S(1)} %get-tuple-element.33), channel_id=1, source_target_pairs={{0,254},{1,255},{2,252},{3,253},{4,0},{5,1},{6,2},{7,3},{8,4},{9,5... | collective-permute-start | bytes 983048 | tf_op jit(solution)/shard_map/ppermute | solution.py:292
  47.3 9.0 %collective-permute-start.8 = (f32[8,8,384]{2,1,0:T(8,128)S(1)}, f32[8,8,384]{2,1,0:T(8,128)S(1)}, u32[]{:S(2)}, u32[]{:S(2)}) collective-permute-start(f32[8,8,384]{2,1,0:T(8,128)S(1)} %get-tuple-element.34.own), channel_id=1, source_target_pairs={{0,254},{1,255},{2,252},{3,253},{4,8},{5,9},{6,10},{7,11},{8,4},{9... | collective-permute-start | bytes 294920 | tf_op jit(solution)/shard_map/ppermute | solution.py:302
  54.0 3.8 %collective-permute-start.7 = (f32[8,8,384]{2,1,0:T(8,128)S(1)}, f32[8,8,384]{2,1,0:T(8,128)S(1)}, u32[]{:S(2)}, u32[]{:S(2)}) collective-permute-start(f32[8,8,384]{2,1,0:T(8,128)S(1)} %get-tuple-element.34.own), channel_id=1, source_target_pairs={{0,4},{1,5},{2,6},{3,7},{4,0},{5,1},{6,2},{7,3},{8,12},{9,13},{10,... | collective-permute-start | bytes 294920 | tf_op jit(solution)/shard_map/ppermute | solution.py:302
  57.7 16.4 %copy-start.1 = (f32[4,16,1024]{2,1,0:T(8,128)S(1)}, f32[4,16,1024]{2,1,0:T(8,128)}, u32[]{:S(2)}) copy-start(f32[4,16,1024]{2,1,0:T(8,128)} %viscosity.1) | copy-start | bytes 786436
  60.1 9.2 %collective-permute-start.9 = (f32[11,8,256]{2,1,0:T(8,128)S(1)}, f32[11,8,256]{2,1,0:T(8,128)S(1)}, u32[]{:S(2)}, u32[]{:S(2)}) collective-permute-start(f32[11,8,256]{2,1,0:T(8,128)S(1)} %get-tuple-element.37), channel_id=1, source_target_pairs={{0,1},{1,0},{2,3},{3,2},{4,5},{5,4},{6,7},{7,6},{8,9},{9,8},{10,11... | collective-permute-start | bytes 270344 | tf_op jit(solution)/shard_map/ppermute | solution.py:283
  63.6 8.1 %collective-permute-start.10 = (f32[11,8,256]{2,1,0:T(8,128)S(1)}, f32[11,8,256]{2,1,0:T(8,128)S(1)}, u32[]{:S(2)}, u32[]{:S(2)}) collective-permute-start(f32[11,8,256]{2,1,0:T(8,128)S(1)} %get-tuple-element.38), channel_id=1, source_target_pairs={{0,2},{1,3},{2,0},{3,1},{4,6},{5,7},{6,4},{7,5},{8,10},{9,11},{10,... | collective-permute-start | bytes 270344 | tf_op jit(solution)/shard_map/ppermute | solution.py:283
  65.6 8.5 %collective-permute-start.11 = (f32[11,8,256]{2,1,0:T(8,128)S(1)}, f32[11,8,256]{2,1,0:T(8,128)S(1)}, u32[]{:S(2)}, u32[]{:S(2)}) collective-permute-start(f32[11,8,256]{2,1,0:T(8,128)S(1)} %get-tuple-element.39), channel_id=1, source_target_pairs={{0,3},{1,2},{2,1},{3,0},{4,7},{5,6},{6,5},{7,4},{8,11},{9,10},{10,... | collective-permute-start | bytes 270344 | tf_op jit(solution)/shard_map/ppermute | solution.py:283

commit v4 on v3

--- a/solution.py
+++ b/solution.py
@@ -46,22 +46,23 @@
         for j in range(LAYERS):
             loads.append(pltpu.make_async_copy(src.at[j], dst.at[j], done.at[f, j]))
             loads[-1].start()
-    for load in loads:
-        load.wait()
-    lane = lanes((LAYERS, ROWS, 128))
+    lane = lanes((ROWS, 128))
     right = lane < EDGE
     left = lane >= 128 - EDGE
-    for m, out in enumerate(outs):
-        base = ids[m] * MAIN
-        main = pl.ds(pl.multiple_of(base, 128), MAIN)
-        after = pl.ds(pl.multiple_of(lax.rem(base + MAIN, 1024), 128), 128)
-        before = pl.ds(pl.multiple_of(lax.rem(base + 1024 - 128, 1024), 128), 128)
-        out[:, :, 0:MAIN] = source[:, :, main]
-        out[:, :, MAIN : 2 * MAIN] = kappa[:, :, main]
-        edge_s = jnp.where(right, source[:, :, after], source[:, :, before])
-        edge_k = jnp.where(right, kappa[:, :, after], kappa[:, :, before])
-        edge_k = pltpu.roll(edge_k, 64, 2)
-        out[:, :, 2 * MAIN :] = jnp.where(right | left, edge_s, edge_k)
+    for j in range(LAYERS):
+        loads[j].wait()
+        loads[LAYERS + j].wait()
+        for m, out in enumerate(outs):
+            base = ids[m] * MAIN
+            main = pl.ds(pl.multiple_of(base, 128), MAIN)
+            after = pl.ds(pl.multiple_of(lax.rem(base + MAIN, 1024), 128), 128)
+            before = pl.ds(pl.multiple_of(lax.rem(base + 1024 - 128, 1024), 128), 128)
+            out[j, :, 0:MAIN] = source[j, :, main]
+            out[j, :, MAIN : 2 * MAIN] = kappa[j, :, main]
+            edge_s = jnp.where(right, source[j, :, after], source[j, :, before])
+            edge_k = jnp.where(right, kappa[j, :, after], kappa[j, :, before])
+            edge_k = pltpu.roll(edge_k, 64, 1)
+            out[j, :, 2 * MAIN :] = jnp.where(right | left, edge_s, edge_k)
 
 
 def pack_rows(ids, p0, p1, p2, p3, up, down):
@@ -310,7 +311,7 @@
         out_specs=[pl.BlockSpec(memory_space=pltpu.VMEM)] * 4,
         scratch_shapes=[slab, slab, pltpu.SemaphoreType.DMA((2, LAYERS))],
         compiler_params=VMEM,
-    )(ids, source, kappa)
+    )(ids, pltpu.with_memory_space_constraint(source, pltpu.HBM), pltpu.with_memory_space_constraint(kappa, pltpu.HBM))
     pieces = trade(pieces)
     near, ahead = lax.optimization_barrier((pieces[1], forward))
     forward_x = lax.ppermute(ahead[:, :1], "lat", [((i + 1) % lat_n, i) for i in range(lat_n)])

time: 75.9 us -> 74.4 us (0.980)
  local copies, waits for them, and re-layouts: 2.01 us -> 0.11 us
    unnamed x8 -> x4, local copies, waits for them, and re-layouts: 1.91 us -> 0.01 us
where the time goes in v4:
time: 74.4 us; the launch traced here: 74.3 us
  starting transfers between devices  41.2 us (55%)
  waiting for transfers between devices  20.9 us (28%)
  Pallas kernels  11.3 us (15%)
    ppermute x6, starting transfers between devices, trade(): lax.ppermute(pieces[m], 'rad', [(k, k ^ m) for k in range(rad_n)])  18.2 us
    pallas_call x4, Pallas kernels, call(): pl.pallas_call(kernel, out_shape=outs, in_specs=[pl.BlockSpec(memory_spac...  9.36 us
    ppermute x1, starting transfers between devices, body(): lax.ppermute(ahead[:, :1], 'lat', [((i + 1) % lat_n, i) for i in range(la...  7.33 us
    ppermute x6, waiting for transfers between devices, trade(): lax.ppermute(pieces[m], 'rad', [(k, k ^ m) for k in range(rad_n)])  7.14 us
    ppermute x2, starting transfers between devices, beside(): return lax.ppermute(v, ('lat', 'rad'), pairs)  6.97 us
    ppermute x2, starting transfers between devices, swaps(): out.append(lax.ppermute(v, ('lat', 'rad'), pairs))  6.69 us
    ppermute x2, waiting for transfers between devices, beside(): return lax.ppermute(v, ('lat', 'rad'), pairs)  6.57 us
    ppermute x2, waiting for transfers between devices, swaps(): out.append(lax.ppermute(v, ('lat', 'rad'), pairs))  3.76 us
  transfers between devices with their start and end apart: 12, of which 7 were waited for; matrix products, arithmetic and copies ran while one was open for 0% of the time, Pallas kernels for 0%

profile of v4, /device:TPU:1, one launch (start us, length us, event | category | flops | bytes accessed | tf_op | source)
XLA Modules:
  0.0 74.3 jit_solution(15059572390441974473)
XLA Ops:
  0.7 0.1 stack.27.ids
  0.8 0.0 copy-start
  0.8 2.0 %shard_map.59 = (f32[4,16,640]{2,1,0:T(8,128)S(1)}, f32[4,16,640]{2,1,0:T(8,128)S(1)}, f32[4,16,640]{2,1,0:T(8,128)S(1)}, f32[4,16,640]{2,1,0:T(8,128)S(1)}) custom-call(s32[6]{0:T(128)S(1)} %stack.27.ids, f32[4,16,1024]{2,1,0:T(8,128)} %source_hbm.1, f32[4,16,1024]{2,1,0:T(8,128)} %kappa_hbm.1), custom_call_target="tpu_custom_call" | custom-call | tf_op jit(solution)/shard_map/pallas_call | solution.py:307
  2.7 3.3 %collective-permute-start = (f32[4,16,640]{2,1,0:T(8,128)S(1)}, f32[4,16,640]{2,1,0:T(8,128)S(1)}, u32[]{:S(2)}, u32[]{:S(2)}) collective-permute-start(f32[4,16,640]{2,1,0:T(8,128)S(1)} %get-tuple-element.22), channel_id=1, source_target_pairs={{0,1},{1,0},{2,3},{3,2},{4,5},{5,4},{6,7},{7,6},{8,9},{9,8},{10,11... | collective-permute-start | bytes 491528 | tf_op jit(solution)/shard_map/ppermute | solution.py:284
  6.0 5.2 %collective-permute-start.3 = (f32[4,16,640]{2,1,0:T(8,128)S(1)}, f32[4,16,640]{2,1,0:T(8,128)S(1)}, u32[]{:S(2)}, u32[]{:S(2)}) collective-permute-start(f32[4,16,640]{2,1,0:T(8,128)S(1)} %get-tuple-element.26), channel_id=1, source_target_pairs={{0,2},{1,3},{2,0},{3,1},{4,6},{5,7},{6,4},{7,5},{8,10},{9,11},{10,... | collective-permute-start | bytes 491528 | tf_op jit(solution)/shard_map/ppermute | solution.py:284
  11.2 0.4 collective-permute-start.4
  11.7 0.0 collective-permute-done.p1
  11.7 0.0 copy-done
  11.7 2.1 %collective-permute-start.2 = (f32[1,16,1024]{2,1,0:T(8,128)S(1)}, f32[1,16,1024]{2,1,0:T(8,128)S(1)}, u32[]{:S(2)}, u32[]{:S(2)}) collective-permute-start(f32[1,16,1024]{2,1,0:T(8,128)S(1)} %slice.7), channel_id=1, source_target_pairs={{1,0},{2,1},{3,2},{5,4},{6,5},{7,6},{9,8},{10,9},{11,10},{13,12},{... | collective-permute-start | bytes 196616 | tf_op jit(solution)/shard_map/ppermute | solution.py:318
  13.8 7.3 %collective-permute-start.1 = (f32[4,1,1024]{2,1,0:T(1,128)S(1)}, f32[4,1,1024]{2,1,0:T(1,128)S(1)}, u32[]{:S(2)}, u32[]{:S(2)}) collective-permute-start(f32[4,1,1024]{2,1,0:T(1,128)S(1)} %slice.6), channel_id=1, source_target_pairs={{4,0},{8,4},{12,8},{16,12},{20,16},{24,20},{28,24},{32,28},{36,32}... | collective-permute-start | bytes 49160 | tf_op jit(solution)/shard_map/ppermute | solution.py:317
  21.1 0.0 collective-permute-done.3.p2
  21.1 2.3 %collective-permute-done.4.p3 = f32[4,16,640]{2,1,0:T(8,128)S(1)} collective-permute-done((f32[4,16,640]{2,1,0:T(8,128)S(1)}, f32[4,16,640]{2,1,0:T(8,128)S(1)}, u32[]{:S(2)}, u32[]{:S(2)}) %collective-permute-start.4) | collective-permute-done | bytes 163872 | tf_op jit(solution)/shard_map/ppermute | solution.py:284
  23.4 3.4 %collective-permute-done.1.forward_x = f32[4,1,1024]{2,1,0:T(1,128)S(1)} collective-permute-done((f32[4,1,1024]{2,1,0:T(1,128)S(1)}, f32[4,1,1024]{2,1,0:T(1,128)S(1)}, u32[]{:S(2)}, u32[]{:S(2)}) %collective-permute-start.1) | collective-permute-done | bytes 16416 | tf_op jit(solution)/shard_map/ppermute | solution.py:317
  26.8 0.0 collective-permute-done.2.forward_r
  26.8 0.6 shard_map.60
  27.4 1.8 %collective-permute-start.5 = (f32[16,8,640]{2,1,0:T(8,128)S(1)}, f32[16,8,640]{2,1,0:T(8,128)S(1)}, u32[]{:S(2)}, u32[]{:S(2)}) collective-permute-start(f32[16,8,640]{2,1,0:T(8,128)S(1)} %get-tuple-element.32), channel_id=1, source_target_pairs={{0,4},{1,5},{2,6},{3,7},{4,8},{5,9},{6,10},{7,11},{8,12},{9,13},{1... | collective-permute-start | bytes 983048 | tf_op jit(solution)/shard_map/ppermute | solution.py:293
  29.2 5.2 %collective-permute-start.6 = (f32[16,8,640]{2,1,0:T(8,128)S(1)}, f32[16,8,640]{2,1,0:T(8,128)S(1)}, u32[]{:S(2)}, u32[]{:S(2)}) collective-permute-start(f32[16,8,640]{2,1,0:T(8,128)S(1)} %get-tuple-element.33), channel_id=1, source_target_pairs={{0,254},{1,255},{2,252},{3,253},{4,0},{5,1},{6,2},{7,3},{8,4},{9,5... | collective-permute-start | bytes 983048 | tf_op jit(solution)/shard_map/ppermute | solution.py:293
  34.4 6.6 %collective-permute-done.5.lo = f32[16,8,640]{2,1,0:T(8,128)S(1)} collective-permute-done((f32[16,8,640]{2,1,0:T(8,128)S(1)}, f32[16,8,640]{2,1,0:T(8,128)S(1)}, u32[]{:S(2)}, u32[]{:S(2)}) %collective-permute-start.5) | collective-permute-done | bytes 327712 | tf_op jit(solution)/shard_map/ppermute | solution.py:293
  41.0 0.0 collective-permute-done.6.hi
  41.0 4.9 %shard_map.61 = (f32[16,24,256]{2,1,0:T(8,128)S(1)}, f32[8,8,384]{2,1,0:T(8,128)S(1)}) custom-call(s32[6]{0:T(128)S(1)} %stack.27.ids, f32[4,16,640]{2,1,0:T(8,128)S(1)} %get-tuple-element.28.p0, f32[4,16,640]{2,1,0:T(8,128)S(1)} %collective-permute-done.p1, f32[4,16,640]{2,1,0:T(8,128)S(1)} %collective-permute-done.3.p2, ...), custom_call_target="tpu_custom_call" | custom-call | tf_op jit(solution)/shard_map/pallas_call | solution.py:258
  45.9 6.7 %collective-permute-start.8 = (f32[8,8,384]{2,1,0:T(8,128)S(1)}, f32[8,8,384]{2,1,0:T(8,128)S(1)}, u32[]{:S(2)}, u32[]{:S(2)}) collective-permute-start(f32[8,8,384]{2,1,0:T(8,128)S(1)} %get-tuple-element.34.own), channel_id=1, source_target_pairs={{0,254},{1,255},{2,252},{3,253},{4,8},{5,9},{6,10},{7,11},{8,4},{9... | collective-permute-start | bytes 294920 | tf_op jit(solution)/shard_map/ppermute | solution.py:303
  52.6 0.0 collective-permute-start.7
  52.6 2.3 %collective-permute-done.8.far = f32[8,8,384]{2,1,0:T(8,128)S(1)} collective-permute-done((f32[8,8,384]{2,1,0:T(8,128)S(1)}, f32[8,8,384]{2,1,0:T(8,128)S(1)}, u32[]{:S(2)}, u32[]{:S(2)}) %collective-permute-start.8) | collective-permute-done | bytes 98336 | tf_op jit(solution)/shard_map/ppermute | solution.py:303
  54.9 1.5 %collective-permute-done.7.near = f32[8,8,384]{2,1,0:T(8,128)S(1)} collective-permute-done((f32[8,8,384]{2,1,0:T(8,128)S(1)}, f32[8,8,384]{2,1,0:T(8,128)S(1)}, u32[]{:S(2)}, u32[]{:S(2)}) %collective-permute-start.7) | collective-permute-done | bytes 98336 | tf_op jit(solution)/shard_map/ppermute | solution.py:303
  56.3 0.0 copy-start.1
  56.3 2.3 %shard_map.62 = (f32[11,8,256]{2,1,0:T(8,128)S(1)}, f32[11,8,256]{2,1,0:T(8,128)S(1)}, f32[11,8,256]{2,1,0:T(8,128)S(1)}, f32[11,8,256]{2,1,0:T(8,128)S(1)}) custom-call(s32[6]{0:T(128)S(1)} %stack.27.ids, f32[8,8,384]{2,1,0:T(8,128)S(1)} %collective-permute-done.7.near, f32[8,8,384]{2,1,0:T(8,128)S(1)} %get-tuple-element.34.own, ...), custom_call_target="tpu_custom_call" | custom-call | tf_op jit(solution)/shard_map/pallas_call | solution.py:258
  58.7 3.6 %collective-permute-start.9 = (f32[11,8,256]{2,1,0:T(8,128)S(1)}, f32[11,8,256]{2,1,0:T(8,128)S(1)}, u32[]{:S(2)}, u32[]{:S(2)}) collective-permute-start(f32[11,8,256]{2,1,0:T(8,128)S(1)} %get-tuple-element.37), channel_id=1, source_target_pairs={{0,1},{1,0},{2,3},{3,2},{4,5},{5,4},{6,7},{7,6},{8,9},{9,8},{10,11... | collective-permute-start | bytes 270344 | tf_op jit(solution)/shard_map/ppermute | solution.py:284
  62.3 2.0 %collective-permute-start.10 = (f32[11,8,256]{2,1,0:T(8,128)S(1)}, f32[11,8,256]{2,1,0:T(8,128)S(1)}, u32[]{:S(2)}, u32[]{:S(2)}) collective-permute-start(f32[11,8,256]{2,1,0:T(8,128)S(1)} %get-tuple-element.38), channel_id=1, source_target_pairs={{0,2},{1,3},{2,0},{3,1},{4,6},{5,7},{6,4},{7,5},{8,10},{9,11},{10,... | collective-permute-start | bytes 270344 | tf_op jit(solution)/shard_map/ppermute | solution.py:284
  64.2 3.7 %collective-permute-start.11 = (f32[11,8,256]{2,1,0:T(8,128)S(1)}, f32[11,8,256]{2,1,0:T(8,128)S(1)}, u32[]{:S(2)}, u32[]{:S(2)}) collective-permute-start(f32[11,8,256]{2,1,0:T(8,128)S(1)} %get-tuple-element.39), channel_id=1, source_target_pairs={{0,3},{1,2},{2,1},{3,0},{4,7},{5,6},{6,5},{7,4},{8,11},{9,10},{10,... | collective-permute-start | bytes 270344 | tf_op jit(solution)/shard_map/ppermute | solution.py:284
  67.9 0.0 collective-permute-done.9.p1
  67.9 2.4 %collective-permute-done.10.p2 = f32[11,8,256]{2,1,0:T(8,128)S(1)} collective-permute-done((f32[11,8,256]{2,1,0:T(8,128)S(1)}, f32[11,8,256]{2,1,0:T(8,128)S(1)}, u32[]{:S(2)}, u32[]{:S(2)}) %collective-permute-start.10) | collective-permute-done | bytes 90144 | tf_op jit(solution)/shard_map/ppermute | solution.py:284
  70.3 2.4 %collective-permute-done.11.p3 = f32[11,8,256]{2,1,0:T(8,128)S(1)} collective-permute-done((f32[11,8,256]{2,1,0:T(8,128)S(1)}, f32[11,8,256]{2,1,0:T(8,128)S(1)}, u32[]{:S(2)}, u32[]{:S(2)}) %collective-permute-start.11) | collective-permute-done | bytes 90144 | tf_op jit(solution)/shard_map/ppermute | solution.py:284
  72.7 0.0 copy-done.1
  72.7 1.6 %shard_map.63 = (f32[4,16,1024]{2,1,0:T(8,128)}, f32[4,16,1024]{2,1,0:T(8,128)}) custom-call(s32[6]{0:T(128)S(1)} %stack.27.ids, f32[11,8,256]{2,1,0:T(8,128)S(1)} %get-tuple-element.36.p0, f32[11,8,256]{2,1,0:T(8,128)S(1)} %collective-permute-done.9.p1, f32[11,8,256]{2,1,0:T(8,128)S(1)} %collective-permute-done.10.p2, ...), custom_call_target="tpu_custom_call" | custom-call | tf_op jit(solution)/shard_map/pallas_call | solution.py:258
  (2 shorter events, 0.0 us)
Async XLA Ops:
  0.8 10.9 %copy-start = (f32[4,16,1024]{2,1,0:T(8,128)S(1)}, f32[4,16,1024]{2,1,0:T(8,128)}, u32[]{:S(2)}) copy-start(f32[4,16,1024]{2,1,0:T(8,128)} %forward.1) | copy-start | bytes 786436
  2.7 9.0 %collective-permute-start = (f32[4,16,640]{2,1,0:T(8,128)S(1)}, f32[4,16,640]{2,1,0:T(8,128)S(1)}, u32[]{:S(2)}, u32[]{:S(2)}) collective-permute-start(f32[4,16,640]{2,1,0:T(8,128)S(1)} %get-tuple-element.22), channel_id=1, source_target_pairs={{0,1},{1,0},{2,3},{3,2},{4,5},{5,4},{6,7},{7,6},{8,9},{9,8},{10,11... | collective-permute-start | bytes 491528 | tf_op jit(solution)/shard_map/ppermute | solution.py:284
  6.0 15.1 %collective-permute-start.3 = (f32[4,16,640]{2,1,0:T(8,128)S(1)}, f32[4,16,640]{2,1,0:T(8,128)S(1)}, u32[]{:S(2)}, u32[]{:S(2)}) collective-permute-start(f32[4,16,640]{2,1,0:T(8,128)S(1)} %get-tuple-element.26), channel_id=1, source_target_pairs={{0,2},{1,3},{2,0},{3,1},{4,6},{5,7},{6,4},{7,5},{8,10},{9,11},{10,... | collective-permute-start | bytes 491528 | tf_op jit(solution)/shard_map/ppermute | solution.py:284
  11.2 12.2 %collective-permute-start.4 = (f32[4,16,640]{2,1,0:T(8,128)S(1)}, f32[4,16,640]{2,1,0:T(8,128)S(1)}, u32[]{:S(2)}, u32[]{:S(2)}) collective-permute-start(f32[4,16,640]{2,1,0:T(8,128)S(1)} %get-tuple-element.27), channel_id=1, source_target_pairs={{0,3},{1,2},{2,1},{3,0},{4,7},{5,6},{6,5},{7,4},{8,11},{9,10},{10,... | collective-permute-start | bytes 491528 | tf_op jit(solution)/shard_map/ppermute | solution.py:284
  11.7 15.1 %collective-permute-start.2 = (f32[1,16,1024]{2,1,0:T(8,128)S(1)}, f32[1,16,1024]{2,1,0:T(8,128)S(1)}, u32[]{:S(2)}, u32[]{:S(2)}) collective-permute-start(f32[1,16,1024]{2,1,0:T(8,128)S(1)} %slice.7), channel_id=1, source_target_pairs={{1,0},{2,1},{3,2},{5,4},{6,5},{7,6},{9,8},{10,9},{11,10},{13,12},{... | collective-permute-start | bytes 196616 | tf_op jit(solution)/shard_map/ppermute | solution.py:318
  13.8 13.1 %collective-permute-start.1 = (f32[4,1,1024]{2,1,0:T(1,128)S(1)}, f32[4,1,1024]{2,1,0:T(1,128)S(1)}, u32[]{:S(2)}, u32[]{:S(2)}) collective-permute-start(f32[4,1,1024]{2,1,0:T(1,128)S(1)} %slice.6), channel_id=1, source_target_pairs={{4,0},{8,4},{12,8},{16,12},{20,16},{24,20},{28,24},{32,28},{36,32}... | collective-permute-start | bytes 49160 | tf_op jit(solution)/shard_map/ppermute | solution.py:317
  27.4 13.5 %collective-permute-start.5 = (f32[16,8,640]{2,1,0:T(8,128)S(1)}, f32[16,8,640]{2,1,0:T(8,128)S(1)}, u32[]{:S(2)}, u32[]{:S(2)}) collective-permute-start(f32[16,8,640]{2,1,0:T(8,128)S(1)} %get-tuple-element.32), channel_id=1, source_target_pairs={{0,4},{1,5},{2,6},{3,7},{4,8},{5,9},{6,10},{7,11},{8,12},{9,13},{1... | collective-permute-start | bytes 983048 | tf_op jit(solution)/shard_map/ppermute | solution.py:293
  29.2 11.8 %collective-permute-start.6 = (f32[16,8,640]{2,1,0:T(8,128)S(1)}, f32[16,8,640]{2,1,0:T(8,128)S(1)}, u32[]{:S(2)}, u32[]{:S(2)}) collective-permute-start(f32[16,8,640]{2,1,0:T(8,128)S(1)} %get-tuple-element.33), channel_id=1, source_target_pairs={{0,254},{1,255},{2,252},{3,253},{4,0},{5,1},{6,2},{7,3},{8,4},{9,5... | collective-permute-start | bytes 983048 | tf_op jit(solution)/shard_map/ppermute | solution.py:293
  45.9 9.0 %collective-permute-start.8 = (f32[8,8,384]{2,1,0:T(8,128)S(1)}, f32[8,8,384]{2,1,0:T(8,128)S(1)}, u32[]{:S(2)}, u32[]{:S(2)}) collective-permute-start(f32[8,8,384]{2,1,0:T(8,128)S(1)} %get-tuple-element.34.own), channel_id=1, source_target_pairs={{0,254},{1,255},{2,252},{3,253},{4,8},{5,9},{6,10},{7,11},{8,4},{9... | collective-permute-start | bytes 294920 | tf_op jit(solution)/shard_map/ppermute | solution.py:303
  52.6 3.8 %collective-permute-start.7 = (f32[8,8,384]{2,1,0:T(8,128)S(1)}, f32[8,8,384]{2,1,0:T(8,128)S(1)}, u32[]{:S(2)}, u32[]{:S(2)}) collective-permute-start(f32[8,8,384]{2,1,0:T(8,128)S(1)} %get-tuple-element.34.own), channel_id=1, source_target_pairs={{0,4},{1,5},{2,6},{3,7},{4,0},{5,1},{6,2},{7,3},{8,12},{9,13},{10,... | collective-permute-start | bytes 294920 | tf_op jit(solution)/shard_map/ppermute | solution.py:303
  56.3 16.4 %copy-start.1 = (f32[4,16,1024]{2,1,0:T(8,128)S(1)}, f32[4,16,1024]{2,1,0:T(8,128)}, u32[]{:S(2)}) copy-start(f32[4,16,1024]{2,1,0:T(8,128)} %viscosity.1) | copy-start | bytes 786436
  58.7 9.2 %collective-permute-start.9 = (f32[11,8,256]{2,1,0:T(8,128)S(1)}, f32[11,8,256]{2,1,0:T(8,128)S(1)}, u32[]{:S(2)}, u32[]{:S(2)}) collective-permute-start(f32[11,8,256]{2,1,0:T(8,128)S(1)} %get-tuple-element.37), channel_id=1, source_target_pairs={{0,1},{1,0},{2,3},{3,2},{4,5},{5,4},{6,7},{7,6},{8,9},{9,8},{10,11... | collective-permute-start | bytes 270344 | tf_op jit(solution)/shard_map/ppermute | solution.py:284
  62.3 8.1 %collective-permute-start.10 = (f32[11,8,256]{2,1,0:T(8,128)S(1)}, f32[11,8,256]{2,1,0:T(8,128)S(1)}, u32[]{:S(2)}, u32[]{:S(2)}) collective-permute-start(f32[11,8,256]{2,1,0:T(8,128)S(1)} %get-tuple-element.38), channel_id=1, source_target_pairs={{0,2},{1,3},{2,0},{3,1},{4,6},{5,7},{6,4},{7,5},{8,10},{9,11},{10,... | collective-permute-start | bytes 270344 | tf_op jit(solution)/shard_map/ppermute | solution.py:284
  64.2 8.5 %collective-permute-start.11 = (f32[11,8,256]{2,1,0:T(8,128)S(1)}, f32[11,8,256]{2,1,0:T(8,128)S(1)}, u32[]{:S(2)}, u32[]{:S(2)}) collective-permute-start(f32[11,8,256]{2,1,0:T(8,128)S(1)} %get-tuple-element.39), channel_id=1, source_target_pairs={{0,3},{1,2},{2,1},{3,0},{4,7},{5,6},{6,5},{7,4},{8,11},{9,10},{10,... | collective-permute-start | bytes 270344 | tf_op jit(solution)/shard_map/ppermute | solution.py:284

commit v5 on v4

--- a/solution.py
+++ b/solution.py
@@ -279,10 +279,12 @@
     ids = jnp.stack(ids).astype(jnp.int32)
 
     def trade(pieces):
-        out = [pieces[0]]
-        for m in range(1, rad_n):
-            out.append(lax.ppermute(pieces[m], "rad", [(k, k ^ m) for k in range(rad_n)]))
-        return out
+        own, near, far, cross = pieces
+        far = lax.ppermute(far, "rad", [(k, k ^ 2) for k in range(rad_n)])
+        cross = lax.ppermute(cross, "rad", [(k, k ^ 3) for k in range(rad_n)])
+        far, near = lax.optimization_barrier((far, near))
+        near = lax.ppermute(near, "rad", [(k, k ^ 1) for k in range(rad_n)])
+        return [own, near, far, cross]
 
     def beside(v, way):
         pairs = []
@@ -313,13 +315,15 @@
         compiler_params=VMEM,
     )(ids, pltpu.with_memory_space_constraint(source, pltpu.HBM), pltpu.with_memory_space_constraint(kappa, pltpu.HBM))
     pieces = trade(pieces)
-    near, ahead = lax.optimization_barrier((pieces[1], forward))
-    forward_x = lax.ppermute(ahead[:, :1], "lat", [((i + 1) % lat_n, i) for i in range(lat_n)])
+    first, ahead = lax.optimization_barrier((pieces[2], forward))
     forward_r = lax.ppermute(ahead[:1], "rad", [(k + 1, k) for k in range(rad_n - 1)])
-    forward_x, forward_r, *pieces = lax.optimization_barrier((forward_x, forward_r, pieces[0], near, *pieces[2:]))
+    pieces[2] = first
     up, down = call(pack_rows, [struct(NR, HALO, PACKED)] * 2, [], ids, *pieces)
+    up, ahead = lax.optimization_barrier((up, forward))
     lo = beside(up, 1)
     hi = beside(down, -1)
+    forward_x = lax.ppermute(ahead[:, :1], "lat", [((i + 1) % lat_n, i) for i in range(lat_n)])
+    lo, hi, forward_r = lax.optimization_barrier((lo, hi, forward_r))
     deep = (NR, 2 * ROWS, WIDE)
     padded = (NR + 2, 2 * ROWS, WIDE)
     smooth, packed = call(
@@ -331,6 +335,7 @@
         lo,
         hi,
     )
+    packed, forward_x = lax.optimization_barrier((packed, forward_x))
     near, far = swaps(packed, packed)
     deep = (NR // 2, 3 * HALO, WIDE)
     padded = (NR // 2 + 2, 3 * HALO, WIDE)

time: 74.4 us -> 72.8 us (0.978)
  starting transfers between devices: 41.2 us -> 37.8 us
  waiting for transfers between devices: 20.9 us -> 22.8 us
    ppermute x2, waiting for transfers between devices: 6.57 us -> 0.01 us  [beside(): return lax.ppermute(v, ('lat', 'rad'), pairs)]
    ppermute x6, waiting for transfers between devices: 7.14 us -> 12.9 us  [the longest x2 6.49 us: trade(): far = lax.ppermute(far, 'rad', [(k, k ^ 2) for k in range(rad_n)])]
    ppermute x1, starting transfers between devices: 7.33 us -> 1.67 us  [body(): lax.ppermute(ahead[:, :1], 'lat', [((i + 1) % lat_n, i) for i in range(la...]
    ppermute x1, waiting for transfers between devices: 0.01 us -> 5.15 us  [body(): lax.ppermute(ahead[:1], 'rad', [(k + 1, k) for k in range(rad_n - 1)])]
    ppermute x1, waiting for transfers between devices: 3.43 us -> 0.01 us  [body(): lax.ppermute(ahead[:, :1], 'lat', [((i + 1) % lat_n, i) for i in range(la...]
    ppermute x2, starting transfers between devices: 6.97 us -> 9.08 us  [beside(): return lax.ppermute(v, ('lat', 'rad'), pairs)]
    ppermute x2, starting transfers between devices: 6.69 us -> 4.93 us  [swaps(): out.append(lax.ppermute(v, ('lat', 'rad'), pairs))]
    ppermute x6, starting transfers between devices: 18.2 us -> 19.4 us  [the longest x2 9.87 us: trade(): far = lax.ppermute(far, 'rad', [(k, k ^ 2) for k in range(rad_n)])]
  transfers between devices with their start and end apart: 12 -> 12, of which waited for: 7 -> 6; matrix products, arithmetic and copies ran while one was open for 0% -> 0% of each run, Pallas kernels for 0% -> 7%
where the time goes in v5:
time: 72.8 us; the launch traced here: 72.7 us
  starting transfers between devices  37.8 us (52%)
  waiting for transfers between devices  22.8 us (31%)
  Pallas kernels  11.3 us (16%)
  between operations  0.74 us (1%)
    ppermute x2, starting transfers between devices, trade(): far = lax.ppermute(far, 'rad', [(k, k ^ 2) for k in range(rad_n)])  9.87 us
    pallas_call x4, Pallas kernels, call(): pl.pallas_call(kernel, out_shape=outs, in_specs=[pl.BlockSpec(memory_spac...  9.36 us
    ppermute x2, starting transfers between devices, beside(): return lax.ppermute(v, ('lat', 'rad'), pairs)  9.08 us
    ppermute x2, waiting for transfers between devices, trade(): far = lax.ppermute(far, 'rad', [(k, k ^ 2) for k in range(rad_n)])  6.49 us
    ppermute x2, waiting for transfers between devices, trade(): cross = lax.ppermute(cross, 'rad', [(k, k ^ 3) for k in range(rad_n)])  6.39 us
    ppermute x1, waiting for transfers between devices, body(): lax.ppermute(ahead[:1], 'rad', [(k + 1, k) for k in range(rad_n - 1)])  5.15 us
    ppermute x2, starting transfers between devices, trade(): near = lax.ppermute(near, 'rad', [(k, k ^ 1) for k in range(rad_n)])  5.06 us
    ppermute x2, starting transfers between devices, swaps(): out.append(lax.ppermute(v, ('lat', 'rad'), pairs))  4.93 us
  transfers between devices with their start and end apart: 12, of which 6 were waited for; matrix products, arithmetic and copies ran while one was open for 0% of the time, Pallas kernels for 7%

profile of v5, /device:TPU:1, one launch (start us, length us, event | category | flops | bytes accessed | tf_op | source)
XLA Modules:
  0.0 72.7 jit_solution(1122928910021204338)
XLA Ops:
  0.7 0.1 stack.27.ids
  0.8 2.0 %shard_map.59 = (f32[4,16,640]{2,1,0:T(8,128)S(1)}, f32[4,16,640]{2,1,0:T(8,128)S(1)}, f32[4,16,640]{2,1,0:T(8,128)S(1)}, f32[4,16,640]{2,1,0:T(8,128)S(1)}) custom-call(s32[6]{0:T(128)S(1)} %stack.27.ids, f32[4,16,1024]{2,1,0:T(8,128)} %source_hbm.1, f32[4,16,1024]{2,1,0:T(8,128)} %kappa_hbm.1), custom_call_target="tpu_custom_call" | custom-call | tf_op jit(solution)/shard_map/pallas_call | solution.py:309
  2.7 7.8 %collective-permute-start = (f32[4,16,640]{2,1,0:T(8,128)S(1)}, f32[4,16,640]{2,1,0:T(8,128)S(1)}, u32[]{:S(2)}, u32[]{:S(2)}) collective-permute-start(f32[4,16,640]{2,1,0:T(8,128)S(1)} %get-tuple-element.28), channel_id=1, source_target_pairs={{0,2},{1,3},{2,0},{3,1},{4,6},{5,7},{6,4},{7,5},{8,10},{9,11},{10,... | collective-permute-start | bytes 491528 | tf_op jit(solution)/shard_map/ppermute | solution.py:283
  10.5 1.0 %collective-permute-start.2 = (f32[4,16,640]{2,1,0:T(8,128)S(1)}, f32[4,16,640]{2,1,0:T(8,128)S(1)}, u32[]{:S(2)}, u32[]{:S(2)}) collective-permute-start(f32[4,16,640]{2,1,0:T(8,128)S(1)} %get-tuple-element.33), channel_id=1, source_target_pairs={{0,3},{1,2},{2,1},{3,0},{4,7},{5,6},{6,5},{7,4},{8,11},{9,10},{10,... | collective-permute-start | bytes 491528 | tf_op jit(solution)/shard_map/ppermute | solution.py:284
  11.6 2.3 %collective-permute-done.p2 = f32[4,16,640]{2,1,0:T(8,128)S(1)} collective-permute-done((f32[4,16,640]{2,1,0:T(8,128)S(1)}, f32[4,16,640]{2,1,0:T(8,128)S(1)}, u32[]{:S(2)}, u32[]{:S(2)}) %collective-permute-start) | collective-permute-done | bytes 163872 | tf_op jit(solution)/shard_map/ppermute | solution.py:283
  13.9 4.6 %collective-permute-start.1 = (f32[4,16,640]{2,1,0:T(8,128)S(1)}, f32[4,16,640]{2,1,0:T(8,128)S(1)}, u32[]{:S(2)}, u32[]{:S(2)}) collective-permute-start(f32[4,16,640]{2,1,0:T(8,128)S(1)} %get-tuple-element.30), channel_id=1, source_target_pairs={{0,1},{1,0},{2,3},{3,2},{4,5},{5,4},{6,7},{7,6},{8,9},{9,8},{10,11... | collective-permute-start | bytes 491528 | tf_op jit(solution)/shard_map/ppermute | solution.py:286
  18.5 4.9 %collective-permute-done.2.p3 = f32[4,16,640]{2,1,0:T(8,128)S(1)} collective-permute-done((f32[4,16,640]{2,1,0:T(8,128)S(1)}, f32[4,16,640]{2,1,0:T(8,128)S(1)}, u32[]{:S(2)}, u32[]{:S(2)}) %collective-permute-start.2) | collective-permute-done | bytes 163872 | tf_op jit(solution)/shard_map/ppermute | solution.py:284
  23.5 0.0 collective-permute-done.1.p1
  23.5 0.0 copy-start
  23.5 0.6 shard_map.60
  24.1 3.0 %collective-permute-start.3 = (f32[16,8,640]{2,1,0:T(8,128)S(1)}, f32[16,8,640]{2,1,0:T(8,128)S(1)}, u32[]{:S(2)}, u32[]{:S(2)}) collective-permute-start(f32[16,8,640]{2,1,0:T(8,128)S(1)} %get-tuple-element.35), channel_id=1, source_target_pairs={{0,4},{1,5},{2,6},{3,7},{4,8},{5,9},{6,10},{7,11},{8,12},{9,13},{1... | collective-permute-start | bytes 983048 | tf_op jit(solution)/shard_map/ppermute | solution.py:295
  27.1 6.1 %collective-permute-start.4 = (f32[16,8,640]{2,1,0:T(8,128)S(1)}, f32[16,8,640]{2,1,0:T(8,128)S(1)}, u32[]{:S(2)}, u32[]{:S(2)}) collective-permute-start(f32[16,8,640]{2,1,0:T(8,128)S(1)} %get-tuple-element.36), channel_id=1, source_target_pairs={{0,254},{1,255},{2,252},{3,253},{4,0},{5,1},{6,2},{7,3},{8,4},{9,5... | collective-permute-start | bytes 983048 | tf_op jit(solution)/shard_map/ppermute | solution.py:295
  33.1 0.0 copy-done
  33.1 2.6 %collective-permute-start.5 = (f32[1,16,1024]{2,1,0:T(8,128)S(1)}, f32[1,16,1024]{2,1,0:T(8,128)S(1)}, u32[]{:S(2)}, u32[]{:S(2)}) collective-permute-start(f32[1,16,1024]{2,1,0:T(8,128)S(1)} %slice.6), channel_id=1, source_target_pairs={{1,0},{2,1},{3,2},{5,4},{6,5},{7,6},{9,8},{10,9},{11,10},{13,12},{... | collective-permute-start | bytes 196616 | tf_op jit(solution)/shard_map/ppermute | solution.py:319
  35.8 1.7 %collective-permute-start.6 = (f32[4,1,1024]{2,1,0:T(1,128)S(1)}, f32[4,1,1024]{2,1,0:T(1,128)S(1)}, u32[]{:S(2)}, u32[]{:S(2)}) collective-permute-start(f32[4,1,1024]{2,1,0:T(1,128)S(1)} %slice.7), channel_id=1, source_target_pairs={{4,0},{8,4},{12,8},{16,12},{20,16},{24,20},{28,24},{32,28},{36,32}... | collective-permute-start | bytes 49160 | tf_op jit(solution)/shard_map/ppermute | solution.py:325
  37.5 5.2 %collective-permute-done.5.forward_r = f32[1,16,1024]{2,1,0:T(8,128)S(1)} collective-permute-done((f32[1,16,1024]{2,1,0:T(8,128)S(1)}, f32[1,16,1024]{2,1,0:T(8,128)S(1)}, u32[]{:S(2)}, u32[]{:S(2)}) %collective-permute-start.5) | collective-permute-done | bytes 65568 | tf_op jit(solution)/shard_map/ppermute | solution.py:319
  42.6 0.0 collective-permute-done.3.lo
  42.6 0.0 collective-permute-done.4.hi
  42.6 4.9 %shard_map.61 = (f32[16,24,256]{2,1,0:T(8,128)S(1)}, f32[8,8,384]{2,1,0:T(8,128)S(1)}) custom-call(s32[6]{0:T(128)S(1)} %stack.27.ids, f32[4,16,640]{2,1,0:T(8,128)S(1)} %get-tuple-element.27.p0, f32[4,16,640]{2,1,0:T(8,128)S(1)} %collective-permute-done.1.p1, f32[4,16,640]{2,1,0:T(8,128)S(1)} %collective-permute-done.p2, ...), custom_call_target="tpu_custom_call" | custom-call | tf_op jit(solution)/shard_map/pallas_call | solution.py:258
  47.5 0.0 collective-permute-done.6.forward_x
  47.6 0.6 collective-permute-start.7
  48.1 4.4 %collective-permute-start.8 = (f32[8,8,384]{2,1,0:T(8,128)S(1)}, f32[8,8,384]{2,1,0:T(8,128)S(1)}, u32[]{:S(2)}, u32[]{:S(2)}) collective-permute-start(f32[8,8,384]{2,1,0:T(8,128)S(1)} %get-tuple-element.42.own), channel_id=1, source_target_pairs={{0,254},{1,255},{2,252},{3,253},{4,8},{5,9},{6,10},{7,11},{8,4},{9... | collective-permute-start | bytes 294920 | tf_op jit(solution)/shard_map/ppermute | solution.py:305
  52.5 0.0 collective-permute-done.7.near
  52.5 4.7 %collective-permute-done.8.far = f32[8,8,384]{2,1,0:T(8,128)S(1)} collective-permute-done((f32[8,8,384]{2,1,0:T(8,128)S(1)}, f32[8,8,384]{2,1,0:T(8,128)S(1)}, u32[]{:S(2)}, u32[]{:S(2)}) %collective-permute-start.8) | collective-permute-done | bytes 98336 | tf_op jit(solution)/shard_map/ppermute | solution.py:305
  57.2 0.0 copy-start.1
  57.2 2.3 %shard_map.62 = (f32[11,8,256]{2,1,0:T(8,128)S(1)}, f32[11,8,256]{2,1,0:T(8,128)S(1)}, f32[11,8,256]{2,1,0:T(8,128)S(1)}, f32[11,8,256]{2,1,0:T(8,128)S(1)}) custom-call(s32[6]{0:T(128)S(1)} %stack.27.ids, f32[8,8,384]{2,1,0:T(8,128)S(1)} %collective-permute-done.7.near, f32[8,8,384]{2,1,0:T(8,128)S(1)} %get-tuple-element.42.own, ...), custom_call_target="tpu_custom_call" | custom-call | tf_op jit(solution)/shard_map/pallas_call | solution.py:258
  59.5 2.0 %collective-permute-start.9 = (f32[11,8,256]{2,1,0:T(8,128)S(1)}, f32[11,8,256]{2,1,0:T(8,128)S(1)}, u32[]{:S(2)}, u32[]{:S(2)}) collective-permute-start(f32[11,8,256]{2,1,0:T(8,128)S(1)} %get-tuple-element.45), channel_id=1, source_target_pairs={{0,2},{1,3},{2,0},{3,1},{4,6},{5,7},{6,4},{7,5},{8,10},{9,11},{10,... | collective-permute-start | bytes 270344 | tf_op jit(solution)/shard_map/ppermute | solution.py:283
  61.6 3.5 %collective-permute-start.11 = (f32[11,8,256]{2,1,0:T(8,128)S(1)}, f32[11,8,256]{2,1,0:T(8,128)S(1)}, u32[]{:S(2)}, u32[]{:S(2)}) collective-permute-start(f32[11,8,256]{2,1,0:T(8,128)S(1)} %get-tuple-element.49), channel_id=1, source_target_pairs={{0,3},{1,2},{2,1},{3,0},{4,7},{5,6},{6,5},{7,4},{8,11},{9,10},{10,... | collective-permute-start | bytes 270344 | tf_op jit(solution)/shard_map/ppermute | solution.py:284
  65.0 4.1 %collective-permute-done.9.p2 = f32[11,8,256]{2,1,0:T(8,128)S(1)} collective-permute-done((f32[11,8,256]{2,1,0:T(8,128)S(1)}, f32[11,8,256]{2,1,0:T(8,128)S(1)}, u32[]{:S(2)}, u32[]{:S(2)}) %collective-permute-start.9) | collective-permute-done | bytes 90144 | tf_op jit(solution)/shard_map/ppermute | solution.py:283
  69.2 0.5 collective-permute-start.10
  69.6 1.5 %collective-permute-done.11.p3 = f32[11,8,256]{2,1,0:T(8,128)S(1)} collective-permute-done((f32[11,8,256]{2,1,0:T(8,128)S(1)}, f32[11,8,256]{2,1,0:T(8,128)S(1)}, u32[]{:S(2)}, u32[]{:S(2)}) %collective-permute-start.11) | collective-permute-done | bytes 90144 | tf_op jit(solution)/shard_map/ppermute | solution.py:284
  71.1 0.0 collective-permute-done.10.p1
  71.1 0.0 copy-done.1
  71.1 1.6 %shard_map.63 = (f32[4,16,1024]{2,1,0:T(8,128)}, f32[4,16,1024]{2,1,0:T(8,128)}) custom-call(s32[6]{0:T(128)S(1)} %stack.27.ids, f32[11,8,256]{2,1,0:T(8,128)S(1)} %get-tuple-element.44.p0, f32[11,8,256]{2,1,0:T(8,128)S(1)} %collective-permute-done.10.p1, f32[11,8,256]{2,1,0:T(8,128)S(1)} %collective-permute-done.9.p2, ...), custom_call_target="tpu_custom_call" | custom-call | tf_op jit(solution)/shard_map/pallas_call | solution.py:258
  (2 shorter events, 0.0 us)
Async XLA Ops:
  2.7 11.2 %collective-permute-start = (f32[4,16,640]{2,1,0:T(8,128)S(1)}, f32[4,16,640]{2,1,0:T(8,128)S(1)}, u32[]{:S(2)}, u32[]{:S(2)}) collective-permute-start(f32[4,16,640]{2,1,0:T(8,128)S(1)} %get-tuple-element.28), channel_id=1, source_target_pairs={{0,2},{1,3},{2,0},{3,1},{4,6},{5,7},{6,4},{7,5},{8,10},{9,11},{10,... | collective-permute-start | bytes 491528 | tf_op jit(solution)/shard_map/ppermute | solution.py:283
  10.5 12.9 %collective-permute-start.2 = (f32[4,16,640]{2,1,0:T(8,128)S(1)}, f32[4,16,640]{2,1,0:T(8,128)S(1)}, u32[]{:S(2)}, u32[]{:S(2)}) collective-permute-start(f32[4,16,640]{2,1,0:T(8,128)S(1)} %get-tuple-element.33), channel_id=1, source_target_pairs={{0,3},{1,2},{2,1},{3,0},{4,7},{5,6},{6,5},{7,4},{8,11},{9,10},{10,... | collective-permute-start | bytes 491528 | tf_op jit(solution)/shard_map/ppermute | solution.py:284
  13.9 9.5 %collective-permute-start.1 = (f32[4,16,640]{2,1,0:T(8,128)S(1)}, f32[4,16,640]{2,1,0:T(8,128)S(1)}, u32[]{:S(2)}, u32[]{:S(2)}) collective-permute-start(f32[4,16,640]{2,1,0:T(8,128)S(1)} %get-tuple-element.30), channel_id=1, source_target_pairs={{0,1},{1,0},{2,3},{3,2},{4,5},{5,4},{6,7},{7,6},{8,9},{9,8},{10,11... | collective-permute-start | bytes 491528 | tf_op jit(solution)/shard_map/ppermute | solution.py:286
  23.5 9.7 %copy-start = (f32[4,16,1024]{2,1,0:T(8,128)S(1)}, f32[4,16,1024]{2,1,0:T(8,128)}, u32[]{:S(2)}) copy-start(f32[4,16,1024]{2,1,0:T(8,128)} %forward.1) | copy-start | bytes 786436
  24.1 18.6 %collective-permute-start.3 = (f32[16,8,640]{2,1,0:T(8,128)S(1)}, f32[16,8,640]{2,1,0:T(8,128)S(1)}, u32[]{:S(2)}, u32[]{:S(2)}) collective-permute-start(f32[16,8,640]{2,1,0:T(8,128)S(1)} %get-tuple-element.35), channel_id=1, source_target_pairs={{0,4},{1,5},{2,6},{3,7},{4,8},{5,9},{6,10},{7,11},{8,12},{9,13},{1... | collective-permute-start | bytes 983048 | tf_op jit(solution)/shard_map/ppermute | solution.py:295
  27.1 15.6 %collective-permute-start.4 = (f32[16,8,640]{2,1,0:T(8,128)S(1)}, f32[16,8,640]{2,1,0:T(8,128)S(1)}, u32[]{:S(2)}, u32[]{:S(2)}) collective-permute-start(f32[16,8,640]{2,1,0:T(8,128)S(1)} %get-tuple-element.36), channel_id=1, source_target_pairs={{0,254},{1,255},{2,252},{3,253},{4,0},{5,1},{6,2},{7,3},{8,4},{9,5... | collective-permute-start | bytes 983048 | tf_op jit(solution)/shard_map/ppermute | solution.py:295
  33.1 9.5 %collective-permute-start.5 = (f32[1,16,1024]{2,1,0:T(8,128)S(1)}, f32[1,16,1024]{2,1,0:T(8,128)S(1)}, u32[]{:S(2)}, u32[]{:S(2)}) collective-permute-start(f32[1,16,1024]{2,1,0:T(8,128)S(1)} %slice.6), channel_id=1, source_target_pairs={{1,0},{2,1},{3,2},{5,4},{6,5},{7,6},{9,8},{10,9},{11,10},{13,12},{... | collective-permute-start | bytes 196616 | tf_op jit(solution)/shard_map/ppermute | solution.py:319
  35.8 11.7 %collective-permute-start.6 = (f32[4,1,1024]{2,1,0:T(1,128)S(1)}, f32[4,1,1024]{2,1,0:T(1,128)S(1)}, u32[]{:S(2)}, u32[]{:S(2)}) collective-permute-start(f32[4,1,1024]{2,1,0:T(1,128)S(1)} %slice.7), channel_id=1, source_target_pairs={{4,0},{8,4},{12,8},{16,12},{20,16},{24,20},{28,24},{32,28},{36,32}... | collective-permute-start | bytes 49160 | tf_op jit(solution)/shard_map/ppermute | solution.py:325
  47.6 4.9 %collective-permute-start.7 = (f32[8,8,384]{2,1,0:T(8,128)S(1)}, f32[8,8,384]{2,1,0:T(8,128)S(1)}, u32[]{:S(2)}, u32[]{:S(2)}) collective-permute-start(f32[8,8,384]{2,1,0:T(8,128)S(1)} %get-tuple-element.42.own), channel_id=1, source_target_pairs={{0,4},{1,5},{2,6},{3,7},{4,0},{5,1},{6,2},{7,3},{8,12},{9,13},{10,... | collective-permute-start | bytes 294920 | tf_op jit(solution)/shard_map/ppermute | solution.py:305
  48.1 9.1 %collective-permute-start.8 = (f32[8,8,384]{2,1,0:T(8,128)S(1)}, f32[8,8,384]{2,1,0:T(8,128)S(1)}, u32[]{:S(2)}, u32[]{:S(2)}) collective-permute-start(f32[8,8,384]{2,1,0:T(8,128)S(1)} %get-tuple-element.42.own), channel_id=1, source_target_pairs={{0,254},{1,255},{2,252},{3,253},{4,8},{5,9},{6,10},{7,11},{8,4},{9... | collective-permute-start | bytes 294920 | tf_op jit(solution)/shard_map/ppermute | solution.py:305
  57.2 13.9 %copy-start.1 = (f32[4,16,1024]{2,1,0:T(8,128)S(1)}, f32[4,16,1024]{2,1,0:T(8,128)}, u32[]{:S(2)}) copy-start(f32[4,16,1024]{2,1,0:T(8,128)} %viscosity.1) | copy-start | bytes 786436
  59.5 9.7 %collective-permute-start.9 = (f32[11,8,256]{2,1,0:T(8,128)S(1)}, f32[11,8,256]{2,1,0:T(8,128)S(1)}, u32[]{:S(2)}, u32[]{:S(2)}) collective-permute-start(f32[11,8,256]{2,1,0:T(8,128)S(1)} %get-tuple-element.45), channel_id=1, source_target_pairs={{0,2},{1,3},{2,0},{3,1},{4,6},{5,7},{6,4},{7,5},{8,10},{9,11},{10,... | collective-permute-start | bytes 270344 | tf_op jit(solution)/shard_map/ppermute | solution.py:283
  61.6 9.5 %collective-permute-start.11 = (f32[11,8,256]{2,1,0:T(8,128)S(1)}, f32[11,8,256]{2,1,0:T(8,128)S(1)}, u32[]{:S(2)}, u32[]{:S(2)}) collective-permute-start(f32[11,8,256]{2,1,0:T(8,128)S(1)} %get-tuple-element.49), channel_id=1, source_target_pairs={{0,3},{1,2},{2,1},{3,0},{4,7},{5,6},{6,5},{7,4},{8,11},{9,10},{10,... | collective-permute-start | bytes 270344 | tf_op jit(solution)/shard_map/ppermute | solution.py:284
  69.2 1.9 %collective-permute-start.10 = (f32[11,8,256]{2,1,0:T(8,128)S(1)}, f32[11,8,256]{2,1,0:T(8,128)S(1)}, u32[]{:S(2)}, u32[]{:S(2)}) collective-permute-start(f32[11,8,256]{2,1,0:T(8,128)S(1)} %get-tuple-element.47), channel_id=1, source_target_pairs={{0,1},{1,0},{2,3},{3,2},{4,5},{5,4},{6,7},{7,6},{8,9},{9,8},{10,11... | collective-permute-start | bytes 270344 | tf_op jit(solution)/shard_map/ppermute | solution.py:286

commit v6 on v5

--- a/solution.py
+++ b/solution.py
@@ -323,7 +323,6 @@
     lo = beside(up, 1)
     hi = beside(down, -1)
     forward_x = lax.ppermute(ahead[:, :1], "lat", [((i + 1) % lat_n, i) for i in range(lat_n)])
-    lo, hi, forward_r = lax.optimization_barrier((lo, hi, forward_r))
     deep = (NR, 2 * ROWS, WIDE)
     padded = (NR + 2, 2 * ROWS, WIDE)
     smooth, packed = call(
@@ -335,7 +334,7 @@
         lo,
         hi,
     )
-    packed, forward_x = lax.optimization_barrier((packed, forward_x))
+    packed, forward_x, forward_r = lax.optimization_barrier((packed, forward_x, forward_r))
     near, far = swaps(packed, packed)
     deep = (NR // 2, 3 * HALO, WIDE)
     padded = (NR // 2 + 2, 3 * HALO, WIDE)

time: 72.8 us -> 72.4 us (level)
  waiting for transfers between devices: 22.8 us -> 16.5 us
  starting transfers between devices: 37.8 us -> 43.6 us
    ppermute x1, waiting for transfers between devices: 5.15 us -> 0.01 us  [body(): lax.ppermute(ahead[:1], 'rad', [(k + 1, k) for k in range(rad_n - 1)])]
    ppermute x2, waiting for transfers between devices: 6.49 us -> 3.13 us  [trade(): far = lax.ppermute(far, 'rad', [(k, k ^ 2) for k in range(rad_n)])]
    ppermute x2, waiting for transfers between devices: 0.01 us -> 3.25 us  [beside(): return lax.ppermute(v, ('lat', 'rad'), pairs)]
    ppermute x2, starting transfers between devices: 9.87 us -> 12.4 us  [trade(): far = lax.ppermute(far, 'rad', [(k, k ^ 2) for k in range(rad_n)])]
    ppermute x2, waiting for transfers between devices: 4.73 us -> 2.24 us  [swaps(): out.append(lax.ppermute(v, ('lat', 'rad'), pairs))]
    ppermute x2, starting transfers between devices: 4.93 us -> 6.83 us  [swaps(): out.append(lax.ppermute(v, ('lat', 'rad'), pairs))]
    ppermute x2, starting transfers between devices: 5.06 us -> 6.71 us  [trade(): near = lax.ppermute(near, 'rad', [(k, k ^ 1) for k in range(rad_n)])]
    ppermute x2, waiting for transfers between devices: 6.39 us -> 7.86 us  [trade(): cross = lax.ppermute(cross, 'rad', [(k, k ^ 3) for k in range(rad_n)])]
where the time goes in v6:
time: 72.4 us; the launch traced here: 72.2 us
  starting transfers between devices  43.6 us (60%)
  waiting for transfers between devices  16.5 us (23%)
  Pallas kernels  11.3 us (16%)
  between operations  0.75 us (1%)
    ppermute x2, starting transfers between devices, trade(): far = lax.ppermute(far, 'rad', [(k, k ^ 2) for k in range(rad_n)])  12.4 us
    pallas_call x4, Pallas kernels, call(): pl.pallas_call(kernel, out_shape=outs, in_specs=[pl.BlockSpec(memory_spac...  9.36 us
    ppermute x2, starting transfers between devices, beside(): return lax.ppermute(v, ('lat', 'rad'), pairs)  9.08 us
    ppermute x2, waiting for transfers between devices, trade(): cross = lax.ppermute(cross, 'rad', [(k, k ^ 3) for k in range(rad_n)])  7.86 us
    ppermute x2, starting transfers between devices, swaps(): out.append(lax.ppermute(v, ('lat', 'rad'), pairs))  6.83 us
    ppermute x2, starting transfers between devices, trade(): near = lax.ppermute(near, 'rad', [(k, k ^ 1) for k in range(rad_n)])  6.71 us
    ppermute x2, starting transfers between devices, trade(): cross = lax.ppermute(cross, 'rad', [(k, k ^ 3) for k in range(rad_n)])  4.26 us
    ppermute x2, waiting for transfers between devices, beside(): return lax.ppermute(v, ('lat', 'rad'), pairs)  3.25 us
  transfers between devices with their start and end apart: 12, of which 6 were waited for; matrix products, arithmetic and copies ran while one was open for 0% of the time, Pallas kernels for 7%

profile of v6, /device:TPU:1, one launch (start us, length us, event | category | flops | bytes accessed | tf_op | source)
XLA Modules:
  0.0 72.2 jit_solution(3171797963182694825)
XLA Ops:
  0.7 0.1 stack.27.ids
  0.8 2.0 %shard_map.59 = (f32[4,16,640]{2,1,0:T(8,128)S(1)}, f32[4,16,640]{2,1,0:T(8,128)S(1)}, f32[4,16,640]{2,1,0:T(8,128)S(1)}, f32[4,16,640]{2,1,0:T(8,128)S(1)}) custom-call(s32[6]{0:T(128)S(1)} %stack.27.ids, f32[4,16,1024]{2,1,0:T(8,128)} %source_hbm.1, f32[4,16,1024]{2,1,0:T(8,128)} %kappa_hbm.1), custom_call_target="tpu_custom_call" | custom-call | tf_op jit(solution)/shard_map/pallas_call | solution.py:309
  2.7 7.8 %collective-permute-start = (f32[4,16,640]{2,1,0:T(8,128)S(1)}, f32[4,16,640]{2,1,0:T(8,128)S(1)}, u32[]{:S(2)}, u32[]{:S(2)}) collective-permute-start(f32[4,16,640]{2,1,0:T(8,128)S(1)} %get-tuple-element.26), channel_id=1, source_target_pairs={{0,2},{1,3},{2,0},{3,1},{4,6},{5,7},{6,4},{7,5},{8,10},{9,11},{10,... | collective-permute-start | bytes 491528 | tf_op jit(solution)/shard_map/ppermute | solution.py:283
  10.5 1.0 %collective-permute-start.2 = (f32[4,16,640]{2,1,0:T(8,128)S(1)}, f32[4,16,640]{2,1,0:T(8,128)S(1)}, u32[]{:S(2)}, u32[]{:S(2)}) collective-permute-start(f32[4,16,640]{2,1,0:T(8,128)S(1)} %get-tuple-element.31), channel_id=1, source_target_pairs={{0,3},{1,2},{2,1},{3,0},{4,7},{5,6},{6,5},{7,4},{8,11},{9,10},{10,... | collective-permute-start | bytes 491528 | tf_op jit(solution)/shard_map/ppermute | solution.py:284
  11.6 2.3 %collective-permute-done.p2 = f32[4,16,640]{2,1,0:T(8,128)S(1)} collective-permute-done((f32[4,16,640]{2,1,0:T(8,128)S(1)}, f32[4,16,640]{2,1,0:T(8,128)S(1)}, u32[]{:S(2)}, u32[]{:S(2)}) %collective-permute-start) | collective-permute-done | bytes 163872 | tf_op jit(solution)/shard_map/ppermute | solution.py:283
  13.9 4.6 %collective-permute-start.1 = (f32[4,16,640]{2,1,0:T(8,128)S(1)}, f32[4,16,640]{2,1,0:T(8,128)S(1)}, u32[]{:S(2)}, u32[]{:S(2)}) collective-permute-start(f32[4,16,640]{2,1,0:T(8,128)S(1)} %get-tuple-element.28), channel_id=1, source_target_pairs={{0,1},{1,0},{2,3},{3,2},{4,5},{5,4},{6,7},{7,6},{8,9},{9,8},{10,11... | collective-permute-start | bytes 491528 | tf_op jit(solution)/shard_map/ppermute | solution.py:286
  18.5 4.9 %collective-permute-done.2.p3 = f32[4,16,640]{2,1,0:T(8,128)S(1)} collective-permute-done((f32[4,16,640]{2,1,0:T(8,128)S(1)}, f32[4,16,640]{2,1,0:T(8,128)S(1)}, u32[]{:S(2)}, u32[]{:S(2)}) %collective-permute-start.2) | collective-permute-done | bytes 163872 | tf_op jit(solution)/shard_map/ppermute | solution.py:284
  23.5 0.0 collective-permute-done.1.p1
  23.5 0.0 copy-start
  23.5 0.6 shard_map.60
  24.1 3.0 %collective-permute-start.3 = (f32[16,8,640]{2,1,0:T(8,128)S(1)}, f32[16,8,640]{2,1,0:T(8,128)S(1)}, u32[]{:S(2)}, u32[]{:S(2)}) collective-permute-start(f32[16,8,640]{2,1,0:T(8,128)S(1)} %get-tuple-element.33), channel_id=1, source_target_pairs={{0,4},{1,5},{2,6},{3,7},{4,8},{5,9},{6,10},{7,11},{8,12},{9,13},{1... | collective-permute-start | bytes 983048 | tf_op jit(solution)/shard_map/ppermute | solution.py:295
  27.1 6.1 %collective-permute-start.4 = (f32[16,8,640]{2,1,0:T(8,128)S(1)}, f32[16,8,640]{2,1,0:T(8,128)S(1)}, u32[]{:S(2)}, u32[]{:S(2)}) collective-permute-start(f32[16,8,640]{2,1,0:T(8,128)S(1)} %get-tuple-element.34), channel_id=1, source_target_pairs={{0,254},{1,255},{2,252},{3,253},{4,0},{5,1},{6,2},{7,3},{8,4},{9,5... | collective-permute-start | bytes 983048 | tf_op jit(solution)/shard_map/ppermute | solution.py:295
  33.1 0.0 copy-done
  33.1 2.6 %collective-permute-start.6 = (f32[1,16,1024]{2,1,0:T(8,128)S(1)}, f32[1,16,1024]{2,1,0:T(8,128)S(1)}, u32[]{:S(2)}, u32[]{:S(2)}) collective-permute-start(f32[1,16,1024]{2,1,0:T(8,128)S(1)} %slice.7), channel_id=1, source_target_pairs={{1,0},{2,1},{3,2},{5,4},{6,5},{7,6},{9,8},{10,9},{11,10},{13,12},{... | collective-permute-start | bytes 196616 | tf_op jit(solution)/shard_map/ppermute | solution.py:319
  35.8 1.7 %collective-permute-start.5 = (f32[4,1,1024]{2,1,0:T(1,128)S(1)}, f32[4,1,1024]{2,1,0:T(1,128)S(1)}, u32[]{:S(2)}, u32[]{:S(2)}) collective-permute-start(f32[4,1,1024]{2,1,0:T(1,128)S(1)} %slice.6), channel_id=1, source_target_pairs={{4,0},{8,4},{12,8},{16,12},{20,16},{24,20},{28,24},{32,28},{36,32}... | collective-permute-start | bytes 49160 | tf_op jit(solution)/shard_map/ppermute | solution.py:325
  37.5 3.2 %collective-permute-done.3.lo = f32[16,8,640]{2,1,0:T(8,128)S(1)} collective-permute-done((f32[16,8,640]{2,1,0:T(8,128)S(1)}, f32[16,8,640]{2,1,0:T(8,128)S(1)}, u32[]{:S(2)}, u32[]{:S(2)}) %collective-permute-start.3) | collective-permute-done | bytes 327712 | tf_op jit(solution)/shard_map/ppermute | solution.py:295
  40.7 0.0 collective-permute-done.4.hi
  40.7 4.9 %shard_map.61 = (f32[16,24,256]{2,1,0:T(8,128)S(1)}, f32[8,8,384]{2,1,0:T(8,128)S(1)}) custom-call(s32[6]{0:T(128)S(1)} %stack.27.ids, f32[4,16,640]{2,1,0:T(8,128)S(1)} %get-tuple-element.25.p0, f32[4,16,640]{2,1,0:T(8,128)S(1)} %collective-permute-done.1.p1, f32[4,16,640]{2,1,0:T(8,128)S(1)} %collective-permute-done.p2, ...), custom_call_target="tpu_custom_call" | custom-call | tf_op jit(solution)/shard_map/pallas_call | solution.py:258
  45.6 0.0 collective-permute-done.6.forward_r
  45.6 0.0 collective-permute-done.5.forward_x
  45.7 0.1 collective-permute-start.7
  45.8 6.7 %collective-permute-start.8 = (f32[8,8,384]{2,1,0:T(8,128)S(1)}, f32[8,8,384]{2,1,0:T(8,128)S(1)}, u32[]{:S(2)}, u32[]{:S(2)}) collective-permute-start(f32[8,8,384]{2,1,0:T(8,128)S(1)} %get-tuple-element.38.own), channel_id=1, source_target_pairs={{0,254},{1,255},{2,252},{3,253},{4,8},{5,9},{6,10},{7,11},{8,4},{9... | collective-permute-start | bytes 294920 | tf_op jit(solution)/shard_map/ppermute | solution.py:305
  52.5 0.0 collective-permute-done.7.near
  52.5 2.2 %collective-permute-done.8.far = f32[8,8,384]{2,1,0:T(8,128)S(1)} collective-permute-done((f32[8,8,384]{2,1,0:T(8,128)S(1)}, f32[8,8,384]{2,1,0:T(8,128)S(1)}, u32[]{:S(2)}, u32[]{:S(2)}) %collective-permute-start.8) | collective-permute-done | bytes 98336 | tf_op jit(solution)/shard_map/ppermute | solution.py:305
  54.7 0.0 copy-start.1
  54.7 2.3 %shard_map.62 = (f32[11,8,256]{2,1,0:T(8,128)S(1)}, f32[11,8,256]{2,1,0:T(8,128)S(1)}, f32[11,8,256]{2,1,0:T(8,128)S(1)}, f32[11,8,256]{2,1,0:T(8,128)S(1)}) custom-call(s32[6]{0:T(128)S(1)} %stack.27.ids, f32[8,8,384]{2,1,0:T(8,128)S(1)} %collective-permute-done.7.near, f32[8,8,384]{2,1,0:T(8,128)S(1)} %get-tuple-element.38.own, ...), custom_call_target="tpu_custom_call" | custom-call | tf_op jit(solution)/shard_map/pallas_call | solution.py:258
  57.1 4.5 %collective-permute-start.9 = (f32[11,8,256]{2,1,0:T(8,128)S(1)}, f32[11,8,256]{2,1,0:T(8,128)S(1)}, u32[]{:S(2)}, u32[]{:S(2)}) collective-permute-start(f32[11,8,256]{2,1,0:T(8,128)S(1)} %get-tuple-element.41), channel_id=1, source_target_pairs={{0,2},{1,3},{2,0},{3,1},{4,6},{5,7},{6,4},{7,5},{8,10},{9,11},{10,... | collective-permute-start | bytes 270344 | tf_op jit(solution)/shard_map/ppermute | solution.py:283
  61.6 3.2 %collective-permute-start.11 = (f32[11,8,256]{2,1,0:T(8,128)S(1)}, f32[11,8,256]{2,1,0:T(8,128)S(1)}, u32[]{:S(2)}, u32[]{:S(2)}) collective-permute-start(f32[11,8,256]{2,1,0:T(8,128)S(1)} %get-tuple-element.45), channel_id=1, source_target_pairs={{0,3},{1,2},{2,1},{3,0},{4,7},{5,6},{6,5},{7,4},{8,11},{9,10},{10,... | collective-permute-start | bytes 270344 | tf_op jit(solution)/shard_map/ppermute | solution.py:284
  64.8 0.8 %collective-permute-done.9.p2 = f32[11,8,256]{2,1,0:T(8,128)S(1)} collective-permute-done((f32[11,8,256]{2,1,0:T(8,128)S(1)}, f32[11,8,256]{2,1,0:T(8,128)S(1)}, u32[]{:S(2)}, u32[]{:S(2)}) %collective-permute-start.9) | collective-permute-done | bytes 90144 | tf_op jit(solution)/shard_map/ppermute | solution.py:283
  65.6 2.1 %collective-permute-start.10 = (f32[11,8,256]{2,1,0:T(8,128)S(1)}, f32[11,8,256]{2,1,0:T(8,128)S(1)}, u32[]{:S(2)}, u32[]{:S(2)}) collective-permute-start(f32[11,8,256]{2,1,0:T(8,128)S(1)} %get-tuple-element.43), channel_id=1, source_target_pairs={{0,1},{1,0},{2,3},{3,2},{4,5},{5,4},{6,7},{7,6},{8,9},{9,8},{10,11... | collective-permute-start | bytes 270344 | tf_op jit(solution)/shard_map/ppermute | solution.py:286
  67.7 2.9 %collective-permute-done.11.p3 = f32[11,8,256]{2,1,0:T(8,128)S(1)} collective-permute-done((f32[11,8,256]{2,1,0:T(8,128)S(1)}, f32[11,8,256]{2,1,0:T(8,128)S(1)}, u32[]{:S(2)}, u32[]{:S(2)}) %collective-permute-start.11) | collective-permute-done | bytes 90144 | tf_op jit(solution)/shard_map/ppermute | solution.py:284
  70.7 0.0 collective-permute-done.10.p1
  70.7 0.0 copy-done.1
  70.7 1.6 %shard_map.63 = (f32[4,16,1024]{2,1,0:T(8,128)}, f32[4,16,1024]{2,1,0:T(8,128)}) custom-call(s32[6]{0:T(128)S(1)} %stack.27.ids, f32[11,8,256]{2,1,0:T(8,128)S(1)} %get-tuple-element.40.p0, f32[11,8,256]{2,1,0:T(8,128)S(1)} %collective-permute-done.10.p1, f32[11,8,256]{2,1,0:T(8,128)S(1)} %collective-permute-done.9.p2, ...), custom_call_target="tpu_custom_call" | custom-call | tf_op jit(solution)/shard_map/pallas_call | solution.py:258
  (2 shorter events, 0.0 us)
Async XLA Ops:
  2.7 11.2 %collective-permute-start = (f32[4,16,640]{2,1,0:T(8,128)S(1)}, f32[4,16,640]{2,1,0:T(8,128)S(1)}, u32[]{:S(2)}, u32[]{:S(2)}) collective-permute-start(f32[4,16,640]{2,1,0:T(8,128)S(1)} %get-tuple-element.26), channel_id=1, source_target_pairs={{0,2},{1,3},{2,0},{3,1},{4,6},{5,7},{6,4},{7,5},{8,10},{9,11},{10,... | collective-permute-start | bytes 491528 | tf_op jit(solution)/shard_map/ppermute | solution.py:283
  10.5 12.9 %collective-permute-start.2 = (f32[4,16,640]{2,1,0:T(8,128)S(1)}, f32[4,16,640]{2,1,0:T(8,128)S(1)}, u32[]{:S(2)}, u32[]{:S(2)}) collective-permute-start(f32[4,16,640]{2,1,0:T(8,128)S(1)} %get-tuple-element.31), channel_id=1, source_target_pairs={{0,3},{1,2},{2,1},{3,0},{4,7},{5,6},{6,5},{7,4},{8,11},{9,10},{10,... | collective-permute-start | bytes 491528 | tf_op jit(solution)/shard_map/ppermute | solution.py:284
  13.9 9.5 %collective-permute-start.1 = (f32[4,16,640]{2,1,0:T(8,128)S(1)}, f32[4,16,640]{2,1,0:T(8,128)S(1)}, u32[]{:S(2)}, u32[]{:S(2)}) collective-permute-start(f32[4,16,640]{2,1,0:T(8,128)S(1)} %get-tuple-element.28), channel_id=1, source_target_pairs={{0,1},{1,0},{2,3},{3,2},{4,5},{5,4},{6,7},{7,6},{8,9},{9,8},{10,11... | collective-permute-start | bytes 491528 | tf_op jit(solution)/shard_map/ppermute | solution.py:286
  23.5 9.7 %copy-start = (f32[4,16,1024]{2,1,0:T(8,128)S(1)}, f32[4,16,1024]{2,1,0:T(8,128)}, u32[]{:S(2)}) copy-start(f32[4,16,1024]{2,1,0:T(8,128)} %forward.1) | copy-start | bytes 786436
  24.1 16.7 %collective-permute-start.3 = (f32[16,8,640]{2,1,0:T(8,128)S(1)}, f32[16,8,640]{2,1,0:T(8,128)S(1)}, u32[]{:S(2)}, u32[]{:S(2)}) collective-permute-start(f32[16,8,640]{2,1,0:T(8,128)S(1)} %get-tuple-element.33), channel_id=1, source_target_pairs={{0,4},{1,5},{2,6},{3,7},{4,8},{5,9},{6,10},{7,11},{8,12},{9,13},{1... | collective-permute-start | bytes 983048 | tf_op jit(solution)/shard_map/ppermute | solution.py:295
  27.1 13.7 %collective-permute-start.4 = (f32[16,8,640]{2,1,0:T(8,128)S(1)}, f32[16,8,640]{2,1,0:T(8,128)S(1)}, u32[]{:S(2)}, u32[]{:S(2)}) collective-permute-start(f32[16,8,640]{2,1,0:T(8,128)S(1)} %get-tuple-element.34), channel_id=1, source_target_pairs={{0,254},{1,255},{2,252},{3,253},{4,0},{5,1},{6,2},{7,3},{8,4},{9,5... | collective-permute-start | bytes 983048 | tf_op jit(solution)/shard_map/ppermute | solution.py:295
  33.1 12.5 %collective-permute-start.6 = (f32[1,16,1024]{2,1,0:T(8,128)S(1)}, f32[1,16,1024]{2,1,0:T(8,128)S(1)}, u32[]{:S(2)}, u32[]{:S(2)}) collective-permute-start(f32[1,16,1024]{2,1,0:T(8,128)S(1)} %slice.7), channel_id=1, source_target_pairs={{1,0},{2,1},{3,2},{5,4},{6,5},{7,6},{9,8},{10,9},{11,10},{13,12},{... | collective-permute-start | bytes 196616 | tf_op jit(solution)/shard_map/ppermute | solution.py:319
  35.8 9.8 %collective-permute-start.5 = (f32[4,1,1024]{2,1,0:T(1,128)S(1)}, f32[4,1,1024]{2,1,0:T(1,128)S(1)}, u32[]{:S(2)}, u32[]{:S(2)}) collective-permute-start(f32[4,1,1024]{2,1,0:T(1,128)S(1)} %slice.6), channel_id=1, source_target_pairs={{4,0},{8,4},{12,8},{16,12},{20,16},{24,20},{28,24},{32,28},{36,32}... | collective-permute-start | bytes 49160 | tf_op jit(solution)/shard_map/ppermute | solution.py:325
  45.7 6.8 %collective-permute-start.7 = (f32[8,8,384]{2,1,0:T(8,128)S(1)}, f32[8,8,384]{2,1,0:T(8,128)S(1)}, u32[]{:S(2)}, u32[]{:S(2)}) collective-permute-start(f32[8,8,384]{2,1,0:T(8,128)S(1)} %get-tuple-element.38.own), channel_id=1, source_target_pairs={{0,4},{1,5},{2,6},{3,7},{4,0},{5,1},{6,2},{7,3},{8,12},{9,13},{10,... | collective-permute-start | bytes 294920 | tf_op jit(solution)/shard_map/ppermute | solution.py:305
  45.8 9.0 %collective-permute-start.8 = (f32[8,8,384]{2,1,0:T(8,128)S(1)}, f32[8,8,384]{2,1,0:T(8,128)S(1)}, u32[]{:S(2)}, u32[]{:S(2)}) collective-permute-start(f32[8,8,384]{2,1,0:T(8,128)S(1)} %get-tuple-element.38.own), channel_id=1, source_target_pairs={{0,254},{1,255},{2,252},{3,253},{4,8},{5,9},{6,10},{7,11},{8,4},{9... | collective-permute-start | bytes 294920 | tf_op jit(solution)/shard_map/ppermute | solution.py:305
  54.7 15.9 %copy-start.1 = (f32[4,16,1024]{2,1,0:T(8,128)S(1)}, f32[4,16,1024]{2,1,0:T(8,128)}, u32[]{:S(2)}) copy-start(f32[4,16,1024]{2,1,0:T(8,128)} %viscosity.1) | copy-start | bytes 786436
  57.1 8.5 %collective-permute-start.9 = (f32[11,8,256]{2,1,0:T(8,128)S(1)}, f32[11,8,256]{2,1,0:T(8,128)S(1)}, u32[]{:S(2)}, u32[]{:S(2)}) collective-permute-start(f32[11,8,256]{2,1,0:T(8,128)S(1)} %get-tuple-element.41), channel_id=1, source_target_pairs={{0,2},{1,3},{2,0},{3,1},{4,6},{5,7},{6,4},{7,5},{8,10},{9,11},{10,... | collective-permute-start | bytes 270344 | tf_op jit(solution)/shard_map/ppermute | solution.py:283
  61.6 9.1 %collective-permute-start.11 = (f32[11,8,256]{2,1,0:T(8,128)S(1)}, f32[11,8,256]{2,1,0:T(8,128)S(1)}, u32[]{:S(2)}, u32[]{:S(2)}) collective-permute-start(f32[11,8,256]{2,1,0:T(8,128)S(1)} %get-tuple-element.45), channel_id=1, source_target_pairs={{0,3},{1,2},{2,1},{3,0},{4,7},{5,6},{6,5},{7,4},{8,11},{9,10},{10,... | collective-permute-start | bytes 270344 | tf_op jit(solution)/shard_map/ppermute | solution.py:284
  65.6 5.1 %collective-permute-start.10 = (f32[11,8,256]{2,1,0:T(8,128)S(1)}, f32[11,8,256]{2,1,0:T(8,128)S(1)}, u32[]{:S(2)}, u32[]{:S(2)}) collective-permute-start(f32[11,8,256]{2,1,0:T(8,128)S(1)} %get-tuple-element.43), channel_id=1, source_target_pairs={{0,1},{1,0},{2,3},{3,2},{4,5},{5,4},{6,7},{7,6},{8,9},{9,8},{10,11... | collective-permute-start | bytes 270344 | tf_op jit(solution)/shard_map/ppermute | solution.py:286

commit v7 on v6

--- a/solution.py
+++ b/solution.py
@@ -1,3 +1,5 @@
+import functools
+
 import jax
 import jax.numpy as jnp
 from jax import lax
@@ -39,8 +41,8 @@
     return 1.0 / theta, pairs
 
 
-def pack_windows(ids, source_hbm, kappa_hbm, *refs):
-    outs, (source, kappa, done) = refs[:4], refs[4:]
+def pack_windows(members, ids, source_hbm, kappa_hbm, *refs):
+    outs, (source, kappa, done) = refs[: len(members)], refs[len(members) :]
     loads = []
     for f, (src, dst) in enumerate(((source_hbm, source), (kappa_hbm, kappa))):
         for j in range(LAYERS):
@@ -52,7 +54,7 @@
     for j in range(LAYERS):
         loads[j].wait()
         loads[LAYERS + j].wait()
-        for m, out in enumerate(outs):
+        for m, out in zip(members, outs):
             base = ids[m] * MAIN
             main = pl.ds(pl.multiple_of(base, 128), MAIN)
             after = pl.ds(pl.multiple_of(lax.rem(base + MAIN, 1024), 128), 128)
@@ -306,14 +308,20 @@
         return out[1], out[0]
 
     slab = pltpu.VMEM((LAYERS, ROWS, 1024), F32)
-    pieces = pl.pallas_call(
-        pack_windows,
-        out_shape=[struct(LAYERS, ROWS, PACKED)] * 4,
-        in_specs=[pl.BlockSpec(memory_space=pltpu.SMEM)] + [pl.BlockSpec(memory_space=pltpu.HBM)] * 2,
-        out_specs=[pl.BlockSpec(memory_space=pltpu.VMEM)] * 4,
-        scratch_shapes=[slab, slab, pltpu.SemaphoreType.DMA((2, LAYERS))],
-        compiler_params=VMEM,
-    )(ids, pltpu.with_memory_space_constraint(source, pltpu.HBM), pltpu.with_memory_space_constraint(kappa, pltpu.HBM))
+    held = [pltpu.with_memory_space_constraint(v, pltpu.HBM) for v in (source, kappa)]
+
+    def windows(*members):
+        return pl.pallas_call(
+            functools.partial(pack_windows, members),
+            out_shape=[struct(LAYERS, ROWS, PACKED)] * len(members),
+            in_specs=[pl.BlockSpec(memory_space=pltpu.SMEM)] + [pl.BlockSpec(memory_space=pltpu.HBM)] * 2,
+            out_specs=[pl.BlockSpec(memory_space=pltpu.VMEM)] * len(members),
+            scratch_shapes=[slab, slab, pltpu.SemaphoreType.DMA((2, LAYERS))],
+            compiler_params=VMEM,
+        )(ids, *held)
+
+    pieces = [*windows(2, 3)]
+    pieces = [*windows(0, 1), *pieces]
     pieces = trade(pieces)
     first, ahead = lax.optimization_barrier((pieces[2], forward))
     forward_r = lax.ppermute(ahead[:1], "rad", [(k + 1, k) for k in range(rad_n - 1)])

time: 72.4 us -> 72.4 us (level)
  waiting for transfers between devices: 16.5 us -> 14.6 us
  Pallas kernels: 11.3 us -> 13.2 us
    ppermute x2, waiting for transfers between devices: 3.13 us -> 1.21 us  [trade(): far = lax.ppermute(far, 'rad', [(k, k ^ 2) for k in range(rad_n)])]
    pallas_call x1 -> x2, Pallas kernels: 1.96 us -> 3.82 us  [windows(): pl.pallas_call(functools.partial(pack_windows, members), out_shape=[struc...]
  transfers between devices with their start and end apart: 12 -> 12, of which waited for: 6 -> 6; matrix products, arithmetic and copies ran while one was open for 0% -> 0% of each run, Pallas kernels for 7% -> 9%
where the time goes in v7:
time: 72.4 us; the launch traced here: 72.2 us
  starting transfers between devices  43.6 us (60%)
  waiting for transfers between devices  14.6 us (20%)
  Pallas kernels  13.2 us (18%)
  between operations  0.76 us (1%)
    ppermute x2, starting transfers between devices, trade(): far = lax.ppermute(far, 'rad', [(k, k ^ 2) for k in range(rad_n)])  12.4 us
    pallas_call x4, Pallas kernels, call(): pl.pallas_call(kernel, out_shape=outs, in_specs=[pl.BlockSpec(memory_spac...  9.36 us
    ppermute x2, starting transfers between devices, beside(): return lax.ppermute(v, ('lat', 'rad'), pairs)  9.08 us
    ppermute x2, waiting for transfers between devices, trade(): cross = lax.ppermute(cross, 'rad', [(k, k ^ 3) for k in range(rad_n)])  7.86 us
    ppermute x2, starting transfers between devices, swaps(): out.append(lax.ppermute(v, ('lat', 'rad'), pairs))  6.83 us
    ppermute x2, starting transfers between devices, trade(): near = lax.ppermute(near, 'rad', [(k, k ^ 1) for k in range(rad_n)])  6.71 us
    ppermute x2, starting transfers between devices, trade(): cross = lax.ppermute(cross, 'rad', [(k, k ^ 3) for k in range(rad_n)])  4.26 us
    pallas_call x2, Pallas kernels, windows(): pl.pallas_call(functools.partial(pack_windows, members), out_shape=[struc...  3.82 us
  transfers between devices with their start and end apart: 12, of which 6 were waited for; matrix products, arithmetic and copies ran while one was open for 0% of the time, Pallas kernels for 9%

profile of v7, /device:TPU:1, one launch (start us, length us, event | category | flops | bytes accessed | tf_op | source)
XLA Modules:
  0.0 72.2 jit_solution(9965095926927144925)
XLA Ops:
  0.7 0.1 stack.27.ids
  0.8 1.9 %shard_map.60 = (f32[4,16,640]{2,1,0:T(8,128)S(1)}, f32[4,16,640]{2,1,0:T(8,128)S(1)}) custom-call(s32[6]{0:T(128)S(1)} %stack.27.ids, f32[4,16,1024]{2,1,0:T(8,128)} %source_hbm.3, f32[4,16,1024]{2,1,0:T(8,128)} %kappa_hbm.3), custom_call_target="tpu_custom_call" | custom-call | tf_op jit(solution)/shard_map/pallas_call | solution.py:314
  2.7 7.8 %collective-permute-start = (f32[4,16,640]{2,1,0:T(8,128)S(1)}, f32[4,16,640]{2,1,0:T(8,128)S(1)}, u32[]{:S(2)}, u32[]{:S(2)}) collective-permute-start(f32[4,16,640]{2,1,0:T(8,128)S(1)} %get-tuple-element.26), channel_id=1, source_target_pairs={{0,2},{1,3},{2,0},{3,1},{4,6},{5,7},{6,4},{7,5},{8,10},{9,11},{10,... | collective-permute-start | bytes 491528 | tf_op jit(solution)/shard_map/ppermute | solution.py:285
  10.5 1.0 %collective-permute-start.2 = (f32[4,16,640]{2,1,0:T(8,128)S(1)}, f32[4,16,640]{2,1,0:T(8,128)S(1)}, u32[]{:S(2)}, u32[]{:S(2)}) collective-permute-start(f32[4,16,640]{2,1,0:T(8,128)S(1)} %get-tuple-element.31), channel_id=1, source_target_pairs={{0,3},{1,2},{2,1},{3,0},{4,7},{5,6},{6,5},{7,4},{8,11},{9,10},{10,... | collective-permute-start | bytes 491528 | tf_op jit(solution)/shard_map/ppermute | solution.py:286
  11.5 1.9 %shard_map.59 = (f32[4,16,640]{2,1,0:T(8,128)S(1)}, f32[4,16,640]{2,1,0:T(8,128)S(1)}) custom-call(s32[6]{0:T(128)S(1)} %stack.27.ids, f32[4,16,1024]{2,1,0:T(8,128)} %source_hbm.3, f32[4,16,1024]{2,1,0:T(8,128)} %kappa_hbm.3), custom_call_target="tpu_custom_call" | custom-call | tf_op jit(solution)/shard_map/pallas_call | solution.py:314
  13.5 0.4 collective-permute-done.p2
  13.9 4.6 %collective-permute-start.1 = (f32[4,16,640]{2,1,0:T(8,128)S(1)}, f32[4,16,640]{2,1,0:T(8,128)S(1)}, u32[]{:S(2)}, u32[]{:S(2)}) collective-permute-start(f32[4,16,640]{2,1,0:T(8,128)S(1)} %get-tuple-element.28), channel_id=1, source_target_pairs={{0,1},{1,0},{2,3},{3,2},{4,5},{5,4},{6,7},{7,6},{8,9},{9,8},{10,11... | collective-permute-start | bytes 491528 | tf_op jit(solution)/shard_map/ppermute | solution.py:288
  18.5 4.9 %collective-permute-done.2.p3 = f32[4,16,640]{2,1,0:T(8,128)S(1)} collective-permute-done((f32[4,16,640]{2,1,0:T(8,128)S(1)}, f32[4,16,640]{2,1,0:T(8,128)S(1)}, u32[]{:S(2)}, u32[]{:S(2)}) %collective-permute-start.2) | collective-permute-done | bytes 163872 | tf_op jit(solution)/shard_map/ppermute | solution.py:286
  23.4 0.0 collective-permute-done.1.p1
  23.4 0.0 copy-start
  23.4 0.6 shard_map.61
  24.0 3.0 %collective-permute-start.3 = (f32[16,8,640]{2,1,0:T(8,128)S(1)}, f32[16,8,640]{2,1,0:T(8,128)S(1)}, u32[]{:S(2)}, u32[]{:S(2)}) collective-permute-start(f32[16,8,640]{2,1,0:T(8,128)S(1)} %get-tuple-element.33), channel_id=1, source_target_pairs={{0,4},{1,5},{2,6},{3,7},{4,8},{5,9},{6,10},{7,11},{8,12},{9,13},{1... | collective-permute-start | bytes 983048 | tf_op jit(solution)/shard_map/ppermute | solution.py:297
  27.0 6.1 %collective-permute-start.4 = (f32[16,8,640]{2,1,0:T(8,128)S(1)}, f32[16,8,640]{2,1,0:T(8,128)S(1)}, u32[]{:S(2)}, u32[]{:S(2)}) collective-permute-start(f32[16,8,640]{2,1,0:T(8,128)S(1)} %get-tuple-element.34), channel_id=1, source_target_pairs={{0,254},{1,255},{2,252},{3,253},{4,0},{5,1},{6,2},{7,3},{8,4},{9,5... | collective-permute-start | bytes 983048 | tf_op jit(solution)/shard_map/ppermute | solution.py:297
  33.1 0.0 copy-done
  33.1 2.6 %collective-permute-start.6 = (f32[1,16,1024]{2,1,0:T(8,128)S(1)}, f32[1,16,1024]{2,1,0:T(8,128)S(1)}, u32[]{:S(2)}, u32[]{:S(2)}) collective-permute-start(f32[1,16,1024]{2,1,0:T(8,128)S(1)} %slice.7), channel_id=1, source_target_pairs={{1,0},{2,1},{3,2},{5,4},{6,5},{7,6},{9,8},{10,9},{11,10},{13,12},{... | collective-permute-start | bytes 196616 | tf_op jit(solution)/shard_map/ppermute | solution.py:327
  35.8 1.7 %collective-permute-start.5 = (f32[4,1,1024]{2,1,0:T(1,128)S(1)}, f32[4,1,1024]{2,1,0:T(1,128)S(1)}, u32[]{:S(2)}, u32[]{:S(2)}) collective-permute-start(f32[4,1,1024]{2,1,0:T(1,128)S(1)} %slice.6), channel_id=1, source_target_pairs={{4,0},{8,4},{12,8},{16,12},{20,16},{24,20},{28,24},{32,28},{36,32}... | collective-permute-start | bytes 49160 | tf_op jit(solution)/shard_map/ppermute | solution.py:333
  37.4 3.2 %collective-permute-done.3.lo = f32[16,8,640]{2,1,0:T(8,128)S(1)} collective-permute-done((f32[16,8,640]{2,1,0:T(8,128)S(1)}, f32[16,8,640]{2,1,0:T(8,128)S(1)}, u32[]{:S(2)}, u32[]{:S(2)}) %collective-permute-start.3) | collective-permute-done | bytes 327712 | tf_op jit(solution)/shard_map/ppermute | solution.py:297
  40.7 0.0 collective-permute-done.4.hi
  40.7 4.9 %shard_map.62 = (f32[16,24,256]{2,1,0:T(8,128)S(1)}, f32[8,8,384]{2,1,0:T(8,128)S(1)}) custom-call(s32[6]{0:T(128)S(1)} %stack.27.ids, f32[4,16,640]{2,1,0:T(8,128)S(1)} %get-tuple-element.25.p0, f32[4,16,640]{2,1,0:T(8,128)S(1)} %collective-permute-done.1.p1, f32[4,16,640]{2,1,0:T(8,128)S(1)} %collective-permute-done.p2, ...), custom_call_target="tpu_custom_call" | custom-call | tf_op jit(solution)/shard_map/pallas_call | solution.py:260
  45.6 0.0 collective-permute-done.6.forward_r
  45.6 0.0 collective-permute-done.5.forward_x
  45.6 0.1 collective-permute-start.7
  45.7 6.7 %collective-permute-start.8 = (f32[8,8,384]{2,1,0:T(8,128)S(1)}, f32[8,8,384]{2,1,0:T(8,128)S(1)}, u32[]{:S(2)}, u32[]{:S(2)}) collective-permute-start(f32[8,8,384]{2,1,0:T(8,128)S(1)} %get-tuple-element.38.own), channel_id=1, source_target_pairs={{0,254},{1,255},{2,252},{3,253},{4,8},{5,9},{6,10},{7,11},{8,4},{9... | collective-permute-start | bytes 294920 | tf_op jit(solution)/shard_map/ppermute | solution.py:307
  52.5 0.0 collective-permute-done.7.near
  52.5 2.2 %collective-permute-done.8.far = f32[8,8,384]{2,1,0:T(8,128)S(1)} collective-permute-done((f32[8,8,384]{2,1,0:T(8,128)S(1)}, f32[8,8,384]{2,1,0:T(8,128)S(1)}, u32[]{:S(2)}, u32[]{:S(2)}) %collective-permute-start.8) | collective-permute-done | bytes 98336 | tf_op jit(solution)/shard_map/ppermute | solution.py:307
  54.7 0.0 copy-start.1
  54.7 2.3 %shard_map.63 = (f32[11,8,256]{2,1,0:T(8,128)S(1)}, f32[11,8,256]{2,1,0:T(8,128)S(1)}, f32[11,8,256]{2,1,0:T(8,128)S(1)}, f32[11,8,256]{2,1,0:T(8,128)S(1)}) custom-call(s32[6]{0:T(128)S(1)} %stack.27.ids, f32[8,8,384]{2,1,0:T(8,128)S(1)} %collective-permute-done.7.near, f32[8,8,384]{2,1,0:T(8,128)S(1)} %get-tuple-element.38.own, ...), custom_call_target="tpu_custom_call" | custom-call | tf_op jit(solution)/shard_map/pallas_call | solution.py:260
  57.0 4.5 %collective-permute-start.9 = (f32[11,8,256]{2,1,0:T(8,128)S(1)}, f32[11,8,256]{2,1,0:T(8,128)S(1)}, u32[]{:S(2)}, u32[]{:S(2)}) collective-permute-start(f32[11,8,256]{2,1,0:T(8,128)S(1)} %get-tuple-element.41), channel_id=1, source_target_pairs={{0,2},{1,3},{2,0},{3,1},{4,6},{5,7},{6,4},{7,5},{8,10},{9,11},{10,... | collective-permute-start | bytes 270344 | tf_op jit(solution)/shard_map/ppermute | solution.py:285
  61.6 3.2 %collective-permute-start.11 = (f32[11,8,256]{2,1,0:T(8,128)S(1)}, f32[11,8,256]{2,1,0:T(8,128)S(1)}, u32[]{:S(2)}, u32[]{:S(2)}) collective-permute-start(f32[11,8,256]{2,1,0:T(8,128)S(1)} %get-tuple-element.45), channel_id=1, source_target_pairs={{0,3},{1,2},{2,1},{3,0},{4,7},{5,6},{6,5},{7,4},{8,11},{9,10},{10,... | collective-permute-start | bytes 270344 | tf_op jit(solution)/shard_map/ppermute | solution.py:286
  64.8 0.8 %collective-permute-done.9.p2 = f32[11,8,256]{2,1,0:T(8,128)S(1)} collective-permute-done((f32[11,8,256]{2,1,0:T(8,128)S(1)}, f32[11,8,256]{2,1,0:T(8,128)S(1)}, u32[]{:S(2)}, u32[]{:S(2)}) %collective-permute-start.9) | collective-permute-done | bytes 90144 | tf_op jit(solution)/shard_map/ppermute | solution.py:285
  65.6 2.1 %collective-permute-start.10 = (f32[11,8,256]{2,1,0:T(8,128)S(1)}, f32[11,8,256]{2,1,0:T(8,128)S(1)}, u32[]{:S(2)}, u32[]{:S(2)}) collective-permute-start(f32[11,8,256]{2,1,0:T(8,128)S(1)} %get-tuple-element.43), channel_id=1, source_target_pairs={{0,1},{1,0},{2,3},{3,2},{4,5},{5,4},{6,7},{7,6},{8,9},{9,8},{10,11... | collective-permute-start | bytes 270344 | tf_op jit(solution)/shard_map/ppermute | solution.py:288
  67.7 2.9 %collective-permute-done.11.p3 = f32[11,8,256]{2,1,0:T(8,128)S(1)} collective-permute-done((f32[11,8,256]{2,1,0:T(8,128)S(1)}, f32[11,8,256]{2,1,0:T(8,128)S(1)}, u32[]{:S(2)}, u32[]{:S(2)}) %collective-permute-start.11) | collective-permute-done | bytes 90144 | tf_op jit(solution)/shard_map/ppermute | solution.py:286
  70.6 0.0 collective-permute-done.10.p1
  70.6 0.0 copy-done.1
  70.6 1.6 %shard_map.64 = (f32[4,16,1024]{2,1,0:T(8,128)}, f32[4,16,1024]{2,1,0:T(8,128)}) custom-call(s32[6]{0:T(128)S(1)} %stack.27.ids, f32[11,8,256]{2,1,0:T(8,128)S(1)} %get-tuple-element.40.p0, f32[11,8,256]{2,1,0:T(8,128)S(1)} %collective-permute-done.10.p1, f32[11,8,256]{2,1,0:T(8,128)S(1)} %collective-permute-done.9.p2, ...), custom_call_target="tpu_custom_call" | custom-call | tf_op jit(solution)/shard_map/pallas_call | solution.py:260
  (2 shorter events, 0.0 us)
Async XLA Ops:
  2.7 11.2 %collective-permute-start = (f32[4,16,640]{2,1,0:T(8,128)S(1)}, f32[4,16,640]{2,1,0:T(8,128)S(1)}, u32[]{:S(2)}, u32[]{:S(2)}) collective-permute-start(f32[4,16,640]{2,1,0:T(8,128)S(1)} %get-tuple-element.26), channel_id=1, source_target_pairs={{0,2},{1,3},{2,0},{3,1},{4,6},{5,7},{6,4},{7,5},{8,10},{9,11},{10,... | collective-permute-start | bytes 491528 | tf_op jit(solution)/shard_map/ppermute | solution.py:285
  10.5 12.9 %collective-permute-start.2 = (f32[4,16,640]{2,1,0:T(8,128)S(1)}, f32[4,16,640]{2,1,0:T(8,128)S(1)}, u32[]{:S(2)}, u32[]{:S(2)}) collective-permute-start(f32[4,16,640]{2,1,0:T(8,128)S(1)} %get-tuple-element.31), channel_id=1, source_target_pairs={{0,3},{1,2},{2,1},{3,0},{4,7},{5,6},{6,5},{7,4},{8,11},{9,10},{10,... | collective-permute-start | bytes 491528 | tf_op jit(solution)/shard_map/ppermute | solution.py:286
  13.9 9.5 %collective-permute-start.1 = (f32[4,16,640]{2,1,0:T(8,128)S(1)}, f32[4,16,640]{2,1,0:T(8,128)S(1)}, u32[]{:S(2)}, u32[]{:S(2)}) collective-permute-start(f32[4,16,640]{2,1,0:T(8,128)S(1)} %get-tuple-element.28), channel_id=1, source_target_pairs={{0,1},{1,0},{2,3},{3,2},{4,5},{5,4},{6,7},{7,6},{8,9},{9,8},{10,11... | collective-permute-start | bytes 491528 | tf_op jit(solution)/shard_map/ppermute | solution.py:288
  23.4 9.7 %copy-start = (f32[4,16,1024]{2,1,0:T(8,128)S(1)}, f32[4,16,1024]{2,1,0:T(8,128)}, u32[]{:S(2)}) copy-start(f32[4,16,1024]{2,1,0:T(8,128)} %forward.1) | copy-start | bytes 786436
  24.0 16.7 %collective-permute-start.3 = (f32[16,8,640]{2,1,0:T(8,128)S(1)}, f32[16,8,640]{2,1,0:T(8,128)S(1)}, u32[]{:S(2)}, u32[]{:S(2)}) collective-permute-start(f32[16,8,640]{2,1,0:T(8,128)S(1)} %get-tuple-element.33), channel_id=1, source_target_pairs={{0,4},{1,5},{2,6},{3,7},{4,8},{5,9},{6,10},{7,11},{8,12},{9,13},{1... | collective-permute-start | bytes 983048 | tf_op jit(solution)/shard_map/ppermute | solution.py:297
  27.0 13.7 %collective-permute-start.4 = (f32[16,8,640]{2,1,0:T(8,128)S(1)}, f32[16,8,640]{2,1,0:T(8,128)S(1)}, u32[]{:S(2)}, u32[]{:S(2)}) collective-permute-start(f32[16,8,640]{2,1,0:T(8,128)S(1)} %get-tuple-element.34), channel_id=1, source_target_pairs={{0,254},{1,255},{2,252},{3,253},{4,0},{5,1},{6,2},{7,3},{8,4},{9,5... | collective-permute-start | bytes 983048 | tf_op jit(solution)/shard_map/ppermute | solution.py:297
  33.1 12.5 %collective-permute-start.6 = (f32[1,16,1024]{2,1,0:T(8,128)S(1)}, f32[1,16,1024]{2,1,0:T(8,128)S(1)}, u32[]{:S(2)}, u32[]{:S(2)}) collective-permute-start(f32[1,16,1024]{2,1,0:T(8,128)S(1)} %slice.7), channel_id=1, source_target_pairs={{1,0},{2,1},{3,2},{5,4},{6,5},{7,6},{9,8},{10,9},{11,10},{13,12},{... | collective-permute-start | bytes 196616 | tf_op jit(solution)/shard_map/ppermute | solution.py:327
  35.8 9.8 %collective-permute-start.5 = (f32[4,1,1024]{2,1,0:T(1,128)S(1)}, f32[4,1,1024]{2,1,0:T(1,128)S(1)}, u32[]{:S(2)}, u32[]{:S(2)}) collective-permute-start(f32[4,1,1024]{2,1,0:T(1,128)S(1)} %slice.6), channel_id=1, source_target_pairs={{4,0},{8,4},{12,8},{16,12},{20,16},{24,20},{28,24},{32,28},{36,32}... | collective-permute-start | bytes 49160 | tf_op jit(solution)/shard_map/ppermute | solution.py:333
  45.6 6.8 %collective-permute-start.7 = (f32[8,8,384]{2,1,0:T(8,128)S(1)}, f32[8,8,384]{2,1,0:T(8,128)S(1)}, u32[]{:S(2)}, u32[]{:S(2)}) collective-permute-start(f32[8,8,384]{2,1,0:T(8,128)S(1)} %get-tuple-element.38.own), channel_id=1, source_target_pairs={{0,4},{1,5},{2,6},{3,7},{4,0},{5,1},{6,2},{7,3},{8,12},{9,13},{10,... | collective-permute-start | bytes 294920 | tf_op jit(solution)/shard_map/ppermute | solution.py:307
  45.7 9.0 %collective-permute-start.8 = (f32[8,8,384]{2,1,0:T(8,128)S(1)}, f32[8,8,384]{2,1,0:T(8,128)S(1)}, u32[]{:S(2)}, u32[]{:S(2)}) collective-permute-start(f32[8,8,384]{2,1,0:T(8,128)S(1)} %get-tuple-element.38.own), channel_id=1, source_target_pairs={{0,254},{1,255},{2,252},{3,253},{4,8},{5,9},{6,10},{7,11},{8,4},{9... | collective-permute-start | bytes 294920 | tf_op jit(solution)/shard_map/ppermute | solution.py:307
  54.7 15.9 %copy-start.1 = (f32[4,16,1024]{2,1,0:T(8,128)S(1)}, f32[4,16,1024]{2,1,0:T(8,128)}, u32[]{:S(2)}) copy-start(f32[4,16,1024]{2,1,0:T(8,128)} %viscosity.1) | copy-start | bytes 786436
  57.0 8.5 %collective-permute-start.9 = (f32[11,8,256]{2,1,0:T(8,128)S(1)}, f32[11,8,256]{2,1,0:T(8,128)S(1)}, u32[]{:S(2)}, u32[]{:S(2)}) collective-permute-start(f32[11,8,256]{2,1,0:T(8,128)S(1)} %get-tuple-element.41), channel_id=1, source_target_pairs={{0,2},{1,3},{2,0},{3,1},{4,6},{5,7},{6,4},{7,5},{8,10},{9,11},{10,... | collective-permute-start | bytes 270344 | tf_op jit(solution)/shard_map/ppermute | solution.py:285
  61.6 9.1 %collective-permute-start.11 = (f32[11,8,256]{2,1,0:T(8,128)S(1)}, f32[11,8,256]{2,1,0:T(8,128)S(1)}, u32[]{:S(2)}, u32[]{:S(2)}) collective-permute-start(f32[11,8,256]{2,1,0:T(8,128)S(1)} %get-tuple-element.45), channel_id=1, source_target_pairs={{0,3},{1,2},{2,1},{3,0},{4,7},{5,6},{6,5},{7,4},{8,11},{9,10},{10,... | collective-permute-start | bytes 270344 | tf_op jit(solution)/shard_map/ppermute | solution.py:286
  65.6 5.1 %collective-permute-start.10 = (f32[11,8,256]{2,1,0:T(8,128)S(1)}, f32[11,8,256]{2,1,0:T(8,128)S(1)}, u32[]{:S(2)}, u32[]{:S(2)}) collective-permute-start(f32[11,8,256]{2,1,0:T(8,128)S(1)} %get-tuple-element.43), channel_id=1, source_target_pairs={{0,1},{1,0},{2,3},{3,2},{4,5},{5,4},{6,7},{7,6},{8,9},{9,8},{10,11... | collective-permute-start | bytes 270344 | tf_op jit(solution)/shard_map/ppermute | solution.py:288
